TPU v7x, 256 devices: a whole 4x4x8 slice. The times are simulated.
256 devices in a mesh: dp: 4 (over y), ctx: 16 (over z, core), tp: 4 (over x).
Axes of the slice: x: 4, y: 4, z: 8, core: 2. Of those that a mesh axis runs over, the one named last changes fastest.
Arguments:
- head_input: bfloat16 [4, 4096, 4096], P('dp', 'ctx', 'tp'), may hold values from -6 to 6
- write_vectors: bfloat16 [4, 4096, 512], P('dp', 'ctx', 'tp'), may hold values from -0.5 to 0.5
- read_vectors: bfloat16 [4, 4096, 512], P('dp', 'ctx', 'tp'), may hold values from -0.5 to 0.5
- log_decay: float32 [4, 64, 4096], P('dp', 'tp', 'ctx'), may hold values from -0.8 to 0, as said below
- cotangent: bfloat16 [4, 4096, 4096], P('dp', 'ctx', 'tp'), may hold values from -8 to 8
- out_weight: bfloat16 [4096, 4096], P(('dp', 'ctx'), 'tp'), may hold values from -0.09375 to 0.09375
- scale_exponent: int32 [128, 4096], P(('dp', 'ctx'), 'tp'), may hold values from -1 to 1
Outputs:
- grad_input: bfloat16 [4, 4096, 4096], P('dp', 'ctx', 'tp')
- grad_write: bfloat16 [4, 4096, 512], P('dp', 'ctx', 'tp')
- grad_read: bfloat16 [4, 4096, 512], P('dp', 'ctx', 'tp')
- grad_weight: float32 [4096, 4096], P(('dp', 'ctx'), 'tp')
Inputs may be any that keep to these rules, and one draw needn't show every extreme that they name: `log_decay`: every entry is negative.
All inputs are finite; a program needn't handle non-finite values.
Results may differ from a plain program's by a relative error of at most 0.015.
Values may be sent and summed in bfloat16 or wider, within the bound.
No kernel may reach another device: no remote copies, remote signals or barrier semaphores. Data moves between devices by JAX's collectives and lax.ppermute only.
A program may use at most 128 MiB of HBM per device.

v0:
```python
import jax
import jax.numpy as jnp
from jax import lax
from jax.sharding import PartitionSpec as P

HEADS = 64
GROUPS = 4
HEAD_DIM = 64
STATE = 128
BLOCK = 256
SCALE_BLOCK = 32


def prefix(x, axis, combine, identity, reverse):
    size, mine = (lax.axis_size(axis), lax.axis_index(axis))
    everything = jax.tree.map(lambda part: lax.all_gather(part, axis), x)
    start = jax.tree.map(
        lambda part, zero: jnp.broadcast_to(jnp.asarray(zero, part.dtype), part.shape), x, identity
    )

    def hop(k, before):
        at = size - 1 - k if reverse else k
        reached = at > mine if reverse else at < mine
        new = combine(before, jax.tree.map(lambda part: part[at], everything))
        return jax.tree.map(lambda a, b: jnp.where(reached, a, b), new, before)

    return lax.fori_loop(0, size, hop, start)


def link_states(earlier, later):
    early_decay, early_state = earlier
    late_decay, late_state = later
    return (early_decay * late_decay, late_state + late_decay[..., None, None] * early_state)


def per_device(
    head_input, write_vectors, read_vectors, log_decay, cotangent, out_weight, scale_exponent
):
    maximum_precision = lax.Precision.HIGHEST
    length = head_input.shape[1]
    blocks = length // BLOCK
    local_heads = log_decay.shape[1]
    per_group = HEADS // GROUPS
    local_groups = local_heads // per_group
    columns = local_heads * HEAD_DIM
    scales = jnp.exp2(scale_exponent.astype(jnp.float32))
    dequant = (out_weight.astype(jnp.float32) * jnp.repeat(scales, SCALE_BLOCK, axis=0)).astype(
        jnp.bfloat16
    )
    full_cot = lax.all_gather(cotangent, "tp", axis=2, tiled=True)[0]
    input_half = head_input[0].reshape(blocks, BLOCK, local_groups, per_group, HEAD_DIM)
    write_half = write_vectors[0].reshape(blocks, BLOCK, local_groups, STATE)
    read_half = read_vectors[0].reshape(blocks, BLOCK, local_groups, STATE)
    inputs = input_half.astype(jnp.float32)
    writes = write_half.astype(jnp.float32)
    readers = read_half.astype(jnp.float32)
    cumulative = jnp.cumsum(log_decay[0].reshape(local_groups, per_group, blocks, BLOCK), axis=-1)
    block_ends = cumulative[..., -1:]
    to_end = jnp.exp(block_ends - cumulative)
    since_beginning = jnp.exp(cumulative)
    decays = jnp.exp(cumulative[..., -1])
    offsets = jnp.arange(BLOCK)
    causal = offsets[:, None] >= offsets[None, :]
    within = jnp.exp(
        jnp.where(causal, cumulative[..., :, None] - cumulative[..., None, :], -jnp.inf)
    )
    intersections = jnp.einsum(
        "ktgn,kugn->gktu", read_half, write_half, preferred_element_type=jnp.float32
    )
    mixing = within * intersections[:, None]
    written = jnp.einsum(
        "ghku,kughp,kugn->kghpn", to_end, inputs, writes, precision=maximum_precision
    )
    device_decay = jnp.exp(jnp.sum(log_decay[0].reshape(local_groups, per_group, length), axis=-1))
    summary = jnp.zeros((local_groups, per_group, HEAD_DIM, STATE), jnp.float32)
    position = 0
    summary = decays[..., position, None, None] * summary + written[position]
    identity = (jnp.ones_like(device_decay), jnp.zeros_like(summary))
    prior_decay, prior_state = prefix((device_decay, summary), "ctx", link_states, identity, False)
    entering = []
    current = prior_state
    entering.append(current)
    entering = jnp.stack(entering)
    mixer_out = jnp.einsum("ghktu,kughp->ktghp", mixing, inputs, precision=maximum_precision)
    mixer_out = mixer_out + jnp.einsum(
        "ghkt,kghpn,ktgn->ktghp", since_beginning, entering, readers, precision=maximum_precision
    )
    mixed_rows = mixer_out.reshape(length, columns).astype(jnp.bfloat16)
    selected = full_cot
    grad_mixer = jnp.dot(
        selected,
        lax.all_gather(dequant, ("dp", "ctx"), axis=0, tiled=True),
        preferred_element_type=jnp.float32,
    ).astype(jnp.bfloat16)
    grad_half = grad_mixer.reshape(blocks, BLOCK, local_groups, per_group, HEAD_DIM)
    grad_blocks = grad_half.astype(jnp.float32)
    produced_rows = jnp.einsum(
        "ghkv,kvghp,kvgn->kghpn", since_beginning, grad_blocks, readers, precision=maximum_precision
    )
    backlog = jnp.zeros_like(summary)
    position = 0
    backlog = produced_rows[position] + decays[..., position, None, None] * backlog
    later_decay, later_state = prefix((device_decay, backlog), "ctx", link_states, identity, True)
    leaving = [None] * blocks
    current = later_state
    position = 0
    leaving[position] = current
    leaving = jnp.stack(leaving)
    pair_dots = jnp.einsum(
        "kvghp,kughp->ghkvu", grad_half, input_half, preferred_element_type=jnp.float32
    )
    weighted = within * pair_dots
    grad_in = jnp.einsum("ghkvt,kvghp->ktghp", mixing, grad_blocks, precision=maximum_precision)
    grad_in = grad_in + jnp.einsum(
        "ghkt,kghpn,ktgn->ktghp", to_end, leaving, writes, precision=maximum_precision
    )
    grad_wr = jnp.einsum("ghkvt,kvgn->ktgn", weighted, readers, precision=maximum_precision)
    grad_wr = grad_wr + jnp.einsum(
        "ghkt,kghpn,ktghp->ktgn", to_end, leaving, inputs, precision=maximum_precision
    )
    grad_rd = jnp.einsum("ghktu,kugn->ktgn", weighted, writes, precision=maximum_precision)
    grad_rd = grad_rd + jnp.einsum(
        "ghkt,kghpn,ktghp->ktgn",
        since_beginning,
        entering,
        grad_blocks,
        precision=maximum_precision,
    )
    grad_input = grad_in.reshape(1, length, columns).astype(jnp.bfloat16)
    grad_write = grad_wr.reshape(1, length, local_groups * STATE).astype(jnp.bfloat16)
    grad_read = grad_rd.reshape(1, length, local_groups * STATE).astype(jnp.bfloat16)
    selected = full_cot
    grad_weight = lax.psum_scatter(
        lax.dot_general(
            selected, mixed_rows, (((0,), (0,)), ((), ())), preferred_element_type=jnp.float32
        ),
        ("dp", "ctx"),
        scatter_dimension=0,
        tiled=True,
    )
    return (grad_input, grad_write, grad_read, grad_weight)


def solution(mesh):
    return jax.shard_map(
        per_device,
        mesh=mesh,
        in_specs=(
            P("dp", "ctx", "tp"),
            P("dp", "ctx", "tp"),
            P("dp", "ctx", "tp"),
            P("dp", "tp", "ctx"),
            P("dp", "ctx", "tp"),
            P(("dp", "ctx"), "tp"),
            P(("dp", "ctx"), "tp"),
        ),
        out_specs=(
            P("dp", "ctx", "tp"),
            P("dp", "ctx", "tp"),
            P("dp", "ctx", "tp"),
            P(("dp", "ctx"), "tp"),
        ),
        check_vma=False,
    )
```

profile of v0, /device:TPU:1, one launch (start us, length us, event | category | flops | bytes accessed | tf_op | source)
XLA Modules:
  0.0 441.1 jit_solution(14350269159355534193)
XLA Ops:
  7.2 0.7 all-gather.10.cloned.1.call-update
  8.0 0.7 multiply_exponential_fusion
  8.7 1.6 fusion.59
  10.3 0.7 reshape.298
  11.1 0.6 reduce-window.6
  12.0 1.2 copy.41
  13.3 0.4 fusion.71
  13.8 1.4 convolution_add_fusion
  15.4 31.7 %all-gather.10.cloned.1.call-done = bf16[1,256,4096]{2,1,0:T(8,128)(2,1)} async-done(((bf16[1,256,1024]{2,1,0:T(8,128)(2,1)}), bf16[1,256,4096]{2,1,0:T(8,128)(2,1)}) %all-gather.10.cloned.1.call-update) | async-done | bytes 2097168 | tf_op jit(solution)/shard_map/all_gather | solution.py:50
  47.0 86.9 %all-gather.8.cloned.1.call-done = bf16[4096,1024]{1,0:T(8,128)(2,1)} async-done(((bf16[64,1024]{1,0:T(8,128)(2,1)}), bf16[4096,1024]{1,0:T(8,128)(2,1)}) %all-gather.8.cloned.1.call-update) | async-done | bytes 8388624 | tf_op jit(solution)/shard_map/all_gather | solution.py:92
  133.9 6.4 %fusion.42 = bf16[1024,256]{1,0:T(8,128)(2,1)S(1)} fusion(bf16[4096,1024]{1,0:T(8,128)(2,1)} %all-gather.8.cloned.1.call-done, bf16[1,256,4096]{2,1,0:T(8,128)(2,1)} %all-gather.10.cloned.1.call-done), kind=kOutput, calls=%fused_computation.37 | convolution fusion | flops 2147745792 | bytes 11010048 | tf_op jit(solution)/shard_map/dot_general | solution.py:90
  140.3 1.4 convolution_add_fusion.1
  142.0 0.6 dynamic-slice
  143.4 24.3 %all-reduce = f32[256]{0:T(256)S(1)} all-reduce(f32[256]{0:T(256)S(1)} %exponential_dynamic-update-slice_fusion), channel_id=3, replica_groups=mesh['dp'=4,'ctx'=16,'tp'=4] {'ctx'}, use_global_device_ids=true, to_apply=%add | all-reduce | flops 256 | bytes 2048
  167.8 0.2 fusion.65
  168.0 21.3 %all-gather.14.cloned.1.call-done = f32[256,64,128]{2,1,0:T(8,128)} async-done(((f32[16,64,128]{2,1,0:T(8,128)}), f32[256,64,128]{2,1,0:T(8,128)}) %all-gather.14.cloned.1.call-update) | async-done | bytes 8388624 | tf_op jit(solution)/shard_map/all_gather | solution.py:16
  189.3 19.5 %while.31 = (s32[]{:T(128)}, f32[1,16,64,128]{3,2,1,0:T(8,128)S(1)}, s32[]{:T(128)}, f32[16,1,16,64,128]{4,3,2,1,0:T(8,128)}, f32[16,1,16]{2,1,0:T(1,128)S(1)}, /*index=5*/s32[]{:T(128)}, s32[]{:T(128)}) while((s32[]{:T(128)}, f32[1,16,64,128]{3,2,1,0:T(8,128)S(1)}, s32[]{:T(128)}, f32[16,1,16,64,128]{4,3,2,1,0:T(8,128)}, ...), condition=%wide.region_7.8_spmd.clone, body=%wide.region_6.7_spmd.clone.sunk | while | flops 524292 | bytes 1573169 | solution.py:27
  189.3 1.2 fusion.83
  190.5 1.2 fusion.83
  191.8 1.2 fusion.83
  193.0 1.2 fusion.83
  194.2 1.2 fusion.83
  195.4 1.2 fusion.83
  196.6 1.2 fusion.83
  197.8 1.2 fusion.83
  199.0 1.2 fusion.83
  200.3 1.3 fusion.83
  201.6 1.2 fusion.83
  202.8 1.2 fusion.83
  204.0 1.2 fusion.83
  205.2 1.2 fusion.83
  206.4 1.2 fusion.83
  207.7 1.2 fusion.83
  208.9 0.6 fusion.29
  209.5 3.6 fusion.39
  213.1 8.3 %convolution_bitcast_fusion = f32[4096,1024]{0,1:T(8,128)} fusion(bf16[256,1024]{0,1:T(8,128)(2,1)S(1)} %bitcast.184, bf16[1,256,4096]{2,1,0:T(8,128)(2,1)S(1)} %copy-done.1), kind=kOutput, calls=%fused_computation.6 | convolution fusion | flops 2147483648 | bytes 19398656 | tf_op jit(solution)/shard_map/dot_general | solution.py:134
  221.3 17.6 %copy.45 = f32[4096,1024]{1,0:T(8,128)} copy(f32[4096,1024]{0,1:T(8,128)} %convolution_bitcast_fusion) | data formatting | bytes 33554432
  238.9 1.8 convolution_bitcast_fusion.5
  240.8 1.5 multiply_reduce_fusion
  242.3 0.9 fusion.50
  243.2 2.8 all-gather.12.cloned.1.call-done
  246.0 19.6 %while.30 = (s32[]{:T(128)}, f32[1,16,64,128]{3,2,1,0:T(8,128)S(1)}, s32[]{:T(128)}, f32[16,1,16,64,128]{4,3,2,1,0:T(8,128)}, f32[16,1,16]{2,1,0:T(1,128)S(1)}, ...) while((s32[]{:T(128)}, f32[1,16,64,128]{3,2,1,0:T(8,128)S(1)}, s32[]{:T(128)}, ...), condition=%wide.region_4.5_spmd.clone, body=%wide.region_3.4_spmd.clone.sunk | while | flops 524296 | bytes 1573231 | solution.py:27
  246.0 1.2 fusion.82
  247.2 1.2 fusion.82
  248.5 1.2 fusion.82
  249.7 1.2 fusion.82
  250.9 1.2 fusion.82
  252.1 1.2 fusion.82
  253.3 1.2 fusion.82
  254.6 1.2 fusion.82
  255.8 1.2 fusion.82
  257.0 1.2 fusion.82
  258.2 1.2 fusion.82
  259.4 1.2 fusion.82
  260.7 1.2 fusion.82
  261.9 1.2 fusion.82
  263.2 1.2 fusion.82
  264.4 1.2 fusion.82
  265.6 0.6 fusion.27
  266.2 3.0 fusion.36
  269.2 1.0 copy.43
  270.2 1.8 convolution_bitcast_fusion.6
  272.0 1.0 fusion.49
  273.0 161.5 %reduce-scatter.4.cloned.1.call-done = f32[64,1024]{1,0:T(8,128)} async-done(((f32[4096,1024]{1,0:T(8,128)}), f32[64,1024]{1,0:T(8,128)}) %reduce-scatter.4.cloned.1.call-update) | async-done | bytes 262160
  (68 shorter events, 1.3 us)
Async XLA Ops:
  7.2 6.6 %copy-start = (bf16[1,256,128]{2,1,0:T(8,128)(2,1)S(1)}, bf16[1,256,128]{2,1,0:T(8,128)(2,1)}, u32[]{:S(2)}) copy-start(bf16[1,256,128]{2,1,0:T(8,128)(2,1)} %param.12) | copy-start | bytes 196612
  7.2 39.8 %all-gather.10.cloned.1.call-start = ((), (), s32[]{:S(2)}) async-start(), calls=%async_computation.2 | async-start | bytes 2621440 | tf_op jit(solution)/shard_map/all_gather | solution.py:50
  7.9 126.0 %all-gather.8.cloned.1.call-start = ((), (), s32[]{:S(2)}) async-start(), calls=%async_computation.1 | async-start | bytes 8519680 | tf_op jit(solution)/shard_map/all_gather | solution.py:92
  10.3 179.0 %all-gather.14.cloned.1.call-start = ((), (), s32[]{:S(2)}) async-start(), calls=%async_computation.4 | async-start | bytes 8912896 | tf_op jit(solution)/shard_map/all_gather | solution.py:16
  15.3 230.8 %all-gather.12.cloned.1.call-start = ((), (), s32[]{:S(2)}) async-start(), calls=%async_computation.3 | async-start | bytes 8912896 | tf_op jit(solution)/shard_map/all_gather | solution.py:16
  15.3 125.0 %copy-start.2 = (bf16[1,256,128]{2,1,0:T(8,128)(2,1)S(1)}, bf16[1,256,128]{2,1,0:T(8,128)(2,1)}, u32[]{:S(2)}) copy-start(bf16[1,256,128]{2,1,0:T(8,128)(2,1)} %param.13) | copy-start | bytes 196612
  15.3 126.5 %copy-start.3 = (f32[1,16,256]{2,1,0:T(8,128)S(1)}, f32[1,16,256]{2,1,0:T(8,128)}, u32[]{:S(2)}) copy-start(f32[1,16,256]{2,1,0:T(8,128)} %param.14) | copy-start | bytes 49156
  15.4 126.7 %copy-start.4 = (u32[256]{0:T(256)S(1)}, u32[256]{0:T(256)}, u32[]{:S(2)}) copy-start(u32[256]{0:T(256)} %constant.90) | copy-start | bytes 3076
  141.8 292.8 %reduce-scatter.4.cloned.1.call-start = ((), (), s32[]{:S(2)}) async-start(), calls=%async_computation.5 | async-start | bytes 17039360
  208.9 4.2 copy-start.1
Sparse Core Ops, SparseCore 0:
  9.8 37.1 all-gather.9
  50.4 83.5 all-gather.7
  135.8 53.4 all-gather.13
  191.6 54.3 all-gather.11
  250.9 183.5 reduce-scatter.3
where the time goes:
time: 446 us; the launch traced here: 441 us
  waiting for transfers between devices  305 us (68%)
  other arithmetic  41.4 us (9%)
  matrix products  32.5 us (7%)
  blocking collectives  24.3 us (5%)
  local copies, waits for them, and re-layouts  22 us (5%)
  between operations  14.7 us (3%)
    unnamed x6, waiting for transfers between devices  162 us
    all_gather x1, waiting for transfers between devices, per_device(): lax.all_gather(dequant, ('dp', 'ctx'), axis=0, tiled=True)  86.9 us
    select_n x32, other arithmetic, hop(): return jax.tree.map(lambda a, b: jnp.where(reached, a, b), new, before)  37.8 us
    all_gather x1, waiting for transfers between devices, per_device(): full_cot = lax.all_gather(cotangent, 'tp', axis=2, tiled=True)[0]  31.7 us
    unnamed x1, blocking collectives  24.3 us
    all_gather x2, waiting for transfers between devices, prefix(): everything = jax.tree.map(lambda part: lax.all_gather(part, axis), x)  24.1 us
    unnamed x16, local copies, waits for them, and re-layouts  20.6 us
  transfers between devices with their start and end apart: 5, of which 5 were waited for; matrix products, arithmetic and copies ran while one was open for 22% of the time, Pallas kernels for 0%

commit v1 on v0

v1 whole, which is shorter than its diff:
```python
import functools

import jax
import jax.numpy as jnp
from jax import lax
from jax.experimental import pallas as pl
from jax.experimental.pallas import tpu as pltpu
from jax.sharding import PartitionSpec as P

HEADS = 64
GROUPS = 4
HEAD_DIM = 64
STATE = 128
SCALE_BLOCK = 32
LANES = 128
VMEM_LIMIT = 50 * 1024 * 1024

bf16 = jnp.bfloat16
f32 = jnp.float32
HIGHEST = lax.Precision.HIGHEST


def call(kernel, out_shape, n_in, flops=0, bytes_accessed=0, scratch=(), in_specs=None):
    out_specs = jax.tree.map(lambda _: pl.BlockSpec(memory_space=pltpu.VMEM), out_shape)
    return pl.pallas_call(
        kernel,
        out_shape=out_shape,
        in_specs=in_specs or [pl.BlockSpec(memory_space=pltpu.VMEM)] * n_in,
        out_specs=out_specs,
        scratch_shapes=list(scratch),
        compiler_params=pltpu.CompilerParams(vmem_limit_bytes=VMEM_LIMIT),
        cost_estimate=pl.CostEstimate(
            flops=flops, bytes_accessed=bytes_accessed, transcendentals=0
        ),
    )


def dot(a, b, contract, precision=None):
    return lax.dot_general(
        a, b, ((contract[:1], contract[1:]), ((), ())),
        precision=precision, preferred_element_type=f32,
    )


def low_half(rows):
    return lax.broadcasted_iota(jnp.int32, (rows, LANES), 1) < HEAD_DIM


def pair_scale(columns, pair, rows):
    first = columns[:, 2 * pair : 2 * pair + 1]
    second = columns[:, 2 * pair + 1 : 2 * pair + 2]
    return jnp.where(low_half(rows), first, second)


def spread_matrix(heads):
    head = lax.broadcasted_iota(jnp.int32, (LANES, heads * HEAD_DIM), 0)
    column = lax.broadcasted_iota(jnp.int32, (LANES, heads * HEAD_DIM), 1)
    return jnp.where(column // HEAD_DIM == head, 1.0, 0.0).astype(f32)


def state_kernel(x_ref, w_ref, decay_ref, packed_ref, rows_ref, columns_ref):
    length, columns = x_ref.shape
    heads = decay_ref.shape[0]
    log_decay = decay_ref[...]
    row = lax.broadcasted_iota(jnp.int32, (length, length), 0)
    column = lax.broadcasted_iota(jnp.int32, (length, length), 1)
    upto = jnp.where(row <= column, 1.0, 0.0).astype(f32)
    cumulative = dot(log_decay, upto, (1, 0), HIGHEST)
    rows_ref[...] = cumulative
    padded = jnp.concatenate(
        [cumulative, jnp.zeros((LANES - heads, length), f32)], axis=0
    )
    turned = jnp.transpose(padded)
    columns_ref[...] = turned
    ends = turned[length - 1 : length, :]
    to_end = jnp.exp(ends - turned)
    w = w_ref[...]
    for pair in range(heads // 2):
        lanes = slice(pair * LANES, (pair + 1) * LANES)
        scaled = x_ref[:, lanes].astype(f32) * pair_scale(to_end, pair, length)
        packed_ref[:, lanes] = dot(w, scaled.astype(bf16), (0, 0)).astype(bf16)
    high = ends.astype(bf16).astype(f32)
    middle = (ends - high).astype(bf16).astype(f32)
    low = ends - high - middle
    which = lax.broadcasted_iota(jnp.int32, (STATE, LANES), 0) % 8
    terms = jnp.where(
        which == 0, high, jnp.where(which == 1, middle, jnp.where(which == 2, low, 0.0))
    )
    packed_ref[:, columns:] = terms.astype(bf16)


def forward_scan_kernel(packed_ref, entering_ref, decay_ref):
    rows, total = packed_ref.shape
    columns = entering_ref.shape[1]
    size = decay_ref.shape[0]
    chunk = rows // size
    everything = packed_ref[...].astype(f32)
    terms = everything[:, columns:]
    sums = [
        jnp.sum(terms[k * chunk : (k + 1) * chunk], axis=0, keepdims=True) for k in range(size)
    ]
    decays = jnp.exp(jnp.concatenate(sums, axis=0))
    spread = dot(decays, spread_matrix(columns // HEAD_DIM), (1, 0), HIGHEST)
    decay_ref[...] = spread
    carry = jnp.zeros((chunk, columns), f32)
    before = []
    for k in range(size):
        before.append(carry)
        carry = spread[k : k + 1] * carry + everything[k * chunk : (k + 1) * chunk, :columns]
    entering_ref[...] = jnp.concatenate(before, axis=0).astype(bf16)


def backward_scan_kernel(summary_ref, decay_ref, leaving_ref):
    rows, columns = summary_ref.shape
    size = decay_ref.shape[0]
    chunk = rows // size
    everything = summary_ref[...].astype(f32)
    spread = decay_ref[...]
    carry = jnp.zeros((chunk, columns), f32)
    after = [None] * size
    for k in range(size - 1, -1, -1):
        after[k] = carry
        carry = spread[k : k + 1] * carry + everything[k * chunk : (k + 1) * chunk]
    leaving_ref[...] = jnp.concatenate(after, axis=0).astype(bf16)


def mixer_kernel(x_ref, w_ref, r_ref, rows_ref, columns_ref, entering_ref, out_ref):
    length = x_ref.shape[0]
    heads = rows_ref.shape[0]
    r = r_ref[...]
    row = lax.broadcasted_iota(jnp.int32, (length, length), 0)
    column = lax.broadcasted_iota(jnp.int32, (length, length), 1)
    meets = jnp.where(row >= column, dot(r, w_ref[...], (1, 1)), 0.0)
    cumulative = columns_ref[...]
    since = jnp.exp(cumulative)
    half = low_half(length)
    for pair in range(heads // 2):
        lanes = slice(pair * LANES, (pair + 1) * LANES)
        x = x_ref[:, lanes]
        parts = []
        for head in (2 * pair, 2 * pair + 1):
            difference = cumulative[:, head : head + 1] - rows_ref[head : head + 1, :]
            mixing = jnp.exp(jnp.minimum(difference, 0.0)) * meets
            parts.append(dot(mixing.astype(bf16), x, (1, 0)))
        carried = dot(r, entering_ref[:, lanes], (1, 0)) * pair_scale(since, pair, length)
        out_ref[:, lanes] = (jnp.where(half, parts[0], parts[1]) + carried).astype(bf16)


def project_kernel(place_ref, c0, c1, c2, c3, weight_ref, o0, o1, o2, o3, held, sems):
    copies = []
    for m, ref in enumerate((c0, c1, c2, c3)):
        slot = lax.rem(place_ref[0] + 8 - m, 4)
        copy = pltpu.make_async_copy(ref, held.at[slot], sems.at[m])
        copy.start()
        copies.append(copy)
    for copy in copies:
        copy.wait()
    weight = weight_ref[...]
    for n, out in enumerate((o0, o1, o2, o3)):
        out[...] = dot(held[n], weight, (1, 0)).astype(bf16)


def adjoint_kernel(g0, g1, g2, g3, r_ref, columns_ref, grad_ref, summary_ref):
    length, columns = g0.shape
    heads = columns // HEAD_DIM
    since = jnp.exp(columns_ref[...])
    r = r_ref[...]
    for pair in range(heads // 2):
        lanes = slice(pair * LANES, (pair + 1) * LANES)
        total = (g0[:, lanes].astype(f32) + g1[:, lanes].astype(f32)) + (
            g2[:, lanes].astype(f32) + g3[:, lanes].astype(f32)
        )
        grad = total.astype(bf16)
        grad_ref[:, lanes] = grad
        scaled = grad.astype(f32) * pair_scale(since, pair, length)
        summary_ref[:, lanes] = dot(r, scaled.astype(bf16), (0, 0)).astype(bf16)


def gradients_kernel(
    x_ref, w_ref, r_ref, g_ref, rows_ref, columns_ref, entering_ref, leaving_ref,
    grad_input_ref, grad_write_ref, grad_read_ref,
):
    length = x_ref.shape[0]
    heads = rows_ref.shape[0]
    w = w_ref[...]
    r = r_ref[...]
    row = lax.broadcasted_iota(jnp.int32, (length, length), 0)
    column = lax.broadcasted_iota(jnp.int32, (length, length), 1)
    later = column >= row
    meets = jnp.where(later, dot(w, r, (1, 1)), 0.0)
    cumulative = columns_ref[...]
    since = jnp.exp(cumulative)
    to_end = jnp.exp(cumulative[length - 1 : length, :] - cumulative)
    half = low_half(length)
    weighted = jnp.zeros((length, length), f32)
    grad_write = jnp.zeros((length, STATE), f32)
    grad_read = jnp.zeros((length, STATE), f32)
    for pair in range(heads // 2):
        lanes = slice(pair * LANES, (pair + 1) * LANES)
        x = x_ref[:, lanes]
        g = g_ref[:, lanes]
        parts = []
        for head in (2 * pair, 2 * pair + 1):
            difference = rows_ref[head : head + 1, :] - cumulative[:, head : head + 1]
            within = jnp.exp(jnp.minimum(difference, 0.0))
            parts.append(dot((within * meets).astype(bf16), g, (1, 0)))
            mine = half if head % 2 == 0 else jnp.logical_not(half)
            own = jnp.where(mine, x, jnp.zeros_like(x))
            weighted = weighted + within * dot(own, g, (1, 1))
        end_scale = pair_scale(to_end, pair, length)
        leaving = leaving_ref[:, lanes]
        carried = dot(w, leaving, (1, 0)) * end_scale
        grad_input_ref[:, lanes] = (jnp.where(half, parts[0], parts[1]) + carried).astype(bf16)
        grad_write += dot((x.astype(f32) * end_scale).astype(bf16), leaving, (1, 1))
        scaled = (g.astype(f32) * pair_scale(since, pair, length)).astype(bf16)
        grad_read += dot(scaled, entering_ref[:, lanes], (1, 1))
    weighted = jnp.where(later, weighted, 0.0).astype(bf16)
    grad_write_ref[...] = (grad_write + dot(weighted, r, (1, 0))).astype(bf16)
    grad_read_ref[...] = (grad_read + dot(weighted, w, (0, 0))).astype(bf16)


def weight_kernel(
    place_ref, c0, c1, c2, c3, m0, m1, m2, m3, mine_ref, other_ref, held, total, sems
):
    copies = []
    for m, ref in enumerate((c0, c1, c2, c3)):
        slot = lax.rem(place_ref[0] + 8 - m, 4)
        copy = pltpu.make_async_copy(ref, held.at[slot], sems.at[m])
        copy.start()
        copies.append(copy)
    for copy in copies:
        copy.wait()
    mixers = (m0, m3, m2, m1)
    acc = dot(held[0], mixers[0][...], (0, 0))
    for n in range(1, 4):
        acc = acc + dot(held[n], mixers[n][...], (0, 0))
    total[...] = acc
    ring, rows = mine_ref.shape[0], mine_ref.shape[1]
    z, core = place_ref[1], place_ref[2]
    for n in range(ring):
        target = 2 * lax.rem(z + n, ring)
        start = pl.multiple_of((target + core) * rows, rows)
        mine_ref[n] = total[pl.ds(start, rows), :].astype(bf16)
        start = pl.multiple_of((target + 1 - core) * rows, rows)
        other_ref[n] = total[pl.ds(start, rows), :].astype(bf16)


def add_kernel(mine_ref, other_ref, *outs):
    for n, out in enumerate(outs):
        out[...] = (mine_ref[n].astype(f32) + other_ref[n].astype(f32)).astype(out.dtype)


def sum_kernel(own_ref, *refs):
    *parts, out_ref = refs
    total = own_ref[...].astype(f32)
    for part in parts:
        total = total + part[...].astype(f32)
    out_ref[...] = total


def shape(dims, dtype=bf16):
    return jax.ShapeDtypeStruct(dims, dtype)


def per_device(
    head_input, write_vectors, read_vectors, log_decay, cotangent, out_weight, scale_exponent
):
    dp, ctx, tp = (lax.axis_size(name) for name in ("dp", "ctx", "tp"))
    ring = ctx // 2
    mine_dp, mine_ctx, mine_tp = (lax.axis_index(name) for name in ("dp", "ctx", "tp"))
    x, w, r = head_input[0], write_vectors[0], read_vectors[0]
    length, columns = x.shape
    heads = log_decay.shape[1]
    place = jnp.stack(
        [mine_tp - mine_dp + dp, mine_ctx // 2, lax.rem(mine_ctx, 2)]
    ).astype(jnp.int32)

    def across(value, m):
        pairs = [
            (a * tp + k, k * tp + (a + m) % tp) for a in range(dp) for k in range(tp)
        ]
        return lax.ppermute(value, ("dp", "tp"), pairs)

    def along_dp(value, n):
        return lax.ppermute(value, "dp", [(i, (i + n) % dp) for i in range(dp)])

    def along_z(value, n):
        return lax.ppermute(value, "ctx", [(i, (i + 2 * n) % ctx) for i in range(ctx)])

    def other_core(value):
        return lax.ppermute(value, "ctx", [(i, i ^ 1) for i in range(ctx)])

    cots = [across(cotangent[0], m) for m in range(tp)]
    scales = jnp.exp2(scale_exponent.astype(f32))
    dequant = (out_weight.astype(f32) * jnp.repeat(scales, SCALE_BLOCK, axis=0)).astype(bf16)
    weight = lax.all_gather(dequant, "ctx", axis=0, tiled=True)

    packed, cum_rows, cum_columns = call(
        state_kernel,
        [shape((STATE, columns + LANES)), shape((heads, length), f32), shape((length, LANES), f32)],
        3,
    )(x, w, log_decay[0])
    packed = lax.all_to_all(packed, "ctx", 0, 0, tiled=True)
    entering, decays = call(
        forward_scan_kernel, [shape((STATE, columns)), shape((ctx, columns), f32)], 1
    )(packed)
    entering = lax.all_to_all(entering, "ctx", 0, 0, tiled=True)
    mixer = call(mixer_kernel, shape((length, columns)), 6)(
        x, w, r, cum_rows, cum_columns, entering
    )
    mixers = [mixer] + [along_dp(mixer, n) for n in range(1, dp)]

    smem = pl.BlockSpec(memory_space=pltpu.SMEM)
    vmem = pl.BlockSpec(memory_space=pltpu.VMEM)
    anywhere = pl.BlockSpec(memory_space=pl.ANY)
    model = cotangent.shape[2]
    parts = call(
        project_kernel,
        [shape((length, columns))] * dp,
        6,
        scratch=[pltpu.VMEM((dp, length, model), bf16), pltpu.SemaphoreType.DMA((dp,))],
        in_specs=[smem] + [anywhere] * dp + [vmem],
    )(place, *cots, weight)
    arrived = [along_dp(parts[n], n) for n in range(1, dp)]
    grad, summary = call(adjoint_kernel, [shape((length, columns)), shape((STATE, columns))], 6)(
        parts[0], *arrived, r, cum_columns
    )
    summary = lax.all_to_all(summary, "ctx", 0, 0, tiled=True)
    leaving = call(backward_scan_kernel, shape((STATE, columns)), 2)(summary, decays)
    leaving = lax.all_to_all(leaving, "ctx", 0, 0, tiled=True)

    rows = model // ctx
    mine, other = call(
        weight_kernel,
        [shape((ring, rows, columns))] * 2,
        9,
        scratch=[
            pltpu.VMEM((dp, length, model), bf16),
            pltpu.VMEM((model, columns), f32),
            pltpu.SemaphoreType.DMA((dp,)),
        ],
        in_specs=[smem] + [anywhere] * dp + [vmem] * dp,
    )(place, *cots, *mixers)
    other = other_core(other)
    blocks = call(add_kernel, [shape((rows, columns))] * ring, 2)(mine, other)
    received = [along_z(blocks[n], n) for n in range(1, ring)]
    grad_weight = call(sum_kernel, shape((rows, columns), f32), ring)(blocks[0], *received)

    grad_input, grad_write, grad_read = call(
        gradients_kernel,
        [shape((length, columns)), shape((length, STATE)), shape((length, STATE))],
        8,
    )(x, w, r, grad, cum_rows, cum_columns, entering, leaving)
    return grad_input[None], grad_write[None], grad_read[None], grad_weight


def solution(mesh):
    return jax.shard_map(
        per_device,
        mesh=mesh,
        in_specs=(
            P("dp", "ctx", "tp"),
            P("dp", "ctx", "tp"),
            P("dp", "ctx", "tp"),
            P("dp", "tp", "ctx"),
            P("dp", "ctx", "tp"),
            P(("dp", "ctx"), "tp"),
            P(("dp", "ctx"), "tp"),
        ),
        out_specs=(
            P("dp", "ctx", "tp"),
            P("dp", "ctx", "tp"),
            P("dp", "ctx", "tp"),
            P(("dp", "ctx"), "tp"),
        ),
        check_vma=False,
    )
```

time: 446 us -> 208 us (0.47)
  the two profiles are of different devices: /device:TPU:1 before, /device:TPU:37 now
where the time goes in v1:
time: 208 us; the launch traced here: 207 us
  waiting for transfers between devices  76.5 us (37%)
  starting transfers between devices  46.8 us (22%)
  blocking collectives  38 us (18%)
  Pallas kernels  20.3 us (10%)
  between operations  14.2 us (7%)
  local copies, waits for them, and re-layouts  8.44 us (4%)
  other arithmetic  2.95 us (1%)
    ppermute x6, waiting for transfers between devices, along_dp(): return lax.ppermute(value, 'dp', [(i, (i + n) % dp) for i in range(dp)])  27.7 us
    ppermute x4, waiting for transfers between devices, across(): return lax.ppermute(value, ('dp', 'tp'), pairs)  24.8 us
    ppermute x7, waiting for transfers between devices, along_z(): lax.ppermute(value, 'ctx', [(i, (i + 2 * n) % ctx) for i in range(ctx)])  21.3 us
    all_to_all x1, blocking collectives, per_device(): packed = lax.all_to_all(packed, 'ctx', 0, 0, tiled=True)  21 us
    all_to_all x1, blocking collectives, per_device(): summary = lax.all_to_all(summary, 'ctx', 0, 0, tiled=True)  17 us
    ppermute x6, starting transfers between devices, along_dp(): return lax.ppermute(value, 'dp', [(i, (i + n) % dp) for i in range(dp)])  14.1 us
    ppermute x7, starting transfers between devices, along_z(): lax.ppermute(value, 'ctx', [(i, (i + 2 * n) % ctx) for i in range(ctx)])  12.6 us
    ppermute x4, starting transfers between devices, across(): return lax.ppermute(value, ('dp', 'tp'), pairs)  8.68 us
  transfers between devices with their start and end apart: 21, of which 11 were waited for; matrix products, arithmetic and copies ran while one was open for 0% of the time, Pallas kernels for 8%

profile of v1, /device:TPU:37, one launch (start us, length us, event | category | flops | bytes accessed | tf_op | source)
XLA Modules:
  0.0 207.2 jit_solution(13514058530236881197)
XLA Ops:
  7.2 0.0 all-gather.2.cloned.1.call-start
  7.2 0.7 multiply_exponential_fusion
  7.9 1.6 fusion
  9.5 0.0 all-gather.2.cloned.1.call-update
  9.5 0.0 copy-start
  9.6 1.0 copy-done
  10.6 0.8 copy-done.5
  11.4 0.7 copy-done.15
  12.1 1.3 shard_map.103
  13.5 21.0 %all_to_all.44 = bf16[16,8,1152]{2,1,0:T(8,128)(2,1)S(1)} all-to-all(bf16[16,8,1152]{2,1,0:T(8,128)(2,1)S(1)} %bitcast.37), channel_id=1, replica_groups=mesh['dp'=4,'ctx'=16,'tp'=4] {'ctx'}, dimensions={0} | all-to-all | bytes 589824 | tf_op jit(solution)/shard_map/all_to_all | solution.py:303
  34.4 1.0 shard_map.105
  35.5 0.6 copy-done.13
  36.1 5.8 %all-to-all-start.1 = ((bf16[16,8,1024]{2,1,0:T(8,128)(2,1)}), bf16[16,8,1024]{2,1,0:T(8,128)(2,1)S(1)}, u32[]{:S(2)}, u32[]{:S(2)}) async-start(bf16[16,8,1024]{2,1,0:T(8,128)(2,1)} %bitcast.11), calls=%async_computation.1 | async-start | bytes 524288 | tf_op jit(solution)/shard_map/all_to_all | solution.py:307
  41.9 4.8 %collective-permute-start = (bf16[256,1024]{1,0:T(8,128)(2,1)}, bf16[256,1024]{1,0:T(8,128)(2,1)S(1)}, u32[]{:S(2)}, u32[]{:S(2)}) collective-permute-start(bf16[256,1024]{1,0:T(8,128)(2,1)} %bitcast.40), channel_id=1, source_target_pairs={{0,0},{1,64},{2,128},{3,192},{64,1},{65,65},{66,129},{67,193},{128... | collective-permute-start | bytes 1572872 | tf_op jit(solution)/shard_map/ppermute | solution.py:282
  46.7 1.2 collective-permute-start.1
  47.9 1.2 collective-permute-start.2
  49.1 1.5 collective-permute-start.3
  50.6 2.7 %all-to-all-done.1 = bf16[16,8,1024]{2,1,0:T(8,128)(2,1)S(1)} async-done(((bf16[16,8,1024]{2,1,0:T(8,128)(2,1)}), bf16[16,8,1024]{2,1,0:T(8,128)(2,1)S(1)}, u32[]{:S(2)}, u32[]{:S(2)}) %all-to-all-start.1) | async-done | bytes 262176 | tf_op jit(solution)/shard_map/all_to_all | solution.py:307
  53.3 0.8 copy-done.6
  54.1 0.8 copy-done.8
  55.0 1.4 shard_map.108.m0
  56.4 1.7 collective-permute-start.7
  58.1 12.1 %collective-permute-done.c0 = bf16[256,1024]{1,0:T(8,128)(2,1)S(1)} collective-permute-done((bf16[256,1024]{1,0:T(8,128)(2,1)}, bf16[256,1024]{1,0:T(8,128)(2,1)S(1)}, u32[]{:S(2)}, u32[]{:S(2)}) %collective-permute-start) | collective-permute-done | bytes 524320 | tf_op jit(solution)/shard_map/ppermute | solution.py:282
  70.3 12.7 %collective-permute-done.1.c1 = bf16[256,1024]{1,0:T(8,128)(2,1)S(1)} collective-permute-done((bf16[256,1024]{1,0:T(8,128)(2,1)}, bf16[256,1024]{1,0:T(8,128)(2,1)S(1)}, u32[]{:S(2)}, u32[]{:S(2)}) %collective-permute-start.1) | collective-permute-done | bytes 524320 | tf_op jit(solution)/shard_map/ppermute | solution.py:282
  82.9 9.7 %collective-permute-start.9 = (bf16[256,1024]{1,0:T(8,128)(2,1)S(1)}, bf16[256,1024]{1,0:T(8,128)(2,1)}, u32[]{:S(2)}, u32[]{:S(2)}) collective-permute-start(bf16[256,1024]{1,0:T(8,128)(2,1)S(1)} %shard_map.108.m0), channel_id=1, source_target_pairs={{0,192},{64,0},{128,64},{192,128},{1,193},{65,1},{129,65},{193,129... | collective-permute-start | bytes 1572872 | tf_op jit(solution)/shard_map/ppermute | solution.py:285
  92.6 0.7 pad_add_fusion.place_ref
  93.3 0.0 all-gather.2.cloned.1.call-done.weight_ref
  93.3 0.8 copy-done.2
  94.1 0.7 copy-done.16
  94.7 5.1 %shard_map.102 = (bf16[256,1024]{1,0:T(8,128)(2,1)S(1)}, bf16[256,1024]{1,0:T(8,128)(2,1)S(1)}, bf16[256,1024]{1,0:T(8,128)(2,1)S(1)}, bf16[256,1024]{1,0:T(8,128)(2,1)S(1)}) custom-call(s32[3]{0:T(128)S(1)} %copy-done.16, bf16[256,1024]{1,0:T(8,128)(2,1)S(1)} %collective-permute-done.c0, bf16[256,1024]{1,0:T(8,128)(2,1)S(1)} %collective-permute-done.1.c1, ...), custom_call_target="tpu_custom_call" | custom-call | tf_op jit(solution)/shard_map/pallas_call | solution.py:317
  99.9 0.1 collective-permute-start.4
  100.0 1.3 collective-permute-start.5
  101.2 0.0 collective-permute-done.7.m1
  101.2 1.4 collective-permute-start.6
  102.6 0.0 collective-permute-done.8.m2
  102.6 12.5 %collective-permute-done.9.m3 = bf16[256,1024]{1,0:T(8,128)(2,1)} collective-permute-done((bf16[256,1024]{1,0:T(8,128)(2,1)S(1)}, bf16[256,1024]{1,0:T(8,128)(2,1)}, u32[]{:S(2)}, u32[]{:S(2)}) %collective-permute-start.9) | collective-permute-done | bytes 524320 | tf_op jit(solution)/shard_map/ppermute | solution.py:285
  115.1 1.0 copy-done.3
  116.2 5.4 %shard_map.109 = (bf16[8,64,1024]{2,1,0:T(8,128)(2,1)}, bf16[8,64,1024]{2,1,0:T(8,128)(2,1)}) custom-call(s32[3]{0:T(128)S(1)} %copy-done.16, bf16[256,1024]{1,0:T(8,128)(2,1)S(1)} %collective-permute-done.c0, bf16[256,1024]{1,0:T(8,128)(2,1)S(1)} %collective-permute-done.1.c1, bf16[256,1024]{1,0:T(8,128)(2,1)S(1)} %collective-permute-done.2.c2, ...), custom_call_target="tpu_custom_call" | custom-call | tf_op jit(solution)/shard_map/pallas_call | solution.py:333
  121.6 0.0 copy-start.14
  121.7 0.7 collective-permute-start.10
  122.3 15.2 %collective-permute-done.6.g3 = bf16[256,1024]{1,0:T(8,128)(2,1)S(1)} collective-permute-done((bf16[256,1024]{1,0:T(8,128)(2,1)S(1)}, bf16[256,1024]{1,0:T(8,128)(2,1)S(1)}, u32[]{:S(2)}, u32[]{:S(2)}) %collective-permute-start.6) | collective-permute-done | bytes 524320 | tf_op jit(solution)/shard_map/ppermute | solution.py:285
  137.5 1.0 shard_map.104
  138.6 0.0 copy-start.11
  138.6 17.0 %all_to_all.45 = bf16[16,8,1024]{2,1,0:T(8,128)(2,1)S(1)} all-to-all(bf16[16,8,1024]{2,1,0:T(8,128)(2,1)S(1)} %bitcast.38), channel_id=1, replica_groups=mesh['dp'=4,'ctx'=16,'tp'=4] {'ctx'}, dimensions={0} | all-to-all | bytes 524288 | tf_op jit(solution)/shard_map/all_to_all | solution.py:328
  155.5 0.8 shard_map.106
  156.4 4.9 %all-to-all-start.3 = ((bf16[16,8,1024]{2,1,0:T(8,128)(2,1)}), bf16[16,8,1024]{2,1,0:T(8,128)(2,1)S(1)}, u32[]{:S(2)}, u32[]{:S(2)}) async-start(bf16[16,8,1024]{2,1,0:T(8,128)(2,1)} %bitcast.15), calls=%async_computation.3 | async-start | bytes 524288 | tf_op jit(solution)/shard_map/all_to_all | solution.py:330
  161.3 0.2 shard_map.110
  161.5 1.3 collective-permute-start.11
  162.8 3.3 %collective-permute-start.12 = (bf16[64,1024]{1,0:T(8,128)(2,1)S(1)}, bf16[64,1024]{1,0:T(8,128)(2,1)S(1)}, u32[]{:S(2)}, u32[]{:S(2)}) collective-permute-start(bf16[64,1024]{1,0:T(8,128)(2,1)S(1)} %get-tuple-element.46), channel_id=1, source_target_pairs={{0,16},{4,20},{8,24},{12,28},{16,32},{20,36},{24,40},{28,44},{32,4... | collective-permute-start | bytes 393224 | tf_op jit(solution)/shard_map/ppermute | solution.py:288
  166.1 0.3 collective-permute-start.13
  166.5 2.9 %collective-permute-start.14 = (bf16[64,1024]{1,0:T(8,128)(2,1)S(1)}, bf16[64,1024]{1,0:T(8,128)(2,1)S(1)}, u32[]{:S(2)}, u32[]{:S(2)}) collective-permute-start(bf16[64,1024]{1,0:T(8,128)(2,1)S(1)} %get-tuple-element.48), channel_id=1, source_target_pairs={{0,32},{4,36},{8,40},{12,44},{16,48},{20,52},{24,56},{28,60},{32,0... | collective-permute-start | bytes 393224 | tf_op jit(solution)/shard_map/ppermute | solution.py:288
  169.4 1.8 collective-permute-start.15
  171.2 0.2 collective-permute-done.11.refs_0_
  171.4 3.0 %collective-permute-start.16 = (bf16[64,1024]{1,0:T(8,128)(2,1)S(1)}, bf16[64,1024]{1,0:T(8,128)(2,1)S(1)}, u32[]{:S(2)}, u32[]{:S(2)}) collective-permute-start(bf16[64,1024]{1,0:T(8,128)(2,1)S(1)} %get-tuple-element.50), channel_id=1, source_target_pairs={{0,48},{4,52},{8,56},{12,60},{16,0},{20,4},{24,8},{28,12},{32,16},... | collective-permute-start | bytes 393224 | tf_op jit(solution)/shard_map/ppermute | solution.py:288
  174.3 4.5 %collective-permute-done.12.refs_1_ = bf16[64,1024]{1,0:T(8,128)(2,1)S(1)} collective-permute-done((bf16[64,1024]{1,0:T(8,128)(2,1)S(1)}, bf16[64,1024]{1,0:T(8,128)(2,1)S(1)}, u32[]{:S(2)}, u32[]{:S(2)}) %collective-permute-start.12) | collective-permute-done | bytes 131104 | tf_op jit(solution)/shard_map/ppermute | solution.py:288
  178.8 0.0 collective-permute-start.17
  178.8 4.8 %collective-permute-done.13.refs_2_ = bf16[64,1024]{1,0:T(8,128)(2,1)S(1)} collective-permute-done((bf16[64,1024]{1,0:T(8,128)(2,1)S(1)}, bf16[64,1024]{1,0:T(8,128)(2,1)S(1)}, u32[]{:S(2)}, u32[]{:S(2)}) %collective-permute-start.13) | collective-permute-done | bytes 131104 | tf_op jit(solution)/shard_map/ppermute | solution.py:288
  183.6 4.1 %collective-permute-done.15.refs_4_ = bf16[64,1024]{1,0:T(8,128)(2,1)S(1)} collective-permute-done((bf16[64,1024]{1,0:T(8,128)(2,1)S(1)}, bf16[64,1024]{1,0:T(8,128)(2,1)S(1)}, u32[]{:S(2)}, u32[]{:S(2)}) %collective-permute-start.15) | collective-permute-done | bytes 131104 | tf_op jit(solution)/shard_map/ppermute | solution.py:288
  187.7 2.0 collective-permute-done.16.refs_5_
  189.7 5.7 %collective-permute-done.17.refs_6_ = bf16[64,1024]{1,0:T(8,128)(2,1)S(1)} collective-permute-done((bf16[64,1024]{1,0:T(8,128)(2,1)S(1)}, bf16[64,1024]{1,0:T(8,128)(2,1)S(1)}, u32[]{:S(2)}, u32[]{:S(2)}) %collective-permute-start.17) | collective-permute-done | bytes 131104 | tf_op jit(solution)/shard_map/ppermute | solution.py:288
  195.4 0.8 shard_map.111
  196.3 0.0 copy-start.12
  196.3 1.0 copy-done.12
  197.3 3.1 %shard_map.107 = (bf16[256,1024]{1,0:T(8,128)(2,1)}, bf16[256,128]{1,0:T(8,128)(2,1)}, bf16[256,128]{1,0:T(8,128)(2,1)}) custom-call(bf16[256,1024]{1,0:T(8,128)(2,1)S(1)} %bitcast.25, bf16[256,128]{1,0:T(8,128)(2,1)S(1)} %bitcast.33, bf16[256,128]{1,0:T(8,128)(2,1)S(1)} %bitcast.36, bf16[256,1024]{1,0:T(8,128)(2,1)S(1)} %copy-done.12, ...), custom_call_target="tpu_custom_call" | custom-call | tf_op jit(solution)/shard_map/pallas_call | solution.py:349
  (28 shorter events, 0.1 us)
Async XLA Ops:
  7.2 86.1 %all-gather.2.cloned.1.call-start = ((), (), s32[]{:S(2)}) async-start(), calls=%async_computation.4 | async-start | bytes 2228224 | tf_op jit(solution)/shard_map/all_gather | solution.py:296
  9.5 1.0 copy-start
  10.6 0.8 copy-start.5
  11.4 0.7 copy-start.15
  12.1 41.2 %copy-start.1 = (bf16[1,256,1024]{2,1,0:T(8,128)(2,1)S(1)}, bf16[1,256,1024]{2,1,0:T(8,128)(2,1)}, u32[]{:S(2)}) copy-start(bf16[1,256,1024]{2,1,0:T(8,128)(2,1)} %param.7) | copy-start | bytes 1572868
  35.5 0.6 copy-start.13
  36.1 17.2 %all-to-all-start.1 = ((bf16[16,8,1024]{2,1,0:T(8,128)(2,1)}), bf16[16,8,1024]{2,1,0:T(8,128)(2,1)S(1)}, u32[]{:S(2)}, u32[]{:S(2)}) async-start(bf16[16,8,1024]{2,1,0:T(8,128)(2,1)} %bitcast.11), calls=%async_computation.1 | async-start | bytes 524288 | tf_op jit(solution)/shard_map/all_to_all | solution.py:307
  41.9 28.4 %collective-permute-start = (bf16[256,1024]{1,0:T(8,128)(2,1)}, bf16[256,1024]{1,0:T(8,128)(2,1)S(1)}, u32[]{:S(2)}, u32[]{:S(2)}) collective-permute-start(bf16[256,1024]{1,0:T(8,128)(2,1)} %bitcast.40), channel_id=1, source_target_pairs={{0,0},{1,64},{2,128},{3,192},{64,1},{65,65},{66,129},{67,193},{128... | collective-permute-start | bytes 1572872 | tf_op jit(solution)/shard_map/ppermute | solution.py:282
  46.7 36.2 %collective-permute-start.1 = (bf16[256,1024]{1,0:T(8,128)(2,1)}, bf16[256,1024]{1,0:T(8,128)(2,1)S(1)}, u32[]{:S(2)}, u32[]{:S(2)}) collective-permute-start(bf16[256,1024]{1,0:T(8,128)(2,1)} %bitcast.41), channel_id=1, source_target_pairs={{0,1},{1,65},{2,129},{3,193},{64,2},{65,66},{66,130},{67,194},{128... | collective-permute-start | bytes 1572872 | tf_op jit(solution)/shard_map/ppermute | solution.py:282
  47.9 45.3 %collective-permute-start.2 = (bf16[256,1024]{1,0:T(8,128)(2,1)}, bf16[256,1024]{1,0:T(8,128)(2,1)S(1)}, u32[]{:S(2)}, u32[]{:S(2)}) collective-permute-start(bf16[256,1024]{1,0:T(8,128)(2,1)} %bitcast.42), channel_id=1, source_target_pairs={{0,2},{1,66},{2,130},{3,194},{64,3},{65,67},{66,131},{67,195},{128... | collective-permute-start | bytes 1572872 | tf_op jit(solution)/shard_map/ppermute | solution.py:282
  49.1 44.2 %collective-permute-start.3 = (bf16[256,1024]{1,0:T(8,128)(2,1)}, bf16[256,1024]{1,0:T(8,128)(2,1)S(1)}, u32[]{:S(2)}, u32[]{:S(2)}) collective-permute-start(bf16[256,1024]{1,0:T(8,128)(2,1)} %bitcast.43), channel_id=1, source_target_pairs={{0,3},{1,67},{2,131},{3,195},{64,0},{65,64},{66,128},{67,192},{128... | collective-permute-start | bytes 1572872 | tf_op jit(solution)/shard_map/ppermute | solution.py:282
  53.3 0.8 copy-start.6
  54.1 0.8 copy-start.8
  56.4 44.8 %collective-permute-start.7 = (bf16[256,1024]{1,0:T(8,128)(2,1)S(1)}, bf16[256,1024]{1,0:T(8,128)(2,1)}, u32[]{:S(2)}, u32[]{:S(2)}) collective-permute-start(bf16[256,1024]{1,0:T(8,128)(2,1)S(1)} %shard_map.108.m0), channel_id=1, source_target_pairs={{0,64},{64,128},{128,192},{192,0},{1,65},{65,129},{129,193},{193,1... | collective-permute-start | bytes 1572872 | tf_op jit(solution)/shard_map/ppermute | solution.py:285
  70.3 32.4 %collective-permute-start.8 = (bf16[256,1024]{1,0:T(8,128)(2,1)S(1)}, bf16[256,1024]{1,0:T(8,128)(2,1)}, u32[]{:S(2)}, u32[]{:S(2)}) collective-permute-start(bf16[256,1024]{1,0:T(8,128)(2,1)S(1)} %shard_map.108.m0), channel_id=1, source_target_pairs={{0,128},{64,192},{128,0},{192,64},{1,129},{65,193},{129,1},{193,65... | collective-permute-start | bytes 1572872 | tf_op jit(solution)/shard_map/ppermute | solution.py:285
  82.9 32.2 %collective-permute-start.9 = (bf16[256,1024]{1,0:T(8,128)(2,1)S(1)}, bf16[256,1024]{1,0:T(8,128)(2,1)}, u32[]{:S(2)}, u32[]{:S(2)}) collective-permute-start(bf16[256,1024]{1,0:T(8,128)(2,1)S(1)} %shard_map.108.m0), channel_id=1, source_target_pairs={{0,192},{64,0},{128,64},{192,128},{1,193},{65,1},{129,65},{193,129... | collective-permute-start | bytes 1572872 | tf_op jit(solution)/shard_map/ppermute | solution.py:285
  93.3 0.8 copy-start.2
  94.0 0.7 copy-start.16
  99.9 22.5 %collective-permute-start.4 = (bf16[256,1024]{1,0:T(8,128)(2,1)S(1)}, bf16[256,1024]{1,0:T(8,128)(2,1)S(1)}, u32[]{:S(2)}, u32[]{:S(2)}) collective-permute-start(bf16[256,1024]{1,0:T(8,128)(2,1)S(1)} %get-tuple-element.29), channel_id=1, source_target_pairs={{0,64},{64,128},{128,192},{192,0},{1,65},{65,129},{129,193},{193,1... | collective-permute-start | bytes 1572872 | tf_op jit(solution)/shard_map/ppermute | solution.py:285
  100.0 22.4 %collective-permute-start.5 = (bf16[256,1024]{1,0:T(8,128)(2,1)S(1)}, bf16[256,1024]{1,0:T(8,128)(2,1)S(1)}, u32[]{:S(2)}, u32[]{:S(2)}) collective-permute-start(bf16[256,1024]{1,0:T(8,128)(2,1)S(1)} %get-tuple-element.30), channel_id=1, source_target_pairs={{0,128},{64,192},{128,0},{192,64},{1,129},{65,193},{129,1},{193,65... | collective-permute-start | bytes 1572872 | tf_op jit(solution)/shard_map/ppermute | solution.py:285
  101.2 36.3 %collective-permute-start.6 = (bf16[256,1024]{1,0:T(8,128)(2,1)S(1)}, bf16[256,1024]{1,0:T(8,128)(2,1)S(1)}, u32[]{:S(2)}, u32[]{:S(2)}) collective-permute-start(bf16[256,1024]{1,0:T(8,128)(2,1)S(1)} %get-tuple-element.31), channel_id=1, source_target_pairs={{0,192},{64,0},{128,64},{192,128},{1,193},{65,1},{129,65},{193,129... | collective-permute-start | bytes 1572872 | tf_op jit(solution)/shard_map/ppermute | solution.py:285
  115.1 1.0 copy-start.3
  116.2 21.4 %copy-start.9 = (bf16[1,256,128]{2,1,0:T(8,128)(2,1)S(1)}, bf16[1,256,128]{2,1,0:T(8,128)(2,1)}, u32[]{:S(2)}) copy-start(bf16[1,256,128]{2,1,0:T(8,128)(2,1)} %param.9) | copy-start | bytes 196612
  121.6 33.9 %copy-start.14 = (f32[16,1024]{1,0:T(8,128)S(1)}, f32[16,1024]{1,0:T(8,128)}, u32[]{:S(2)}) copy-start(f32[16,1024]{1,0:T(8,128)} %copy-done.13) | copy-start | bytes 196612
  121.6 39.6 %copy-start.4 = (bf16[8,64,1024]{2,1,0:T(8,128)(2,1)S(1)}, bf16[8,64,1024]{2,1,0:T(8,128)(2,1)}, u32[]{:S(2)}) copy-start(bf16[8,64,1024]{2,1,0:T(8,128)(2,1)} %get-tuple-element.42.mine_ref) | copy-start | bytes 3145732
  121.7 39.6 %collective-permute-start.10 = (bf16[8,64,1024]{2,1,0:T(8,128)(2,1)}, bf16[8,64,1024]{2,1,0:T(8,128)(2,1)S(1)}, u32[]{:S(2)}, u32[]{:S(2)}) collective-permute-start(bf16[8,64,1024]{2,1,0:T(8,128)(2,1)} %get-tuple-element.43), channel_id=1, source_target_pairs={{0,4},{4,0},{8,12},{12,8},{16,20},{20,16},{24,28},{28,24},{32,36},... | collective-permute-start | bytes 3145736 | tf_op jit(solution)/shard_map/ppermute | solution.py:291
  138.6 17.8 %copy-start.11 = (bf16[256,1024]{1,0:T(8,128)(2,1)}, bf16[256,1024]{1,0:T(8,128)(2,1)S(1)}, u32[]{:S(2)}) copy-start(bf16[256,1024]{1,0:T(8,128)(2,1)S(1)} %get-tuple-element.33.g_ref) | copy-start | bytes 1572868
  156.4 39.9 %copy-start.7 = (bf16[1,256,128]{2,1,0:T(8,128)(2,1)S(1)}, bf16[1,256,128]{2,1,0:T(8,128)(2,1)}, u32[]{:S(2)}) copy-start(bf16[1,256,128]{2,1,0:T(8,128)(2,1)} %param.8) | copy-start | bytes 196612
  156.4 39.9 %copy-start.10 = (bf16[1,256,128]{2,1,0:T(8,128)(2,1)S(1)}, bf16[1,256,128]{2,1,0:T(8,128)(2,1)}, u32[]{:S(2)}) copy-start(bf16[1,256,128]{2,1,0:T(8,128)(2,1)} %param.9) | copy-start | bytes 196612
  156.4 39.9 %all-to-all-start.3 = ((bf16[16,8,1024]{2,1,0:T(8,128)(2,1)}), bf16[16,8,1024]{2,1,0:T(8,128)(2,1)S(1)}, u32[]{:S(2)}, u32[]{:S(2)}) async-start(bf16[16,8,1024]{2,1,0:T(8,128)(2,1)} %bitcast.15), calls=%async_computation.3 | async-start | bytes 524288 | tf_op jit(solution)/shard_map/all_to_all | solution.py:330
  161.5 9.8 %collective-permute-start.11 = (bf16[64,1024]{1,0:T(8,128)(2,1)S(1)}, bf16[64,1024]{1,0:T(8,128)(2,1)S(1)}, u32[]{:S(2)}, u32[]{:S(2)}) collective-permute-start(bf16[64,1024]{1,0:T(8,128)(2,1)S(1)} %get-tuple-element.45), channel_id=1, source_target_pairs={{0,8},{4,12},{8,16},{12,20},{16,24},{20,28},{24,32},{28,36},{32,40... | collective-permute-start | bytes 393224 | tf_op jit(solution)/shard_map/ppermute | solution.py:288
  162.8 16.0 %collective-permute-start.12 = (bf16[64,1024]{1,0:T(8,128)(2,1)S(1)}, bf16[64,1024]{1,0:T(8,128)(2,1)S(1)}, u32[]{:S(2)}, u32[]{:S(2)}) collective-permute-start(bf16[64,1024]{1,0:T(8,128)(2,1)S(1)} %get-tuple-element.46), channel_id=1, source_target_pairs={{0,16},{4,20},{8,24},{12,28},{16,32},{20,36},{24,40},{28,44},{32,4... | collective-permute-start | bytes 393224 | tf_op jit(solution)/shard_map/ppermute | solution.py:288
  166.1 17.4 %collective-permute-start.13 = (bf16[64,1024]{1,0:T(8,128)(2,1)S(1)}, bf16[64,1024]{1,0:T(8,128)(2,1)S(1)}, u32[]{:S(2)}, u32[]{:S(2)}) collective-permute-start(bf16[64,1024]{1,0:T(8,128)(2,1)S(1)} %get-tuple-element.47), channel_id=1, source_target_pairs={{0,24},{4,28},{8,32},{12,36},{16,40},{20,44},{24,48},{28,52},{32,5... | collective-permute-start | bytes 393224 | tf_op jit(solution)/shard_map/ppermute | solution.py:288
  166.5 17.1 %collective-permute-start.14 = (bf16[64,1024]{1,0:T(8,128)(2,1)S(1)}, bf16[64,1024]{1,0:T(8,128)(2,1)S(1)}, u32[]{:S(2)}, u32[]{:S(2)}) collective-permute-start(bf16[64,1024]{1,0:T(8,128)(2,1)S(1)} %get-tuple-element.48), channel_id=1, source_target_pairs={{0,32},{4,36},{8,40},{12,44},{16,48},{20,52},{24,56},{28,60},{32,0... | collective-permute-start | bytes 393224 | tf_op jit(solution)/shard_map/ppermute | solution.py:288
  169.4 18.3 %collective-permute-start.15 = (bf16[64,1024]{1,0:T(8,128)(2,1)S(1)}, bf16[64,1024]{1,0:T(8,128)(2,1)S(1)}, u32[]{:S(2)}, u32[]{:S(2)}) collective-permute-start(bf16[64,1024]{1,0:T(8,128)(2,1)S(1)} %get-tuple-element.49), channel_id=1, source_target_pairs={{0,40},{4,44},{8,48},{12,52},{16,56},{20,60},{24,0},{28,4},{32,8},... | collective-permute-start | bytes 393224 | tf_op jit(solution)/shard_map/ppermute | solution.py:288
  171.4 18.4 %collective-permute-start.16 = (bf16[64,1024]{1,0:T(8,128)(2,1)S(1)}, bf16[64,1024]{1,0:T(8,128)(2,1)S(1)}, u32[]{:S(2)}, u32[]{:S(2)}) collective-permute-start(bf16[64,1024]{1,0:T(8,128)(2,1)S(1)} %get-tuple-element.50), channel_id=1, source_target_pairs={{0,48},{4,52},{8,56},{12,60},{16,0},{20,4},{24,8},{28,12},{32,16},... | collective-permute-start | bytes 393224 | tf_op jit(solution)/shard_map/ppermute | solution.py:288
  178.8 16.6 %collective-permute-start.17 = (bf16[64,1024]{1,0:T(8,128)(2,1)S(1)}, bf16[64,1024]{1,0:T(8,128)(2,1)S(1)}, u32[]{:S(2)}, u32[]{:S(2)}) collective-permute-start(bf16[64,1024]{1,0:T(8,128)(2,1)S(1)} %get-tuple-element.51), channel_id=1, source_target_pairs={{0,56},{4,60},{8,0},{12,4},{16,8},{20,12},{24,16},{28,20},{32,24},... | collective-permute-start | bytes 393224 | tf_op jit(solution)/shard_map/ppermute | solution.py:288
  196.3 1.0 copy-start.12
Sparse Core Ops, SparseCore 0:
  9.8 46.2 all-gather.1

commit v2 on v1

--- a/solution.py
+++ b/solution.py
@@ -56,6 +56,15 @@
     head = lax.broadcasted_iota(jnp.int32, (LANES, heads * HEAD_DIM), 0)
     column = lax.broadcasted_iota(jnp.int32, (LANES, heads * HEAD_DIM), 1)
     return jnp.where(column // HEAD_DIM == head, 1.0, 0.0).astype(f32)
+
+
+def dequant_kernel(weight_ref, exponent_ref, out_ref):
+    scales = jnp.exp2(exponent_ref[...].astype(f32))
+    for block in range(scales.shape[0]):
+        rows = slice(block * SCALE_BLOCK, (block + 1) * SCALE_BLOCK)
+        out_ref[rows, :] = (
+            weight_ref[rows, :].astype(f32) * scales[block : block + 1, :]
+        ).astype(bf16)
 
 
 def state_kernel(x_ref, w_ref, decay_ref, packed_ref, rows_ref, columns_ref):
@@ -146,10 +155,10 @@
         out_ref[:, lanes] = (jnp.where(half, parts[0], parts[1]) + carried).astype(bf16)
 
 
-def project_kernel(place_ref, c0, c1, c2, c3, weight_ref, o0, o1, o2, o3, held, sems):
+def project_kernel(c0, c1, c2, c3, weight_ref, o0, o1, o2, o3, held, sems):
     copies = []
     for m, ref in enumerate((c0, c1, c2, c3)):
-        slot = lax.rem(place_ref[0] + 8 - m, 4)
+        slot = lax.rem(lax.axis_index("tp") - lax.axis_index("dp") + 8 - m, 4)
         copy = pltpu.make_async_copy(ref, held.at[slot], sems.at[m])
         copy.start()
         copies.append(copy)
@@ -220,11 +229,11 @@
 
 
 def weight_kernel(
-    place_ref, c0, c1, c2, c3, m0, m1, m2, m3, mine_ref, other_ref, held, total, sems
+    c0, c1, c2, c3, m0, m1, m2, m3, out_ref, held, sems
 ):
     copies = []
     for m, ref in enumerate((c0, c1, c2, c3)):
-        slot = lax.rem(place_ref[0] + 8 - m, 4)
+        slot = lax.rem(lax.axis_index("tp") - lax.axis_index("dp") + 8 - m, 4)
         copy = pltpu.make_async_copy(ref, held.at[slot], sems.at[m])
         copy.start()
         copies.append(copy)
@@ -234,28 +243,7 @@
     acc = dot(held[0], mixers[0][...], (0, 0))
     for n in range(1, 4):
         acc = acc + dot(held[n], mixers[n][...], (0, 0))
-    total[...] = acc
-    ring, rows = mine_ref.shape[0], mine_ref.shape[1]
-    z, core = place_ref[1], place_ref[2]
-    for n in range(ring):
-        target = 2 * lax.rem(z + n, ring)
-        start = pl.multiple_of((target + core) * rows, rows)
-        mine_ref[n] = total[pl.ds(start, rows), :].astype(bf16)
-        start = pl.multiple_of((target + 1 - core) * rows, rows)
-        other_ref[n] = total[pl.ds(start, rows), :].astype(bf16)
-
-
-def add_kernel(mine_ref, other_ref, *outs):
-    for n, out in enumerate(outs):
-        out[...] = (mine_ref[n].astype(f32) + other_ref[n].astype(f32)).astype(out.dtype)
-
-
-def sum_kernel(own_ref, *refs):
-    *parts, out_ref = refs
-    total = own_ref[...].astype(f32)
-    for part in parts:
-        total = total + part[...].astype(f32)
-    out_ref[...] = total
+    out_ref[...] = acc
 
 
 def shape(dims, dtype=bf16):
@@ -266,33 +254,23 @@
     head_input, write_vectors, read_vectors, log_decay, cotangent, out_weight, scale_exponent
 ):
     dp, ctx, tp = (lax.axis_size(name) for name in ("dp", "ctx", "tp"))
-    ring = ctx // 2
-    mine_dp, mine_ctx, mine_tp = (lax.axis_index(name) for name in ("dp", "ctx", "tp"))
     x, w, r = head_input[0], write_vectors[0], read_vectors[0]
     length, columns = x.shape
     heads = log_decay.shape[1]
-    place = jnp.stack(
-        [mine_tp - mine_dp + dp, mine_ctx // 2, lax.rem(mine_ctx, 2)]
-    ).astype(jnp.int32)
-
-    def across(value, m):
-        pairs = [
-            (a * tp + k, k * tp + (a + m) % tp) for a in range(dp) for k in range(tp)
-        ]
+
+    def transposed(value):
+        pairs = [(a * tp + k, k * tp + a) for a in range(dp) for k in range(tp)]
         return lax.ppermute(value, ("dp", "tp"), pairs)
+
+    def along_tp(value, n):
+        return lax.ppermute(value, "tp", [(i, (i + n) % tp) for i in range(tp)])
 
     def along_dp(value, n):
         return lax.ppermute(value, "dp", [(i, (i + n) % dp) for i in range(dp)])
 
-    def along_z(value, n):
-        return lax.ppermute(value, "ctx", [(i, (i + 2 * n) % ctx) for i in range(ctx)])
-
-    def other_core(value):
-        return lax.ppermute(value, "ctx", [(i, i ^ 1) for i in range(ctx)])
-
-    cots = [across(cotangent[0], m) for m in range(tp)]
-    scales = jnp.exp2(scale_exponent.astype(f32))
-    dequant = (out_weight.astype(f32) * jnp.repeat(scales, SCALE_BLOCK, axis=0)).astype(bf16)
+    turned = transposed(cotangent[0])
+    cots = [turned] + [along_tp(turned, m) for m in range(1, tp)]
+    dequant = call(dequant_kernel, shape(out_weight.shape), 2)(out_weight, scale_exponent)
     weight = lax.all_gather(dequant, "ctx", axis=0, tiled=True)
 
     packed, cum_rows, cum_columns = call(
@@ -305,47 +283,40 @@
         forward_scan_kernel, [shape((STATE, columns)), shape((ctx, columns), f32)], 1
     )(packed)
     entering = lax.all_to_all(entering, "ctx", 0, 0, tiled=True)
+
     mixer = call(mixer_kernel, shape((length, columns)), 6)(
         x, w, r, cum_rows, cum_columns, entering
     )
+    mixer, weight = lax.optimization_barrier((mixer, weight))
     mixers = [mixer] + [along_dp(mixer, n) for n in range(1, dp)]
 
-    smem = pl.BlockSpec(memory_space=pltpu.SMEM)
     vmem = pl.BlockSpec(memory_space=pltpu.VMEM)
     anywhere = pl.BlockSpec(memory_space=pl.ANY)
     model = cotangent.shape[2]
     parts = call(
         project_kernel,
         [shape((length, columns))] * dp,
-        6,
+        5,
         scratch=[pltpu.VMEM((dp, length, model), bf16), pltpu.SemaphoreType.DMA((dp,))],
-        in_specs=[smem] + [anywhere] * dp + [vmem],
-    )(place, *cots, weight)
+        in_specs=[anywhere] * dp + [vmem],
+    )(*cots, weight)
     arrived = [along_dp(parts[n], n) for n in range(1, dp)]
+
+    parts, mixers = lax.optimization_barrier((parts, mixers))
+    total = call(
+        weight_kernel,
+        shape((model, columns), f32),
+        8,
+        scratch=[pltpu.VMEM((dp, length, model), bf16), pltpu.SemaphoreType.DMA((dp,))],
+        in_specs=[anywhere] * dp + [vmem] * dp,
+    )(*cots, *mixers)
+    grad_weight = lax.psum_scatter(total, "ctx", scatter_dimension=0, tiled=True)
     grad, summary = call(adjoint_kernel, [shape((length, columns)), shape((STATE, columns))], 6)(
         parts[0], *arrived, r, cum_columns
     )
     summary = lax.all_to_all(summary, "ctx", 0, 0, tiled=True)
     leaving = call(backward_scan_kernel, shape((STATE, columns)), 2)(summary, decays)
     leaving = lax.all_to_all(leaving, "ctx", 0, 0, tiled=True)
-
-    rows = model // ctx
-    mine, other = call(
-        weight_kernel,
-        [shape((ring, rows, columns))] * 2,
-        9,
-        scratch=[
-            pltpu.VMEM((dp, length, model), bf16),
-            pltpu.VMEM((model, columns), f32),
-            pltpu.SemaphoreType.DMA((dp,)),
-        ],
-        in_specs=[smem] + [anywhere] * dp + [vmem] * dp,
-    )(place, *cots, *mixers)
-    other = other_core(other)
-    blocks = call(add_kernel, [shape((rows, columns))] * ring, 2)(mine, other)
-    received = [along_z(blocks[n], n) for n in range(1, ring)]
-    grad_weight = call(sum_kernel, shape((rows, columns), f32), ring)(blocks[0], *received)
-
     grad_input, grad_write, grad_read = call(
         gradients_kernel,
         [shape((length, columns)), shape((length, STATE)), shape((length, STATE))],

time: 208 us -> 175 us (0.84)
  the two profiles are of different devices: /device:TPU:37 before, /device:TPU:1 now
where the time goes in v2:
time: 175 us; the launch traced here: 174 us
  waiting for transfers between devices  52.1 us (30%)
  starting transfers between devices  43.1 us (25%)
  blocking collectives  32.5 us (19%)
  Pallas kernels  20 us (11%)
  between operations  14.2 us (8%)
  local copies, waits for them, and re-layouts  12.1 us (7%)
    ppermute x6, waiting for transfers between devices, along_dp(): return lax.ppermute(value, 'dp', [(i, (i + n) % dp) for i in range(dp)])  31.9 us
    all_to_all x1, blocking collectives, per_device(): summary = lax.all_to_all(summary, 'ctx', 0, 0, tiled=True)  17.1 us
    ppermute x3, starting transfers between devices, along_tp(): return lax.ppermute(value, 'tp', [(i, (i + n) % tp) for i in range(tp)])  16.9 us
    all_to_all x1, blocking collectives, per_device(): leaving = lax.all_to_all(leaving, 'ctx', 0, 0, tiled=True)  15.4 us
    unnamed x44, local copies, waits for them, and re-layouts  12.1 us
    all_to_all x1, waiting for transfers between devices, per_device(): entering = lax.all_to_all(entering, 'ctx', 0, 0, tiled=True)  11.3 us
    all_to_all x1, starting transfers between devices, per_device(): entering = lax.all_to_all(entering, 'ctx', 0, 0, tiled=True)  10.3 us
    all_to_all x1, starting transfers between devices, per_device(): packed = lax.all_to_all(packed, 'ctx', 0, 0, tiled=True)  9.98 us
  transfers between devices with their start and end apart: 14, of which 6 were waited for; matrix products, arithmetic and copies ran while one was open for 0% of the time, Pallas kernels for 8%

profile of v2, /device:TPU:1, one launch (start us, length us, event | category | flops | bytes accessed | tf_op | source)
XLA Modules:
  0.0 174.0 jit_solution(9054003146971641050)
XLA Ops:
  7.2 0.0 all-gather.2.cloned.1.call-start
  7.2 0.0 copy-start.10
  7.2 0.9 copy-done.10
  8.1 0.7 copy-done.14
  8.8 0.7 shard_map.105
  9.5 0.0 all-gather.2.cloned.1.call-update
  9.5 1.7 collective-permute-start
  11.2 1.0 copy-done
  12.3 0.8 copy-done.5
  13.1 0.7 copy-done.13
  13.8 2.0 %shard_map.102 = (bf16[128,1152]{1,0:T(8,128)(2,1)}, f32[16,256]{1,0:T(8,128)S(1)}, f32[256,128]{1,0:T(8,128)S(1)}) custom-call(bf16[256,1024]{1,0:T(8,128)(2,1)S(1)} %bitcast.16, bf16[256,128]{1,0:T(8,128)(2,1)S(1)} %bitcast.25, f32[16,256]{1,0:T(8,128)S(1)} %bitcast.32), custom_call_target="tpu_custom_call" | custom-call | tf_op jit(solution)/shard_map/pallas_call | solution.py:276
  15.8 10.0 %all-to-all-start = ((bf16[16,8,1152]{2,1,0:T(8,128)(2,1)}), bf16[16,8,1152]{2,1,0:T(8,128)(2,1)S(1)}, u32[]{:S(2)}, u32[]{:S(2)}) async-start(bf16[16,8,1152]{2,1,0:T(8,128)(2,1)} %bitcast.5), calls=%async_computation | async-start | bytes 589824 | tf_op jit(solution)/shard_map/all_to_all | solution.py:281
  25.8 0.0 collective-permute-done.c0
  25.8 16.4 %collective-permute-start.3 = (bf16[256,1024]{1,0:T(8,128)(2,1)S(1)}, bf16[256,1024]{1,0:T(8,128)(2,1)S(1)}, u32[]{:S(2)}, u32[]{:S(2)}) collective-permute-start(bf16[256,1024]{1,0:T(8,128)(2,1)S(1)} %collective-permute-done.c0), channel_id=1, source_target_pairs={{0,3},{1,0},{2,1},{3,2},{4,7},{5,4},{6,5},{7,6},{8,11},{9,8},{10,9... | collective-permute-start | bytes 1572872 | tf_op jit(solution)/shard_map/ppermute | solution.py:266
  42.3 0.0 all-to-all-done
  42.3 1.0 shard_map.103
  43.3 0.6 copy-done.11
  44.0 10.3 %all-to-all-start.1 = ((bf16[16,8,1024]{2,1,0:T(8,128)(2,1)}), bf16[16,8,1024]{2,1,0:T(8,128)(2,1)S(1)}, u32[]{:S(2)}, u32[]{:S(2)}) async-start(bf16[16,8,1024]{2,1,0:T(8,128)(2,1)} %bitcast.7), calls=%async_computation.1 | async-start | bytes 524288 | tf_op jit(solution)/shard_map/all_to_all | solution.py:285
  54.3 0.0 reduce-scatter.2.cloned.1.call-start
  54.3 0.1 collective-permute-start.2
  54.4 0.3 collective-permute-start.1
  54.7 11.3 %all-to-all-done.1 = bf16[16,8,1024]{2,1,0:T(8,128)(2,1)S(1)} async-done(((bf16[16,8,1024]{2,1,0:T(8,128)(2,1)}), bf16[16,8,1024]{2,1,0:T(8,128)(2,1)S(1)}, u32[]{:S(2)}, u32[]{:S(2)}) %all-to-all-start.1) | async-done | bytes 262176 | tf_op jit(solution)/shard_map/all_to_all | solution.py:285
  66.0 1.0 copy-done.1
  67.0 0.8 copy-done.6
  67.9 0.8 copy-done.8
  68.7 1.4 shard_map.104.m0
  70.1 0.0 all-gather.2.cloned.1.call-done.weight_ref
  70.2 0.1 collective-permute-start.6
  70.3 0.6 collective-permute-start.5
  70.8 0.0 collective-permute-done.3.c3
  70.8 1.0 collective-permute-start.4
  71.8 0.0 collective-permute-done.2.c2
  71.8 8.8 %collective-permute-done.1.c1 = bf16[256,1024]{1,0:T(8,128)(2,1)S(1)} collective-permute-done((bf16[256,1024]{1,0:T(8,128)(2,1)S(1)}, bf16[256,1024]{1,0:T(8,128)(2,1)S(1)}, u32[]{:S(2)}, u32[]{:S(2)}) %collective-permute-start.1) | collective-permute-done | bytes 524320 | tf_op jit(solution)/shard_map/ppermute | solution.py:266
  80.6 0.0 copy-done.3
  80.6 5.1 %shard_map.106 = (bf16[256,1024]{1,0:T(8,128)(2,1)S(1)}, bf16[256,1024]{1,0:T(8,128)(2,1)S(1)}, bf16[256,1024]{1,0:T(8,128)(2,1)S(1)}, bf16[256,1024]{1,0:T(8,128)(2,1)S(1)}) custom-call(bf16[256,1024]{1,0:T(8,128)(2,1)S(1)} %collective-permute-done.c0, bf16[256,1024]{1,0:T(8,128)(2,1)S(1)} %collective-permute-done.1.c1, ...), custom_call_target="tpu_custom_call" | custom-call | tf_op jit(solution)/shard_map/pallas_call | solution.py:296
  85.7 0.0 copy-start.15
  85.7 0.8 copy-done.15
  86.5 0.8 copy-done.17
  87.4 0.8 copy-done.19
  88.2 0.0 collective-permute-done.6.m3
  88.2 0.0 collective-permute-done.5.m2
  88.2 8.8 %collective-permute-done.4.m1 = bf16[256,1024]{1,0:T(8,128)(2,1)S(1)} collective-permute-done((bf16[256,1024]{1,0:T(8,128)(2,1)S(1)}, bf16[256,1024]{1,0:T(8,128)(2,1)S(1)}, u32[]{:S(2)}, u32[]{:S(2)}) %collective-permute-start.4) | collective-permute-done | bytes 524320 | tf_op jit(solution)/shard_map/ppermute | solution.py:269
  97.0 0.0 copy-done.21
  97.0 1.0 copy-done.4
  98.0 5.6 %shard_map.110 = f32[1024,1024]{1,0:T(8,128)} custom-call(bf16[256,1024]{1,0:T(8,128)(2,1)S(1)} %collective-permute-done.c0, bf16[256,1024]{1,0:T(8,128)(2,1)S(1)} %collective-permute-done.1.c1, bf16[256,1024]{1,0:T(8,128)(2,1)S(1)} %collective-permute-done.2.c2, bf16[256,1024]{1,0:T(8,128)(2,1)S(1)} %copy-done.4, bf16[256,1024]{1,0:T(8,128)(2,1)S(1)} %shard_map.104.m0, ...), custom_call_target="tpu_custom_call" | custom-call | tf_op jit(solution)/shard_map/pallas_call | solution.py:306
  103.7 0.0 copy-start.9
  103.7 0.0 copy-start.12
  103.7 0.0 copy-start.2
  103.7 0.0 copy-start.7
  103.7 0.0 reduce-scatter.2.cloned.1.call-update
  103.7 0.9 copy-done.20
  104.7 0.0 collective-permute-start.7
  104.7 0.2 copy-done.18
  104.8 1.8 %collective-permute-start.8 = (bf16[256,1024]{1,0:T(8,128)(2,1)S(1)}, bf16[256,1024]{1,0:T(8,128)(2,1)S(1)}, u32[]{:S(2)}, u32[]{:S(2)}) collective-permute-start(bf16[256,1024]{1,0:T(8,128)(2,1)S(1)} %copy-done.18), channel_id=1, source_target_pairs={{0,128},{64,192},{128,0},{192,64},{1,129},{65,193},{129,1},{193,65... | collective-permute-start | bytes 1572872 | tf_op jit(solution)/shard_map/ppermute | solution.py:269
  106.7 0.8 collective-permute-start.9
  107.5 12.3 %collective-permute-done.7.g1 = bf16[256,1024]{1,0:T(8,128)(2,1)S(1)} collective-permute-done((bf16[256,1024]{1,0:T(8,128)(2,1)S(1)}, bf16[256,1024]{1,0:T(8,128)(2,1)S(1)}, u32[]{:S(2)}, u32[]{:S(2)}) %collective-permute-start.7) | collective-permute-done | bytes 524320 | tf_op jit(solution)/shard_map/ppermute | solution.py:269
  119.8 9.8 %collective-permute-done.8.g2 = bf16[256,1024]{1,0:T(8,128)(2,1)S(1)} collective-permute-done((bf16[256,1024]{1,0:T(8,128)(2,1)S(1)}, bf16[256,1024]{1,0:T(8,128)(2,1)S(1)}, u32[]{:S(2)}, u32[]{:S(2)}) %collective-permute-start.8) | collective-permute-done | bytes 524320 | tf_op jit(solution)/shard_map/ppermute | solution.py:269
  129.5 1.0 collective-permute-done.9.g3
  130.6 1.0 shard_map.107
  131.5 17.1 %all_to_all.44 = bf16[16,8,1024]{2,1,0:T(8,128)(2,1)S(1)} all-to-all(bf16[16,8,1024]{2,1,0:T(8,128)(2,1)S(1)} %bitcast.31), channel_id=1, replica_groups=mesh['dp'=4,'ctx'=16,'tp'=4] {'ctx'}, dimensions={0} | all-to-all | bytes 524288 | tf_op jit(solution)/shard_map/all_to_all | solution.py:317
  148.6 0.1 shard_map.108
  148.7 15.4 %all_to_all.45 = bf16[16,8,1024]{2,1,0:T(8,128)(2,1)S(1)} all-to-all(bf16[16,8,1024]{2,1,0:T(8,128)(2,1)S(1)} %bitcast.24), channel_id=1, replica_groups=mesh['dp'=4,'ctx'=16,'tp'=4] {'ctx'}, dimensions={0} | all-to-all | bytes 524288 | tf_op jit(solution)/shard_map/all_to_all | solution.py:319
  164.1 0.0 copy-done.7
  164.1 3.1 %shard_map.109 = (bf16[256,1024]{1,0:T(8,128)(2,1)}, bf16[256,128]{1,0:T(8,128)(2,1)}, bf16[256,128]{1,0:T(8,128)(2,1)}) custom-call(bf16[256,1024]{1,0:T(8,128)(2,1)S(1)} %bitcast.18, bf16[256,128]{1,0:T(8,128)(2,1)S(1)} %bitcast.27, bf16[256,128]{1,0:T(8,128)(2,1)S(1)} %bitcast.30, bf16[256,1024]{1,0:T(8,128)(2,1)S(1)} %get-tuple-element.36.g_ref, ...), custom_call_target="tpu_custom_call" | custom-call | tf_op jit(solution)/shard_map/pallas_call | solution.py:320
  (21 shorter events, 0.0 us)
Async XLA Ops:
  7.2 63.0 %all-gather.2.cloned.1.call-start = ((), (), s32[]{:S(2)}) async-start(), calls=%async_computation.5 | async-start | bytes 2228224 | tf_op jit(solution)/shard_map/all_gather | solution.py:274
  7.2 0.9 copy-start.10
  8.1 0.7 copy-start.14
  9.5 16.3 %collective-permute-start = (bf16[256,1024]{1,0:T(8,128)(2,1)}, bf16[256,1024]{1,0:T(8,128)(2,1)S(1)}, u32[]{:S(2)}, u32[]{:S(2)}) collective-permute-start(bf16[256,1024]{1,0:T(8,128)(2,1)} %bitcast.33), channel_id=1, source_target_pairs={{0,0},{1,64},{2,128},{3,192},{64,1},{65,65},{66,129},{67,193},{128... | collective-permute-start | bytes 1572872 | tf_op jit(solution)/shard_map/ppermute | solution.py:263
  11.2 1.0 copy-start
  12.3 0.8 copy-start.5
  13.1 0.7 copy-start.13
  15.8 26.4 %all-to-all-start = ((bf16[16,8,1152]{2,1,0:T(8,128)(2,1)}), bf16[16,8,1152]{2,1,0:T(8,128)(2,1)S(1)}, u32[]{:S(2)}, u32[]{:S(2)}) async-start(bf16[16,8,1152]{2,1,0:T(8,128)(2,1)} %bitcast.5), calls=%async_computation | async-start | bytes 589824 | tf_op jit(solution)/shard_map/all_to_all | solution.py:281
  25.8 45.0 %collective-permute-start.3 = (bf16[256,1024]{1,0:T(8,128)(2,1)S(1)}, bf16[256,1024]{1,0:T(8,128)(2,1)S(1)}, u32[]{:S(2)}, u32[]{:S(2)}) collective-permute-start(bf16[256,1024]{1,0:T(8,128)(2,1)S(1)} %collective-permute-done.c0), channel_id=1, source_target_pairs={{0,3},{1,0},{2,1},{3,2},{4,7},{5,4},{6,5},{7,6},{8,11},{9,8},{10,9... | collective-permute-start | bytes 1572872 | tf_op jit(solution)/shard_map/ppermute | solution.py:266
  43.3 0.6 copy-start.11
  44.0 22.0 %all-to-all-start.1 = ((bf16[16,8,1024]{2,1,0:T(8,128)(2,1)}), bf16[16,8,1024]{2,1,0:T(8,128)(2,1)S(1)}, u32[]{:S(2)}, u32[]{:S(2)}) async-start(bf16[16,8,1024]{2,1,0:T(8,128)(2,1)} %bitcast.7), calls=%async_computation.1 | async-start | bytes 524288 | tf_op jit(solution)/shard_map/all_to_all | solution.py:285
  54.3 112.9 %reduce-scatter.2.cloned.1.call-start = ((), (), s32[]{:S(2)}) async-start(), calls=%async_computation.6 | async-start | bytes 4456448 | tf_op jit(solution)/shard_map/reduce_scatter | solution.py:313
  54.3 17.5 %collective-permute-start.2 = (bf16[256,1024]{1,0:T(8,128)(2,1)S(1)}, bf16[256,1024]{1,0:T(8,128)(2,1)S(1)}, u32[]{:S(2)}, u32[]{:S(2)}) collective-permute-start(bf16[256,1024]{1,0:T(8,128)(2,1)S(1)} %collective-permute-done.c0), channel_id=1, source_target_pairs={{0,2},{1,3},{2,0},{3,1},{4,6},{5,7},{6,4},{7,5},{8,10},{9,11},{10,... | collective-permute-start | bytes 1572872 | tf_op jit(solution)/shard_map/ppermute | solution.py:266
  54.4 26.2 %collective-permute-start.1 = (bf16[256,1024]{1,0:T(8,128)(2,1)S(1)}, bf16[256,1024]{1,0:T(8,128)(2,1)S(1)}, u32[]{:S(2)}, u32[]{:S(2)}) collective-permute-start(bf16[256,1024]{1,0:T(8,128)(2,1)S(1)} %collective-permute-done.c0), channel_id=1, source_target_pairs={{0,1},{1,2},{2,3},{3,0},{4,5},{5,6},{6,7},{7,4},{8,9},{9,10},{10,1... | collective-permute-start | bytes 1572872 | tf_op jit(solution)/shard_map/ppermute | solution.py:266
  66.0 1.0 copy-start.1
  67.0 0.8 copy-start.6
  67.9 0.8 copy-start.8
  70.2 18.0 %collective-permute-start.6 = (bf16[256,1024]{1,0:T(8,128)(2,1)S(1)}, bf16[256,1024]{1,0:T(8,128)(2,1)S(1)}, u32[]{:S(2)}, u32[]{:S(2)}) collective-permute-start(bf16[256,1024]{1,0:T(8,128)(2,1)S(1)} %shard_map.104.m0), channel_id=1, source_target_pairs={{0,192},{64,0},{128,64},{192,128},{1,193},{65,1},{129,65},{193,129... | collective-permute-start | bytes 1572872 | tf_op jit(solution)/shard_map/ppermute | solution.py:269
  70.3 17.9 %collective-permute-start.5 = (bf16[256,1024]{1,0:T(8,128)(2,1)S(1)}, bf16[256,1024]{1,0:T(8,128)(2,1)S(1)}, u32[]{:S(2)}, u32[]{:S(2)}) collective-permute-start(bf16[256,1024]{1,0:T(8,128)(2,1)S(1)} %shard_map.104.m0), channel_id=1, source_target_pairs={{0,128},{64,192},{128,0},{192,64},{1,129},{65,193},{129,1},{193,65... | collective-permute-start | bytes 1572872 | tf_op jit(solution)/shard_map/ppermute | solution.py:269
  70.8 9.8 %copy-start.3 = (bf16[256,1024]{1,0:T(8,128)(2,1)}, bf16[256,1024]{1,0:T(8,128)(2,1)S(1)}, u32[]{:S(2)}) copy-start(bf16[256,1024]{1,0:T(8,128)(2,1)S(1)} %collective-permute-done.3.c3) | copy-start | bytes 1572868
  70.8 26.2 %collective-permute-start.4 = (bf16[256,1024]{1,0:T(8,128)(2,1)S(1)}, bf16[256,1024]{1,0:T(8,128)(2,1)S(1)}, u32[]{:S(2)}, u32[]{:S(2)}) collective-permute-start(bf16[256,1024]{1,0:T(8,128)(2,1)S(1)} %shard_map.104.m0), channel_id=1, source_target_pairs={{0,64},{64,128},{128,192},{192,0},{1,65},{65,129},{129,193},{193,1... | collective-permute-start | bytes 1572872 | tf_op jit(solution)/shard_map/ppermute | solution.py:269
  85.7 0.8 copy-start.15
  86.5 0.8 copy-start.17
  87.4 0.8 copy-start.19
  88.2 8.8 %copy-start.21 = (bf16[256,1024]{1,0:T(8,128)(2,1)}, bf16[256,1024]{1,0:T(8,128)(2,1)S(1)}, u32[]{:S(2)}) copy-start(bf16[256,1024]{1,0:T(8,128)(2,1)S(1)} %collective-permute-done.6.m3) | copy-start | bytes 1572868
  97.0 1.0 copy-start.4
  103.6 1.0 copy-start.20
  103.7 1.2 copy-start.18
  103.7 3.0 %copy-start.16 = (bf16[256,1024]{1,0:T(8,128)(2,1)S(1)}, bf16[256,1024]{1,0:T(8,128)(2,1)}, u32[]{:S(2)}) copy-start(bf16[256,1024]{1,0:T(8,128)(2,1)} %copy-done.15) | copy-start | bytes 1572868
  103.7 26.9 %copy-start.9 = (bf16[1,256,128]{2,1,0:T(8,128)(2,1)S(1)}, bf16[1,256,128]{2,1,0:T(8,128)(2,1)}, u32[]{:S(2)}) copy-start(bf16[1,256,128]{2,1,0:T(8,128)(2,1)} %param.9) | copy-start | bytes 196612
  103.7 44.9 %copy-start.12 = (f32[16,1024]{1,0:T(8,128)S(1)}, f32[16,1024]{1,0:T(8,128)}, u32[]{:S(2)}) copy-start(f32[16,1024]{1,0:T(8,128)} %copy-done.11) | copy-start | bytes 196612
  103.7 60.4 %copy-start.2 = (bf16[1,256,1024]{2,1,0:T(8,128)(2,1)S(1)}, bf16[1,256,1024]{2,1,0:T(8,128)(2,1)}, u32[]{:S(2)}) copy-start(bf16[1,256,1024]{2,1,0:T(8,128)(2,1)} %param.7) | copy-start | bytes 1572868
  103.7 60.4 %copy-start.7 = (bf16[1,256,128]{2,1,0:T(8,128)(2,1)S(1)}, bf16[1,256,128]{2,1,0:T(8,128)(2,1)}, u32[]{:S(2)}) copy-start(bf16[1,256,128]{2,1,0:T(8,128)(2,1)} %param.8) | copy-start | bytes 196612
  104.7 15.1 %collective-permute-start.7 = (bf16[256,1024]{1,0:T(8,128)(2,1)S(1)}, bf16[256,1024]{1,0:T(8,128)(2,1)S(1)}, u32[]{:S(2)}, u32[]{:S(2)}) collective-permute-start(bf16[256,1024]{1,0:T(8,128)(2,1)S(1)} %copy-done.20), channel_id=1, source_target_pairs={{0,64},{64,128},{128,192},{192,0},{1,65},{65,129},{129,193},{193,1... | collective-permute-start | bytes 1572872 | tf_op jit(solution)/shard_map/ppermute | solution.py:269
  104.8 24.7 %collective-permute-start.8 = (bf16[256,1024]{1,0:T(8,128)(2,1)S(1)}, bf16[256,1024]{1,0:T(8,128)(2,1)S(1)}, u32[]{:S(2)}, u32[]{:S(2)}) collective-permute-start(bf16[256,1024]{1,0:T(8,128)(2,1)S(1)} %copy-done.18), channel_id=1, source_target_pairs={{0,128},{64,192},{128,0},{192,64},{1,129},{65,193},{129,1},{193,65... | collective-permute-start | bytes 1572872 | tf_op jit(solution)/shard_map/ppermute | solution.py:269
  106.7 23.9 %collective-permute-start.9 = (bf16[256,1024]{1,0:T(8,128)(2,1)S(1)}, bf16[256,1024]{1,0:T(8,128)(2,1)S(1)}, u32[]{:S(2)}, u32[]{:S(2)}) collective-permute-start(bf16[256,1024]{1,0:T(8,128)(2,1)S(1)} %copy-done.16), channel_id=1, source_target_pairs={{0,192},{64,0},{128,64},{192,128},{1,193},{65,1},{129,65},{193,129... | collective-permute-start | bytes 1572872 | tf_op jit(solution)/shard_map/ppermute | solution.py:269
Sparse Core Ops, SparseCore 0:
  9.8 45.4 all-gather.1
  103.9 61.6 reduce-scatter.1

commit v3 on v2

--- a/solution.py
+++ b/solution.py
@@ -155,7 +155,7 @@
         out_ref[:, lanes] = (jnp.where(half, parts[0], parts[1]) + carried).astype(bf16)
 
 
-def project_kernel(c0, c1, c2, c3, weight_ref, o0, o1, o2, o3, held, sems):
+def project_kernel(c0, c1, c2, c3, weight_ref, o0, o1, o2, o3, o4, held, sems):
     copies = []
     for m, ref in enumerate((c0, c1, c2, c3)):
         slot = lax.rem(lax.axis_index("tp") - lax.axis_index("dp") + 8 - m, 4)
@@ -165,20 +165,30 @@
     for copy in copies:
         copy.wait()
     weight = weight_ref[...]
-    for n, out in enumerate((o0, o1, o2, o3)):
+    half = o3.shape[0]
+    opposite = dot(held[2], weight, (1, 0)).astype(bf16)
+    o3[...] = opposite[:half]
+    o4[...] = opposite[half:]
+    for n, out in ((1, o1), (3, o2), (0, o0)):
         out[...] = dot(held[n], weight, (1, 0)).astype(bf16)
 
 
-def adjoint_kernel(g0, g1, g2, g3, r_ref, columns_ref, grad_ref, summary_ref):
+def fold_kernel(p1, p2, top, bottom, o1, o2):
+    half = top.shape[0]
+    o1[:half, :] = (p1[:half, :].astype(f32) + top[...].astype(f32)).astype(bf16)
+    o1[half:, :] = p1[half:, :]
+    o2[:half, :] = p2[:half, :]
+    o2[half:, :] = (p2[half:, :].astype(f32) + bottom[...].astype(f32)).astype(bf16)
+
+
+def adjoint_kernel(g0, g1, g2, r_ref, columns_ref, grad_ref, summary_ref):
     length, columns = g0.shape
     heads = columns // HEAD_DIM
     since = jnp.exp(columns_ref[...])
     r = r_ref[...]
     for pair in range(heads // 2):
         lanes = slice(pair * LANES, (pair + 1) * LANES)
-        total = (g0[:, lanes].astype(f32) + g1[:, lanes].astype(f32)) + (
-            g2[:, lanes].astype(f32) + g3[:, lanes].astype(f32)
-        )
+        total = g0[:, lanes].astype(f32) + g1[:, lanes].astype(f32) + g2[:, lanes].astype(f32)
         grad = total.astype(bf16)
         grad_ref[:, lanes] = grad
         scaled = grad.astype(f32) * pair_scale(since, pair, length)
@@ -229,7 +239,7 @@
 
 
 def weight_kernel(
-    c0, c1, c2, c3, m0, m1, m2, m3, out_ref, held, sems
+    c0, c1, c2, c3, m0, m1, m2, m3, mine_ref, other_ref, held, total, sems
 ):
     copies = []
     for m, ref in enumerate((c0, c1, c2, c3)):
@@ -243,7 +253,18 @@
     acc = dot(held[0], mixers[0][...], (0, 0))
     for n in range(1, 4):
         acc = acc + dot(held[n], mixers[n][...], (0, 0))
-    out_ref[...] = acc
+    total[...] = acc
+    ring, rows = mine_ref.shape[0], mine_ref.shape[1]
+    core = lax.rem(lax.axis_index("ctx"), 2)
+    for n in range(ring):
+        start = pl.multiple_of((2 * n + core) * rows, rows)
+        mine_ref[n] = total[pl.ds(start, rows), :].astype(bf16)
+        start = pl.multiple_of((2 * n + 1 - core) * rows, rows)
+        other_ref[n] = total[pl.ds(start, rows), :].astype(bf16)
+
+
+def add_kernel(mine_ref, other_ref, out_ref):
+    out_ref[...] = mine_ref[...].astype(f32) + other_ref[...].astype(f32)
 
 
 def shape(dims, dtype=bf16):
@@ -295,23 +316,41 @@
     model = cotangent.shape[2]
     parts = call(
         project_kernel,
-        [shape((length, columns))] * dp,
+        [shape((length, columns))] * 3 + [shape((length // 2, columns))] * 2,
         5,
         scratch=[pltpu.VMEM((dp, length, model), bf16), pltpu.SemaphoreType.DMA((dp,))],
         in_specs=[anywhere] * dp + [vmem],
     )(*cots, weight)
-    arrived = [along_dp(parts[n], n) for n in range(1, dp)]
+    top, bottom = along_dp(parts[3], 1), along_dp(parts[4], -1)
+    folded = call(fold_kernel, [shape((length, columns))] * 2, 4, flops=40_000_000_000)(
+        parts[1], parts[2], top, bottom
+    )
+    arrived = [along_dp(folded[0], 1), along_dp(folded[1], -1)]
 
     parts, mixers = lax.optimization_barrier((parts, mixers))
-    total = call(
+    rows = model // ctx
+    mine, other = call(
         weight_kernel,
-        shape((model, columns), f32),
+        [shape((ctx // 2, rows, columns))] * 2,
         8,
-        scratch=[pltpu.VMEM((dp, length, model), bf16), pltpu.SemaphoreType.DMA((dp,))],
+        flops=20_000_000_000,
+        scratch=[
+            pltpu.VMEM((dp, length, model), bf16),
+            pltpu.VMEM((model, columns), f32),
+            pltpu.SemaphoreType.DMA((dp,)),
+        ],
         in_specs=[anywhere] * dp + [vmem] * dp,
     )(*cots, *mixers)
-    grad_weight = lax.psum_scatter(total, "ctx", scatter_dimension=0, tiled=True)
-    grad, summary = call(adjoint_kernel, [shape((length, columns)), shape((STATE, columns))], 6)(
+    other = lax.ppermute(other, "ctx", [(i, i ^ 1) for i in range(ctx)])
+    total = call(add_kernel, shape((ctx // 2, rows, columns), f32), 2)(mine, other)
+    chips = [[2 * k + core for k in range(ctx // 2)] for core in range(2)]
+    grad_weight = lax.psum_scatter(total, "ctx", axis_index_groups=chips)
+    grad, summary = call(
+        adjoint_kernel,
+        [shape((length, columns)), shape((STATE, columns))],
+        5,
+        flops=50_000_000_000,
+    )(
         parts[0], *arrived, r, cum_columns
     )
     summary = lax.all_to_all(summary, "ctx", 0, 0, tiled=True)

time: 175 us -> 162 us (0.926)
  waiting for transfers between devices: 52.1 us -> 35.6 us
  local copies, waits for them, and re-layouts: 12.1 us -> 5.01 us
  starting transfers between devices: 43.1 us -> 48.3 us
  Pallas kernels: 20 us -> 24.4 us
    ppermute x6 -> x7, waiting for transfers between devices: 31.9 us -> 16 us  [along_dp(): return lax.ppermute(value, 'dp', [(i, (i + n) % dp) for i in range(dp)])]
    ppermute x6 -> x7, starting transfers between devices: 4.22 us -> 12.9 us  [along_dp(): return lax.ppermute(value, 'dp', [(i, (i + n) % dp) for i in range(dp)])]
    unnamed x44 -> x24, local copies, waits for them, and re-layouts: 12.1 us -> 5.01 us
    all_to_all x1, waiting for transfers between devices: 11.3 us -> 4.83 us  [per_device(): entering = lax.all_to_all(entering, 'ctx', 0, 0, tiled=True)]
    all_to_all x1, waiting for transfers between devices: 0.01 us -> 5.25 us  [per_device(): packed = lax.all_to_all(packed, 'ctx', 0, 0, tiled=True)]
    pallas_call x3 -> x5, Pallas kernels: 11.7 us -> 16 us  [the longest x1 6.49 us: per_device(): call(weight_kernel, [shape((ctx // 2, rows, columns))] * 2, 8, flops=2000...]
    all_to_all x1, starting transfers between devices: 10.3 us -> 6.78 us  [per_device(): entering = lax.all_to_all(entering, 'ctx', 0, 0, tiled=True)]
  transfers between devices with their start and end apart: 14 -> 16, of which waited for: 6 -> 5; matrix products, arithmetic and copies ran while one was open for 0% -> 0% of each run, Pallas kernels for 8% -> 15%
where the time goes in v3:
time: 162 us; the launch traced here: 161 us
  starting transfers between devices  48.3 us (30%)
  waiting for transfers between devices  35.6 us (22%)
  blocking collectives  33.8 us (21%)
  Pallas kernels  24.4 us (15%)
  between operations  14.2 us (9%)
  local copies, waits for them, and re-layouts  5.01 us (3%)
    all_to_all x1, blocking collectives, per_device(): summary = lax.all_to_all(summary, 'ctx', 0, 0, tiled=True)  17.8 us
    ppermute x7, waiting for transfers between devices, along_dp(): return lax.ppermute(value, 'dp', [(i, (i + n) % dp) for i in range(dp)])  16 us
    ppermute x3, starting transfers between devices, along_tp(): return lax.ppermute(value, 'tp', [(i, (i + n) % tp) for i in range(tp)])  16 us
    all_to_all x1, blocking collectives, per_device(): leaving = lax.all_to_all(leaving, 'ctx', 0, 0, tiled=True)  15.9 us
    ppermute x7, starting transfers between devices, along_dp(): return lax.ppermute(value, 'dp', [(i, (i + n) % dp) for i in range(dp)])  12.9 us
    all_to_all x1, starting transfers between devices, per_device(): packed = lax.all_to_all(packed, 'ctx', 0, 0, tiled=True)  9.98 us
    ppermute x3, waiting for transfers between devices, along_tp(): return lax.ppermute(value, 'tp', [(i, (i + n) % tp) for i in range(tp)])  9.46 us
    all_to_all x1, starting transfers between devices, per_device(): entering = lax.all_to_all(entering, 'ctx', 0, 0, tiled=True)  6.78 us
  transfers between devices with their start and end apart: 16, of which 5 were waited for; matrix products, arithmetic and copies ran while one was open for 0% of the time, Pallas kernels for 15%

profile of v3, /device:TPU:1, one launch (start us, length us, event | category | flops | bytes accessed | tf_op | source)
XLA Modules:
  0.0 161.3 jit_solution(3361531507727874663)
XLA Ops:
  7.2 0.0 copy-start.4
  7.2 0.0 copy-start.5
  7.2 0.0 all-gather.2.cloned.1.call-start
  7.2 0.0 copy-start.6
  7.2 0.9 copy-done.6
  8.1 0.0 copy-start.8
  8.1 0.7 copy-done.8
  8.8 0.7 shard_map.105
  9.5 0.0 all-gather.2.cloned.1.call-update
  9.5 1.7 %collective-permute-start = (bf16[256,1024]{1,0:T(8,128)(2,1)}, bf16[256,1024]{1,0:T(8,128)(2,1)S(1)}, u32[]{:S(2)}, u32[]{:S(2)}) collective-permute-start(bf16[256,1024]{1,0:T(8,128)(2,1)} %bitcast.34), channel_id=1, source_target_pairs={{0,0},{1,64},{2,128},{3,192},{64,1},{65,65},{66,129},{67,193},{128... | collective-permute-start | bytes 1572872 | tf_op jit(solution)/shard_map/ppermute | solution.py:284
  11.2 1.0 copy-done
  12.3 0.8 copy-done.3
  13.1 0.7 copy-done.7
  13.8 2.0 %shard_map.102 = (bf16[128,1152]{1,0:T(8,128)(2,1)}, f32[16,256]{1,0:T(8,128)S(1)}, f32[256,128]{1,0:T(8,128)S(1)}) custom-call(bf16[256,1024]{1,0:T(8,128)(2,1)S(1)} %bitcast.17, bf16[256,128]{1,0:T(8,128)(2,1)S(1)} %bitcast.26, f32[16,256]{1,0:T(8,128)S(1)} %bitcast.33), custom_call_target="tpu_custom_call" | custom-call | tf_op jit(solution)/shard_map/pallas_call | solution.py:297
  15.9 10.0 %all-to-all-start = ((bf16[16,8,1152]{2,1,0:T(8,128)(2,1)}), bf16[16,8,1152]{2,1,0:T(8,128)(2,1)S(1)}, u32[]{:S(2)}, u32[]{:S(2)}) async-start(bf16[16,8,1152]{2,1,0:T(8,128)(2,1)} %bitcast.5), calls=%async_computation | async-start | bytes 589824 | tf_op jit(solution)/shard_map/all_to_all | solution.py:302
  25.8 0.0 collective-permute-done.c0
  25.9 9.3 %collective-permute-start.1 = (bf16[256,1024]{1,0:T(8,128)(2,1)S(1)}, bf16[256,1024]{1,0:T(8,128)(2,1)S(1)}, u32[]{:S(2)}, u32[]{:S(2)}) collective-permute-start(bf16[256,1024]{1,0:T(8,128)(2,1)S(1)} %collective-permute-done.c0), channel_id=1, source_target_pairs={{0,1},{1,2},{2,3},{3,0},{4,5},{5,6},{6,7},{7,4},{8,9},{9,10},{10,1... | collective-permute-start | bytes 1572872 | tf_op jit(solution)/shard_map/ppermute | solution.py:287
  35.2 5.2 %all-to-all-done = bf16[16,8,1152]{2,1,0:T(8,128)(2,1)S(1)} async-done(((bf16[16,8,1152]{2,1,0:T(8,128)(2,1)}), bf16[16,8,1152]{2,1,0:T(8,128)(2,1)S(1)}, u32[]{:S(2)}, u32[]{:S(2)}) %all-to-all-start) | async-done | bytes 294944 | tf_op jit(solution)/shard_map/all_to_all | solution.py:302
  40.4 1.0 shard_map.103
  41.5 6.8 %all-to-all-start.1 = ((bf16[16,8,1024]{2,1,0:T(8,128)(2,1)}), bf16[16,8,1024]{2,1,0:T(8,128)(2,1)S(1)}, u32[]{:S(2)}, u32[]{:S(2)}) async-start(bf16[16,8,1024]{2,1,0:T(8,128)(2,1)} %bitcast.7), calls=%async_computation.1 | async-start | bytes 524288 | tf_op jit(solution)/shard_map/all_to_all | solution.py:306
  48.2 0.0 reduce-scatter.2.cloned.1.call-start
  48.3 6.7 %collective-permute-start.2 = (bf16[256,1024]{1,0:T(8,128)(2,1)S(1)}, bf16[256,1024]{1,0:T(8,128)(2,1)S(1)}, u32[]{:S(2)}, u32[]{:S(2)}) collective-permute-start(bf16[256,1024]{1,0:T(8,128)(2,1)S(1)} %collective-permute-done.c0), channel_id=1, source_target_pairs={{0,2},{1,3},{2,0},{3,1},{4,6},{5,7},{6,4},{7,5},{8,10},{9,11},{10,... | collective-permute-start | bytes 1572872 | tf_op jit(solution)/shard_map/ppermute | solution.py:287
  55.0 0.0 collective-permute-start.3
  55.0 4.8 %all-to-all-done.1 = bf16[16,8,1024]{2,1,0:T(8,128)(2,1)S(1)} async-done(((bf16[16,8,1024]{2,1,0:T(8,128)(2,1)}), bf16[16,8,1024]{2,1,0:T(8,128)(2,1)S(1)}, u32[]{:S(2)}, u32[]{:S(2)}) %all-to-all-start.1) | async-done | bytes 262176 | tf_op jit(solution)/shard_map/all_to_all | solution.py:306
  59.8 0.0 copy-done.4
  59.8 0.0 copy-done.5
  59.8 0.0 copy-done.1
  59.8 1.4 shard_map.104.m0
  61.3 0.0 all-gather.2.cloned.1.call-done.weight_ref
  61.3 2.0 %collective-permute-start.4 = (bf16[256,1024]{1,0:T(8,128)(2,1)S(1)}, bf16[256,1024]{1,0:T(8,128)(2,1)S(1)}, u32[]{:S(2)}, u32[]{:S(2)}) collective-permute-start(bf16[256,1024]{1,0:T(8,128)(2,1)S(1)} %shard_map.104.m0), channel_id=1, source_target_pairs={{0,64},{64,128},{128,192},{192,0},{1,65},{65,129},{129,193},{193,1... | collective-permute-start | bytes 1572872 | tf_op jit(solution)/shard_map/ppermute | solution.py:290
  63.3 4.7 %collective-permute-start.5 = (bf16[256,1024]{1,0:T(8,128)(2,1)S(1)}, bf16[256,1024]{1,0:T(8,128)(2,1)S(1)}, u32[]{:S(2)}, u32[]{:S(2)}) collective-permute-start(bf16[256,1024]{1,0:T(8,128)(2,1)S(1)} %shard_map.104.m0), channel_id=1, source_target_pairs={{0,128},{64,192},{128,0},{192,64},{1,129},{65,193},{129,1},{193,65... | collective-permute-start | bytes 1572872 | tf_op jit(solution)/shard_map/ppermute | solution.py:290
  68.0 0.0 collective-permute-done.1.c1
  68.0 0.0 collective-permute-start.6
  68.0 0.0 collective-permute-done.2.c2
  68.0 9.5 %collective-permute-done.3.c3 = bf16[256,1024]{1,0:T(8,128)(2,1)} collective-permute-done((bf16[256,1024]{1,0:T(8,128)(2,1)S(1)}, bf16[256,1024]{1,0:T(8,128)(2,1)}, u32[]{:S(2)}, u32[]{:S(2)}) %collective-permute-start.3) | collective-permute-done | bytes 524320 | tf_op jit(solution)/shard_map/ppermute | solution.py:287
  77.5 5.1 %shard_map.106 = (bf16[256,1024]{1,0:T(8,128)(2,1)S(1)}, bf16[256,1024]{1,0:T(8,128)(2,1)S(1)}, bf16[256,1024]{1,0:T(8,128)(2,1)S(1)}, bf16[128,1024]{1,0:T(8,128)(2,1)S(1)}, bf16[128,1024]{1,0:T(8,128)(2,1)S(1)}) custom-call(bf16[256,1024]{1,0:T(8,128)(2,1)S(1)} %collective-permute-done.c0, bf16[256,1024]{1,0:T(8,128)(2,1)S(1)} %collective-permute-done.1.c1, ...), custom_call_target="tpu_custom_call" | custom-call | tf_op jit(solution)/shard_map/pallas_call | solution.py:317
  82.6 0.0 copy-start.9
  82.6 0.1 collective-permute-start.7
  82.7 3.5 %collective-permute-start.8 = (bf16[128,1024]{1,0:T(8,128)(2,1)S(1)}, bf16[128,1024]{1,0:T(8,128)(2,1)S(1)}, u32[]{:S(2)}, u32[]{:S(2)}) collective-permute-start(bf16[128,1024]{1,0:T(8,128)(2,1)S(1)} %get-tuple-element.39), channel_id=1, source_target_pairs={{0,192},{64,0},{128,64},{192,128},{1,193},{65,1},{129,65},{193,129... | collective-permute-start | bytes 786440 | tf_op jit(solution)/shard_map/ppermute | solution.py:290
  86.2 0.0 collective-permute-done.4.m1
  86.2 5.4 %collective-permute-done.5.m2 = bf16[256,1024]{1,0:T(8,128)(2,1)S(1)} collective-permute-done((bf16[256,1024]{1,0:T(8,128)(2,1)S(1)}, bf16[256,1024]{1,0:T(8,128)(2,1)S(1)}, u32[]{:S(2)}, u32[]{:S(2)}) %collective-permute-start.5) | collective-permute-done | bytes 524320 | tf_op jit(solution)/shard_map/ppermute | solution.py:290
  91.6 0.0 collective-permute-done.6.m3
  91.6 0.8 copy-done.11
  92.4 6.5 %shard_map.111 = (bf16[8,64,1024]{2,1,0:T(8,128)(2,1)}, bf16[8,64,1024]{2,1,0:T(8,128)(2,1)}) custom-call(bf16[256,1024]{1,0:T(8,128)(2,1)S(1)} %collective-permute-done.c0, bf16[256,1024]{1,0:T(8,128)(2,1)S(1)} %collective-permute-done.1.c1, bf16[256,1024]{1,0:T(8,128)(2,1)S(1)} %collective-permute-done.2.c2, bf16[256,1024]{1,0:T(8,128)(2,1)} %collective-permute-done.3.c3, ...), custom_call_target="tpu_custom_call" | custom-call | flops 20000000000 | tf_op jit(solution)/shard_map/pallas_call | solution.py:332
  98.9 0.0 copy-done.9
  98.9 0.0 copy-start.2
  98.9 0.8 collective-permute-start.11
  99.7 0.0 collective-permute-done.7.top
  99.7 0.0 collective-permute-done.8.bottom
  99.7 0.9 shard_map.107
  100.6 0.0 collective-permute-start.9
  100.6 2.7 %collective-permute-start.10 = (bf16[256,1024]{1,0:T(8,128)(2,1)S(1)}, bf16[256,1024]{1,0:T(8,128)(2,1)}, u32[]{:S(2)}, u32[]{:S(2)}) collective-permute-start(bf16[256,1024]{1,0:T(8,128)(2,1)S(1)} %get-tuple-element.43), channel_id=1, source_target_pairs={{0,192},{64,0},{128,64},{192,128},{1,193},{65,1},{129,65},{193,129... | collective-permute-start | bytes 1572872 | tf_op jit(solution)/shard_map/ppermute | solution.py:290
  103.3 0.0 collective-permute-done.11.other_ref
  103.3 0.0 copy-done.2
  103.3 1.6 shard_map.112
  104.9 0.0 reduce-scatter.2.cloned.1.call-update
  104.9 10.7 %collective-permute-done.9.g1 = bf16[256,1024]{1,0:T(8,128)(2,1)S(1)} collective-permute-done((bf16[256,1024]{1,0:T(8,128)(2,1)}, bf16[256,1024]{1,0:T(8,128)(2,1)S(1)}, u32[]{:S(2)}, u32[]{:S(2)}) %collective-permute-start.9) | collective-permute-done | bytes 524320 | tf_op jit(solution)/shard_map/ppermute | solution.py:290
  115.6 0.0 collective-permute-done.10.g2
  115.6 0.0 copy-done.10
  115.6 2.0 %shard_map.108 = (bf16[256,1024]{1,0:T(8,128)(2,1)S(1)}, bf16[128,1024]{1,0:T(8,128)(2,1)S(1)}) custom-call(bf16[256,1024]{1,0:T(8,128)(2,1)S(1)} %copy-done.10, bf16[256,1024]{1,0:T(8,128)(2,1)S(1)} %collective-permute-done.9.g1, bf16[256,1024]{1,0:T(8,128)(2,1)} %collective-permute-done.10.g2, bf16[256,128]{1,0:T(8,128)(2,1)S(1)} %bitcast.30, ...), custom_call_target="tpu_custom_call" | custom-call | flops 49999998976 | tf_op jit(solution)/shard_map/pallas_call | solution.py:348
  117.5 17.8 %all_to_all.44 = bf16[16,8,1024]{2,1,0:T(8,128)(2,1)S(1)} all-to-all(bf16[16,8,1024]{2,1,0:T(8,128)(2,1)S(1)} %bitcast.32), channel_id=1, replica_groups=mesh['dp'=4,'ctx'=16,'tp'=4] {'ctx'}, dimensions={0} | all-to-all | bytes 524288 | tf_op jit(solution)/shard_map/all_to_all | solution.py:356
  135.4 0.1 shard_map.109
  135.4 15.9 %all_to_all.45 = bf16[16,8,1024]{2,1,0:T(8,128)(2,1)S(1)} all-to-all(bf16[16,8,1024]{2,1,0:T(8,128)(2,1)S(1)} %bitcast.25), channel_id=1, replica_groups=mesh['dp'=4,'ctx'=16,'tp'=4] {'ctx'}, dimensions={0} | all-to-all | bytes 524288 | tf_op jit(solution)/shard_map/all_to_all | solution.py:358
  151.4 3.1 %shard_map.110 = (bf16[256,1024]{1,0:T(8,128)(2,1)}, bf16[256,128]{1,0:T(8,128)(2,1)}, bf16[256,128]{1,0:T(8,128)(2,1)}) custom-call(bf16[256,1024]{1,0:T(8,128)(2,1)S(1)} %bitcast.19, bf16[256,128]{1,0:T(8,128)(2,1)S(1)} %bitcast.28, bf16[256,128]{1,0:T(8,128)(2,1)S(1)} %bitcast.31, bf16[256,1024]{1,0:T(8,128)(2,1)S(1)} %get-tuple-element.44.g_ref, ...), custom_call_target="tpu_custom_call" | custom-call | tf_op jit(solution)/shard_map/pallas_call | solution.py:359
  (7 shorter events, 0.0 us)
Async XLA Ops:
  7.2 52.7 %copy-start.4 = (bf16[1,256,128]{2,1,0:T(8,128)(2,1)S(1)}, bf16[1,256,128]{2,1,0:T(8,128)(2,1)}, u32[]{:S(2)}) copy-start(bf16[1,256,128]{2,1,0:T(8,128)(2,1)} %param.8) | copy-start | bytes 196612
  7.2 52.7 %copy-start.5 = (bf16[1,256,128]{2,1,0:T(8,128)(2,1)S(1)}, bf16[1,256,128]{2,1,0:T(8,128)(2,1)}, u32[]{:S(2)}) copy-start(bf16[1,256,128]{2,1,0:T(8,128)(2,1)} %param.9) | copy-start | bytes 196612
  7.2 54.1 %all-gather.2.cloned.1.call-start = ((), (), s32[]{:S(2)}) async-start(), calls=%async_computation.5 | async-start | bytes 2228224 | tf_op jit(solution)/shard_map/all_gather | solution.py:295
  7.2 0.9 copy-start.6
  8.1 0.7 copy-start.8
  9.5 16.3 %collective-permute-start = (bf16[256,1024]{1,0:T(8,128)(2,1)}, bf16[256,1024]{1,0:T(8,128)(2,1)S(1)}, u32[]{:S(2)}, u32[]{:S(2)}) collective-permute-start(bf16[256,1024]{1,0:T(8,128)(2,1)} %bitcast.34), channel_id=1, source_target_pairs={{0,0},{1,64},{2,128},{3,192},{64,1},{65,65},{66,129},{67,193},{128... | collective-permute-start | bytes 1572872 | tf_op jit(solution)/shard_map/ppermute | solution.py:284
  11.2 1.0 copy-start
  12.3 0.8 copy-start.3
  13.1 0.7 copy-start.7
  13.8 46.0 %copy-start.1 = (bf16[1,256,1024]{2,1,0:T(8,128)(2,1)S(1)}, bf16[1,256,1024]{2,1,0:T(8,128)(2,1)}, u32[]{:S(2)}) copy-start(bf16[1,256,1024]{2,1,0:T(8,128)(2,1)} %param.7) | copy-start | bytes 1572868
  15.9 24.5 %all-to-all-start = ((bf16[16,8,1152]{2,1,0:T(8,128)(2,1)}), bf16[16,8,1152]{2,1,0:T(8,128)(2,1)S(1)}, u32[]{:S(2)}, u32[]{:S(2)}) async-start(bf16[16,8,1152]{2,1,0:T(8,128)(2,1)} %bitcast.5), calls=%async_computation | async-start | bytes 589824 | tf_op jit(solution)/shard_map/all_to_all | solution.py:302
  25.9 42.2 %collective-permute-start.1 = (bf16[256,1024]{1,0:T(8,128)(2,1)S(1)}, bf16[256,1024]{1,0:T(8,128)(2,1)S(1)}, u32[]{:S(2)}, u32[]{:S(2)}) collective-permute-start(bf16[256,1024]{1,0:T(8,128)(2,1)S(1)} %collective-permute-done.c0), channel_id=1, source_target_pairs={{0,1},{1,2},{2,3},{3,0},{4,5},{5,6},{6,7},{7,4},{8,9},{9,10},{10,1... | collective-permute-start | bytes 1572872 | tf_op jit(solution)/shard_map/ppermute | solution.py:287
  41.5 18.4 %all-to-all-start.1 = ((bf16[16,8,1024]{2,1,0:T(8,128)(2,1)}), bf16[16,8,1024]{2,1,0:T(8,128)(2,1)S(1)}, u32[]{:S(2)}, u32[]{:S(2)}) async-start(bf16[16,8,1024]{2,1,0:T(8,128)(2,1)} %bitcast.7), calls=%async_computation.1 | async-start | bytes 524288 | tf_op jit(solution)/shard_map/all_to_all | solution.py:306
  48.2 106.2 %reduce-scatter.2.cloned.1.call-start = ((), (), s32[]{:S(2)}) async-start(), calls=%async_computation.6 | async-start | bytes 2359296 | tf_op jit(solution)/shard_map/reduce_scatter | solution.py:347
  48.3 19.8 %collective-permute-start.2 = (bf16[256,1024]{1,0:T(8,128)(2,1)S(1)}, bf16[256,1024]{1,0:T(8,128)(2,1)S(1)}, u32[]{:S(2)}, u32[]{:S(2)}) collective-permute-start(bf16[256,1024]{1,0:T(8,128)(2,1)S(1)} %collective-permute-done.c0), channel_id=1, source_target_pairs={{0,2},{1,3},{2,0},{3,1},{4,6},{5,7},{6,4},{7,5},{8,10},{9,11},{10,... | collective-permute-start | bytes 1572872 | tf_op jit(solution)/shard_map/ppermute | solution.py:287
  55.0 22.5 %collective-permute-start.3 = (bf16[256,1024]{1,0:T(8,128)(2,1)S(1)}, bf16[256,1024]{1,0:T(8,128)(2,1)}, u32[]{:S(2)}, u32[]{:S(2)}) collective-permute-start(bf16[256,1024]{1,0:T(8,128)(2,1)S(1)} %collective-permute-done.c0), channel_id=1, source_target_pairs={{0,3},{1,0},{2,1},{3,2},{4,7},{5,4},{6,5},{7,6},{8,11},{9,8},{10,9... | collective-permute-start | bytes 1572872 | tf_op jit(solution)/shard_map/ppermute | solution.py:287
  61.3 24.9 %collective-permute-start.4 = (bf16[256,1024]{1,0:T(8,128)(2,1)S(1)}, bf16[256,1024]{1,0:T(8,128)(2,1)S(1)}, u32[]{:S(2)}, u32[]{:S(2)}) collective-permute-start(bf16[256,1024]{1,0:T(8,128)(2,1)S(1)} %shard_map.104.m0), channel_id=1, source_target_pairs={{0,64},{64,128},{128,192},{192,0},{1,65},{65,129},{129,193},{193,1... | collective-permute-start | bytes 1572872 | tf_op jit(solution)/shard_map/ppermute | solution.py:290
  63.3 28.3 %collective-permute-start.5 = (bf16[256,1024]{1,0:T(8,128)(2,1)S(1)}, bf16[256,1024]{1,0:T(8,128)(2,1)S(1)}, u32[]{:S(2)}, u32[]{:S(2)}) collective-permute-start(bf16[256,1024]{1,0:T(8,128)(2,1)S(1)} %shard_map.104.m0), channel_id=1, source_target_pairs={{0,128},{64,192},{128,0},{192,64},{1,129},{65,193},{129,1},{193,65... | collective-permute-start | bytes 1572872 | tf_op jit(solution)/shard_map/ppermute | solution.py:290
  68.0 23.5 %collective-permute-start.6 = (bf16[256,1024]{1,0:T(8,128)(2,1)S(1)}, bf16[256,1024]{1,0:T(8,128)(2,1)S(1)}, u32[]{:S(2)}, u32[]{:S(2)}) collective-permute-start(bf16[256,1024]{1,0:T(8,128)(2,1)S(1)} %shard_map.104.m0), channel_id=1, source_target_pairs={{0,192},{64,0},{128,64},{192,128},{1,193},{65,1},{129,65},{193,129... | collective-permute-start | bytes 1572872 | tf_op jit(solution)/shard_map/ppermute | solution.py:290
  82.6 16.2 %copy-start.9 = (bf16[256,1024]{1,0:T(8,128)(2,1)}, bf16[256,1024]{1,0:T(8,128)(2,1)S(1)}, u32[]{:S(2)}) copy-start(bf16[256,1024]{1,0:T(8,128)(2,1)S(1)} %get-tuple-element.41.g0) | copy-start | bytes 1572868
  82.6 17.1 %collective-permute-start.7 = (bf16[128,1024]{1,0:T(8,128)(2,1)S(1)}, bf16[128,1024]{1,0:T(8,128)(2,1)S(1)}, u32[]{:S(2)}, u32[]{:S(2)}) collective-permute-start(bf16[128,1024]{1,0:T(8,128)(2,1)S(1)} %get-tuple-element.38), channel_id=1, source_target_pairs={{0,64},{64,128},{128,192},{192,0},{1,65},{65,129},{129,193},{193,1... | collective-permute-start | bytes 786440 | tf_op jit(solution)/shard_map/ppermute | solution.py:290
  82.7 17.0 %collective-permute-start.8 = (bf16[128,1024]{1,0:T(8,128)(2,1)S(1)}, bf16[128,1024]{1,0:T(8,128)(2,1)S(1)}, u32[]{:S(2)}, u32[]{:S(2)}) collective-permute-start(bf16[128,1024]{1,0:T(8,128)(2,1)S(1)} %get-tuple-element.39), channel_id=1, source_target_pairs={{0,192},{64,0},{128,64},{192,128},{1,193},{65,1},{129,65},{193,129... | collective-permute-start | bytes 786440 | tf_op jit(solution)/shard_map/ppermute | solution.py:290
  91.6 0.8 copy-start.11
  98.9 4.4 %copy-start.2 = (bf16[8,64,1024]{2,1,0:T(8,128)(2,1)S(1)}, bf16[8,64,1024]{2,1,0:T(8,128)(2,1)}, u32[]{:S(2)}) copy-start(bf16[8,64,1024]{2,1,0:T(8,128)(2,1)} %get-tuple-element.54.mine_ref) | copy-start | bytes 3145732
  98.9 4.4 %collective-permute-start.11 = (bf16[8,64,1024]{2,1,0:T(8,128)(2,1)}, bf16[8,64,1024]{2,1,0:T(8,128)(2,1)S(1)}, u32[]{:S(2)}, u32[]{:S(2)}) collective-permute-start(bf16[8,64,1024]{2,1,0:T(8,128)(2,1)} %get-tuple-element.55), channel_id=1, source_target_pairs={{0,4},{4,0},{8,12},{12,8},{16,20},{20,16},{24,28},{28,24},{32,36},... | collective-permute-start | bytes 3145736 | tf_op jit(solution)/shard_map/ppermute | solution.py:344
  100.6 14.9 %collective-permute-start.9 = (bf16[256,1024]{1,0:T(8,128)(2,1)}, bf16[256,1024]{1,0:T(8,128)(2,1)S(1)}, u32[]{:S(2)}, u32[]{:S(2)}) collective-permute-start(bf16[256,1024]{1,0:T(8,128)(2,1)} %get-tuple-element.42), channel_id=1, source_target_pairs={{0,64},{64,128},{128,192},{192,0},{1,65},{65,129},{129,193},{193,1... | collective-permute-start | bytes 1572872 | tf_op jit(solution)/shard_map/ppermute | solution.py:290
  100.6 14.9 %collective-permute-start.10 = (bf16[256,1024]{1,0:T(8,128)(2,1)S(1)}, bf16[256,1024]{1,0:T(8,128)(2,1)}, u32[]{:S(2)}, u32[]{:S(2)}) collective-permute-start(bf16[256,1024]{1,0:T(8,128)(2,1)S(1)} %get-tuple-element.43), channel_id=1, source_target_pairs={{0,192},{64,0},{128,64},{192,128},{1,193},{65,1},{129,65},{193,129... | collective-permute-start | bytes 1572872 | tf_op jit(solution)/shard_map/ppermute | solution.py:290
  104.9 10.7 %copy-start.10 = (bf16[256,1024]{1,0:T(8,128)(2,1)S(1)}, bf16[256,1024]{1,0:T(8,128)(2,1)}, u32[]{:S(2)}) copy-start(bf16[256,1024]{1,0:T(8,128)(2,1)} %copy-done.9) | copy-start | bytes 1572868
Sparse Core Ops, SparseCore 0:
  9.8 47.2 all-gather.1
  105.0 39.9 reduce-scatter.1

commit v4 on v3

--- a/solution.py
+++ b/solution.py
@@ -33,6 +33,20 @@
             flops=flops, bytes_accessed=bytes_accessed, transcendentals=0
         ),
     )
+
+
+def staged(kernel, out_shape, *args):
+    def whole(value):
+        return pl.BlockSpec(value.shape, lambda i: (0,) * len(value.shape))
+
+    return pl.pallas_call(
+        kernel,
+        grid=(1,),
+        out_shape=out_shape,
+        in_specs=[whole(value) for value in args],
+        out_specs=jax.tree.map(whole, out_shape),
+        compiler_params=pltpu.CompilerParams(vmem_limit_bytes=VMEM_LIMIT),
+    )(*args)
 
 
 def dot(a, b, contract, precision=None):
@@ -155,15 +169,25 @@
         out_ref[:, lanes] = (jnp.where(half, parts[0], parts[1]) + carried).astype(bf16)
 
 
-def project_kernel(c0, c1, c2, c3, weight_ref, o0, o1, o2, o3, o4, held, sems):
-    copies = []
-    for m, ref in enumerate((c0, c1, c2, c3)):
-        slot = lax.rem(lax.axis_index("tp") - lax.axis_index("dp") + 8 - m, 4)
-        copy = pltpu.make_async_copy(ref, held.at[slot], sems.at[m])
+def hold_slices(refs, held, sems):
+    own, before, after, top, bottom = refs
+    place = lax.axis_index("tp") - lax.axis_index("dp") + 8
+    half = top.shape[0]
+    copies = [
+        pltpu.make_async_copy(own, held.at[lax.rem(place, 4)], sems.at[0]),
+        pltpu.make_async_copy(before, held.at[lax.rem(place - 1, 4)], sems.at[1]),
+        pltpu.make_async_copy(after, held.at[lax.rem(place + 1, 4)], sems.at[2]),
+        pltpu.make_async_copy(top, held.at[lax.rem(place + 2, 4), pl.ds(0, half)], sems.at[3]),
+        pltpu.make_async_copy(bottom, held.at[lax.rem(place + 2, 4), pl.ds(half, half)], sems.at[4]),
+    ]
+    for copy in copies:
         copy.start()
-        copies.append(copy)
     for copy in copies:
         copy.wait()
+
+
+def project_kernel(c0, c1, c2, c3, c4, weight_ref, o0, o1, o2, o3, o4, held, sems):
+    hold_slices((c0, c1, c2, c3, c4), held, sems)
     weight = weight_ref[...]
     half = o3.shape[0]
     opposite = dot(held[2], weight, (1, 0)).astype(bf16)
@@ -195,9 +219,9 @@
         summary_ref[:, lanes] = dot(r, scaled.astype(bf16), (0, 0)).astype(bf16)
 
 
-def gradients_kernel(
-    x_ref, w_ref, r_ref, g_ref, rows_ref, columns_ref, entering_ref, leaving_ref,
-    grad_input_ref, grad_write_ref, grad_read_ref,
+def local_kernel(
+    x_ref, w_ref, r_ref, g_ref, rows_ref, columns_ref, entering_ref,
+    input_ref, write_ref, grad_read_ref,
 ):
     length = x_ref.shape[0]
     heads = rows_ref.shape[0]
@@ -209,10 +233,8 @@
     meets = jnp.where(later, dot(w, r, (1, 1)), 0.0)
     cumulative = columns_ref[...]
     since = jnp.exp(cumulative)
-    to_end = jnp.exp(cumulative[length - 1 : length, :] - cumulative)
     half = low_half(length)
     weighted = jnp.zeros((length, length), f32)
-    grad_write = jnp.zeros((length, STATE), f32)
     grad_read = jnp.zeros((length, STATE), f32)
     for pair in range(heads // 2):
         lanes = slice(pair * LANES, (pair + 1) * LANES)
@@ -226,33 +248,50 @@
             mine = half if head % 2 == 0 else jnp.logical_not(half)
             own = jnp.where(mine, x, jnp.zeros_like(x))
             weighted = weighted + within * dot(own, g, (1, 1))
-        end_scale = pair_scale(to_end, pair, length)
-        leaving = leaving_ref[:, lanes]
-        carried = dot(w, leaving, (1, 0)) * end_scale
-        grad_input_ref[:, lanes] = (jnp.where(half, parts[0], parts[1]) + carried).astype(bf16)
-        grad_write += dot((x.astype(f32) * end_scale).astype(bf16), leaving, (1, 1))
+        input_ref[:, lanes] = jnp.where(half, parts[0], parts[1])
         scaled = (g.astype(f32) * pair_scale(since, pair, length)).astype(bf16)
         grad_read += dot(scaled, entering_ref[:, lanes], (1, 1))
     weighted = jnp.where(later, weighted, 0.0).astype(bf16)
-    grad_write_ref[...] = (grad_write + dot(weighted, r, (1, 0))).astype(bf16)
+    write_ref[...] = dot(weighted, r, (1, 0))
     grad_read_ref[...] = (grad_read + dot(weighted, w, (0, 0))).astype(bf16)
 
 
+def gradients_kernel(
+    x_ref, w_ref, columns_ref, leaving_ref, input_ref, write_ref, grad_input_ref, grad_write_ref
+):
+    length, columns = x_ref.shape
+    w = w_ref[...]
+    cumulative = columns_ref[...]
+    to_end = jnp.exp(cumulative[length - 1 : length, :] - cumulative)
+    grad_write = write_ref[...]
+    for pair in range(columns // LANES):
+        lanes = slice(pair * LANES, (pair + 1) * LANES)
+        scale = pair_scale(to_end, pair, length)
+        leaving = leaving_ref[:, lanes]
+        carried = dot(w, leaving, (1, 0)) * scale
+        grad_input_ref[:, lanes] = (input_ref[:, lanes] + carried).astype(bf16)
+        scaled = (x_ref[:, lanes].astype(f32) * scale).astype(bf16)
+        grad_write += dot(scaled, leaving, (1, 1))
+    grad_write_ref[...] = grad_write.astype(bf16)
+
+
 def weight_kernel(
-    c0, c1, c2, c3, m0, m1, m2, m3, mine_ref, other_ref, held, total, sems
+    c0, c1, c2, c3, c4, m0, m1, m2, m3, m4, mine_ref, other_ref, held, mixers, total, sems, mixer_sems
 ):
-    copies = []
-    for m, ref in enumerate((c0, c1, c2, c3)):
-        slot = lax.rem(lax.axis_index("tp") - lax.axis_index("dp") + 8 - m, 4)
-        copy = pltpu.make_async_copy(ref, held.at[slot], sems.at[m])
+    half = m3.shape[0]
+    places = (0, 3, 1, (2, pl.ds(0, half)), (2, pl.ds(half, half)))
+    copies = [
+        pltpu.make_async_copy(ref, mixers.at[place], mixer_sems.at[k])
+        for k, (ref, place) in enumerate(zip((m0, m1, m2, m3, m4), places))
+    ]
+    for copy in copies:
         copy.start()
-        copies.append(copy)
+    hold_slices((c0, c1, c2, c3, c4), held, sems)
     for copy in copies:
         copy.wait()
-    mixers = (m0, m3, m2, m1)
-    acc = dot(held[0], mixers[0][...], (0, 0))
+    acc = dot(held[0], mixers[0], (0, 0))
     for n in range(1, 4):
-        acc = acc + dot(held[n], mixers[n][...], (0, 0))
+        acc = acc + dot(held[n], mixers[n], (0, 0))
     total[...] = acc
     ring, rows = mine_ref.shape[0], mine_ref.shape[1]
     core = lax.rem(lax.axis_index("ctx"), 2)
@@ -267,6 +306,12 @@
     out_ref[...] = mine_ref[...].astype(f32) + other_ref[...].astype(f32)
 
 
+def ring_gather(value, along):
+    half = value.shape[0] // 2
+    before, after = along(value, 1), along(value, -1)
+    return [value, before, after, along(before[:half], 1), along(after[half:], -1)]
+
+
 def shape(dims, dtype=bf16):
     return jax.ShapeDtypeStruct(dims, dtype)
 
@@ -290,15 +335,15 @@
         return lax.ppermute(value, "dp", [(i, (i + n) % dp) for i in range(dp)])
 
     turned = transposed(cotangent[0])
-    cots = [turned] + [along_tp(turned, m) for m in range(1, tp)]
-    dequant = call(dequant_kernel, shape(out_weight.shape), 2)(out_weight, scale_exponent)
+    cots = ring_gather(turned, along_tp)
+    dequant = staged(dequant_kernel, shape(out_weight.shape), out_weight, scale_exponent)
     weight = lax.all_gather(dequant, "ctx", axis=0, tiled=True)
 
-    packed, cum_rows, cum_columns = call(
+    packed, cum_rows, cum_columns = staged(
         state_kernel,
         [shape((STATE, columns + LANES)), shape((heads, length), f32), shape((length, LANES), f32)],
-        3,
-    )(x, w, log_decay[0])
+        x, w, log_decay[0],
+    )
     packed = lax.all_to_all(packed, "ctx", 0, 0, tiled=True)
     entering, decays = call(
         forward_scan_kernel, [shape((STATE, columns)), shape((ctx, columns), f32)], 1
@@ -309,7 +354,7 @@
         x, w, r, cum_rows, cum_columns, entering
     )
     mixer, weight = lax.optimization_barrier((mixer, weight))
-    mixers = [mixer] + [along_dp(mixer, n) for n in range(1, dp)]
+    mixers = ring_gather(mixer, along_dp)
 
     vmem = pl.BlockSpec(memory_space=pltpu.VMEM)
     anywhere = pl.BlockSpec(memory_space=pl.ANY)
@@ -317,9 +362,9 @@
     parts = call(
         project_kernel,
         [shape((length, columns))] * 3 + [shape((length // 2, columns))] * 2,
-        5,
-        scratch=[pltpu.VMEM((dp, length, model), bf16), pltpu.SemaphoreType.DMA((dp,))],
-        in_specs=[anywhere] * dp + [vmem],
+        6,
+        scratch=[pltpu.VMEM((dp, length, model), bf16), pltpu.SemaphoreType.DMA((5,))],
+        in_specs=[anywhere] * 5 + [vmem],
     )(*cots, weight)
     top, bottom = along_dp(parts[3], 1), along_dp(parts[4], -1)
     folded = call(fold_kernel, [shape((length, columns))] * 2, 4, flops=40_000_000_000)(
@@ -336,10 +381,12 @@
         flops=20_000_000_000,
         scratch=[
             pltpu.VMEM((dp, length, model), bf16),
+            pltpu.VMEM((dp, length, columns), bf16),
             pltpu.VMEM((model, columns), f32),
-            pltpu.SemaphoreType.DMA((dp,)),
+            pltpu.SemaphoreType.DMA((5,)),
+            pltpu.SemaphoreType.DMA((5,)),
         ],
-        in_specs=[anywhere] * dp + [vmem] * dp,
+        in_specs=[anywhere] * 10,
     )(*cots, *mixers)
     other = lax.ppermute(other, "ctx", [(i, i ^ 1) for i in range(ctx)])
     total = call(add_kernel, shape((ctx // 2, rows, columns), f32), 2)(mine, other)
@@ -356,11 +403,14 @@
     summary = lax.all_to_all(summary, "ctx", 0, 0, tiled=True)
     leaving = call(backward_scan_kernel, shape((STATE, columns)), 2)(summary, decays)
     leaving = lax.all_to_all(leaving, "ctx", 0, 0, tiled=True)
-    grad_input, grad_write, grad_read = call(
-        gradients_kernel,
-        [shape((length, columns)), shape((length, STATE)), shape((length, STATE))],
-        8,
-    )(x, w, r, grad, cum_rows, cum_columns, entering, leaving)
+    local_input, local_write, grad_read = call(
+        local_kernel,
+        [shape((length, columns), f32), shape((length, STATE), f32), shape((length, STATE))],
+        7,
+    )(x, w, r, grad, cum_rows, cum_columns, entering)
+    grad_input, grad_write = call(
+        gradients_kernel, [shape((length, columns)), shape((length, STATE))], 6
+    )(x, w, cum_columns, leaving, local_input, local_write)
     return grad_input[None], grad_write[None], grad_read[None], grad_weight
 
 

time: 162 us -> 159 us (0.981)
  blocking collectives: 33.8 us -> 21.5 us
  waiting for transfers between devices: 35.6 us -> 42.5 us
    all_to_all x1 -> x0, blocking collectives: 15.9 us -> none  [per_device(): leaving = lax.all_to_all(leaving, 'ctx', 0, 0, tiled=True)]
    all_to_all x0 -> x1, waiting for transfers between devices: none -> 8.95 us  [per_device(): leaving = lax.all_to_all(leaving, 'ctx', 0, 0, tiled=True)]
    all_to_all x1, waiting for transfers between devices: 5.25 us -> 13.6 us  [per_device(): packed = lax.all_to_all(packed, 'ctx', 0, 0, tiled=True)]
    all_to_all x1, waiting for transfers between devices: 4.83 us -> 0.01 us  [per_device(): entering = lax.all_to_all(entering, 'ctx', 0, 0, tiled=True)]
    ppermute x7 -> x8, waiting for transfers between devices: 16 us -> 12.2 us  [along_dp(): return lax.ppermute(value, 'dp', [(i, (i + n) % dp) for i in range(dp)])]
    all_to_all x1, blocking collectives: 17.8 us -> 21.5 us  [per_device(): summary = lax.all_to_all(summary, 'ctx', 0, 0, tiled=True)]
    all_to_all x0 -> x1, starting transfers between devices: none -> 3.43 us  [per_device(): leaving = lax.all_to_all(leaving, 'ctx', 0, 0, tiled=True)]
    all_to_all x1, starting transfers between devices: 6.78 us -> 3.43 us  [per_device(): entering = lax.all_to_all(entering, 'ctx', 0, 0, tiled=True)]
  transfers between devices with their start and end apart: 16 -> 19, of which waited for: 5 -> 7; matrix products, arithmetic and copies ran while one was open for 0% -> 0% of each run, Pallas kernels for 15% -> 16%
where the time goes in v4:
time: 159 us; the launch traced here: 158 us
  starting transfers between devices  48.1 us (30%)
  waiting for transfers between devices  42.5 us (27%)
  Pallas kernels  25.2 us (16%)
  blocking collectives  21.5 us (14%)
  between operations  14.2 us (9%)
  local copies, waits for them, and re-layouts  6.13 us (4%)
    all_to_all x1, blocking collectives, per_device(): summary = lax.all_to_all(summary, 'ctx', 0, 0, tiled=True)  21.5 us
    ppermute x4, starting transfers between devices, along_tp(): return lax.ppermute(value, 'tp', [(i, (i + n) % tp) for i in range(tp)])  15.6 us
    all_to_all x1, waiting for transfers between devices, per_device(): packed = lax.all_to_all(packed, 'ctx', 0, 0, tiled=True)  13.6 us
    ppermute x8, waiting for transfers between devices, along_dp(): return lax.ppermute(value, 'dp', [(i, (i + n) % dp) for i in range(dp)])  12.2 us
    ppermute x8, starting transfers between devices, along_dp(): return lax.ppermute(value, 'dp', [(i, (i + n) % dp) for i in range(dp)])  11 us
    all_to_all x1, starting transfers between devices, per_device(): packed = lax.all_to_all(packed, 'ctx', 0, 0, tiled=True)  9.98 us
    all_to_all x1, waiting for transfers between devices, per_device(): leaving = lax.all_to_all(leaving, 'ctx', 0, 0, tiled=True)  8.95 us
    ppermute x4, waiting for transfers between devices, along_tp(): return lax.ppermute(value, 'tp', [(i, (i + n) % tp) for i in range(tp)])  7.19 us
  transfers between devices with their start and end apart: 19, of which 7 were waited for; matrix products, arithmetic and copies ran while one was open for 0% of the time, Pallas kernels for 16%

profile of v4, /device:TPU:1, one launch (start us, length us, event | category | flops | bytes accessed | tf_op | source)
XLA Modules:
  0.0 157.7 jit_solution(4254052227841748105)
XLA Ops:
  7.2 0.0 copy-start.5
  7.2 0.0 copy-start.7
  7.2 0.0 all-gather.2.cloned.1.call-start
  7.2 0.0 copy-start.8
  7.2 0.9 copy-done.8
  8.1 0.7 copy-done.10
  8.8 0.7 shard_map.105
  9.5 0.0 all-gather.2.cloned.1.call-update
  9.5 0.0 copy-start
  9.5 1.0 copy-done
  10.6 0.8 copy-done.4
  11.4 0.7 copy-done.9
  12.1 2.0 %shard_map.102 = (bf16[128,1152]{1,0:T(8,128)(2,1)}, f32[16,256]{1,0:T(8,128)S(1)}, f32[256,128]{1,0:T(8,128)S(1)}) custom-call(bf16[256,1024]{1,0:T(8,128)(2,1)S(1)} %bitcast.17, bf16[256,128]{1,0:T(8,128)(2,1)S(1)} %bitcast.24, f32[16,256]{1,0:T(8,128)S(1)} %bitcast.34), custom_call_target="tpu_custom_call" | custom-call | tf_op jit(solution)/shard_map/pallas_call | solution.py:42
  14.2 10.0 %all-to-all-start = ((bf16[16,8,1152]{2,1,0:T(8,128)(2,1)}), bf16[16,8,1152]{2,1,0:T(8,128)(2,1)S(1)}, u32[]{:S(2)}, u32[]{:S(2)}) async-start(bf16[16,8,1152]{2,1,0:T(8,128)(2,1)} %bitcast.5), calls=%async_computation | async-start | bytes 589824 | tf_op jit(solution)/shard_map/all_to_all | solution.py:347
  24.1 1.7 %collective-permute-start = (bf16[256,1024]{1,0:T(8,128)(2,1)}, bf16[256,1024]{1,0:T(8,128)(2,1)S(1)}, u32[]{:S(2)}, u32[]{:S(2)}) collective-permute-start(bf16[256,1024]{1,0:T(8,128)(2,1)} %bitcast.35), channel_id=1, source_target_pairs={{0,0},{1,64},{2,128},{3,192},{64,1},{65,65},{66,129},{67,193},{128... | collective-permute-start | bytes 1572872 | tf_op jit(solution)/shard_map/ppermute | solution.py:329
  25.8 13.6 %all-to-all-done = bf16[16,8,1152]{2,1,0:T(8,128)(2,1)S(1)} async-done(((bf16[16,8,1152]{2,1,0:T(8,128)(2,1)}), bf16[16,8,1152]{2,1,0:T(8,128)(2,1)S(1)}, u32[]{:S(2)}, u32[]{:S(2)}) %all-to-all-start) | async-done | bytes 294944 | tf_op jit(solution)/shard_map/all_to_all | solution.py:347
  39.5 1.0 shard_map.103
  40.5 3.4 %all-to-all-start.1 = ((bf16[16,8,1024]{2,1,0:T(8,128)(2,1)}), bf16[16,8,1024]{2,1,0:T(8,128)(2,1)S(1)}, u32[]{:S(2)}, u32[]{:S(2)}) async-start(bf16[16,8,1024]{2,1,0:T(8,128)(2,1)} %bitcast.7), calls=%async_computation.1 | async-start | bytes 524288 | tf_op jit(solution)/shard_map/all_to_all | solution.py:351
  44.0 0.0 reduce-scatter.2.cloned.1.call-start
  44.0 0.0 collective-permute-done.c0
  44.0 6.6 %collective-permute-start.1 = (bf16[256,1024]{1,0:T(8,128)(2,1)S(1)}, bf16[256,1024]{1,0:T(8,128)(2,1)S(1)}, u32[]{:S(2)}, u32[]{:S(2)}) collective-permute-start(bf16[256,1024]{1,0:T(8,128)(2,1)S(1)} %collective-permute-done.c0), channel_id=1, source_target_pairs={{0,1},{1,2},{2,3},{3,0},{4,5},{5,6},{6,7},{7,4},{8,9},{9,10},{10,1... | collective-permute-start | bytes 1572872 | tf_op jit(solution)/shard_map/ppermute | solution.py:332
  50.6 6.1 %collective-permute-start.2 = (bf16[256,1024]{1,0:T(8,128)(2,1)S(1)}, bf16[256,1024]{1,0:T(8,128)(2,1)S(1)}, u32[]{:S(2)}, u32[]{:S(2)}) collective-permute-start(bf16[256,1024]{1,0:T(8,128)(2,1)S(1)} %collective-permute-done.c0), channel_id=1, source_target_pairs={{0,3},{1,0},{2,1},{3,2},{4,7},{5,4},{6,5},{7,6},{8,11},{9,8},{10,9... | collective-permute-start | bytes 1572872 | tf_op jit(solution)/shard_map/ppermute | solution.py:332
  56.8 0.0 all-to-all-done.1
  56.8 1.4 shard_map.104.m0
  58.2 0.4 all-gather.2.cloned.1.call-done.weight_ref
  58.7 1.4 collective-permute-start.5
  60.0 1.5 collective-permute-start.6
  61.5 6.7 %collective-permute-done.1.c1 = bf16[256,1024]{1,0:T(8,128)(2,1)S(1)} collective-permute-done((bf16[256,1024]{1,0:T(8,128)(2,1)S(1)}, bf16[256,1024]{1,0:T(8,128)(2,1)S(1)}, u32[]{:S(2)}, u32[]{:S(2)}) %collective-permute-start.1) | collective-permute-done | bytes 524320 | tf_op jit(solution)/shard_map/ppermute | solution.py:332
  68.2 0.1 collective-permute-start.3
  68.3 0.0 collective-permute-done.2.c2
  68.3 0.0 copy-start.2
  68.4 2.7 %collective-permute-start.4 = (bf16[128,1024]{1,0:T(8,128)(2,1)S(1)}, bf16[128,1024]{1,0:T(8,128)(2,1)S(1)}, u32[]{:S(2)}, u32[]{:S(2)}) collective-permute-start(bf16[128,1024]{1,0:T(8,128)(2,1)S(1)} %slice.17), channel_id=1, source_target_pairs={{0,3},{1,0},{2,1},{3,2},{4,7},{5,4},{6,5},{7,6},{8,11},{9,8},{10,9... | collective-permute-start | bytes 786440 | tf_op jit(solution)/shard_map/ppermute | solution.py:332
  71.1 1.4 collective-permute-done.5.m1
  72.5 0.9 collective-permute-start.7
  73.4 0.0 collective-permute-done.6.m2
  73.4 2.0 %collective-permute-start.8 = (bf16[128,1024]{1,0:T(8,128)(2,1)S(1)}, bf16[128,1024]{1,0:T(8,128)(2,1)S(1)}, u32[]{:S(2)}, u32[]{:S(2)}) collective-permute-start(bf16[128,1024]{1,0:T(8,128)(2,1)S(1)} %slice.19), channel_id=1, source_target_pairs={{0,192},{64,0},{128,64},{192,128},{1,193},{65,1},{129,65},{193,129... | collective-permute-start | bytes 786440 | tf_op jit(solution)/shard_map/ppermute | solution.py:335
  75.4 0.5 collective-permute-done.3.c3
  75.8 0.0 collective-permute-done.4.c4
  75.9 5.1 %shard_map.106 = (bf16[256,1024]{1,0:T(8,128)(2,1)S(1)}, bf16[256,1024]{1,0:T(8,128)(2,1)S(1)}, bf16[256,1024]{1,0:T(8,128)(2,1)S(1)}, bf16[128,1024]{1,0:T(8,128)(2,1)S(1)}, bf16[128,1024]{1,0:T(8,128)(2,1)S(1)}) custom-call(bf16[256,1024]{1,0:T(8,128)(2,1)S(1)} %collective-permute-done.c0, bf16[256,1024]{1,0:T(8,128)(2,1)S(1)} %collective-permute-done.1.c1, ...), custom_call_target="tpu_custom_call" | custom-call | tf_op jit(solution)/shard_map/pallas_call | solution.py:362
  81.0 0.8 copy-done.11
  81.8 0.0 collective-permute-start.9
  81.8 2.7 %collective-permute-start.10 = (bf16[128,1024]{1,0:T(8,128)(2,1)S(1)}, bf16[128,1024]{1,0:T(8,128)(2,1)S(1)}, u32[]{:S(2)}, u32[]{:S(2)}) collective-permute-start(bf16[128,1024]{1,0:T(8,128)(2,1)S(1)} %get-tuple-element.42), channel_id=1, source_target_pairs={{0,192},{64,0},{128,64},{192,128},{1,193},{65,1},{129,65},{193,129... | collective-permute-start | bytes 786440 | tf_op jit(solution)/shard_map/ppermute | solution.py:335
  84.4 0.0 collective-permute-done.7.m3
  84.4 0.0 collective-permute-done.8.m4
  84.5 1.0 copy-done.3
  85.5 5.5 %shard_map.112 = (bf16[8,64,1024]{2,1,0:T(8,128)(2,1)}, bf16[8,64,1024]{2,1,0:T(8,128)(2,1)}) custom-call(bf16[256,1024]{1,0:T(8,128)(2,1)S(1)} %collective-permute-done.c0, bf16[256,1024]{1,0:T(8,128)(2,1)S(1)} %collective-permute-done.1.c1, bf16[256,1024]{1,0:T(8,128)(2,1)S(1)} %copy-done.3, bf16[128,1024]{1,0:T(8,128)(2,1)S(1)} %collective-permute-done.3.c3, ...), custom_call_target="tpu_custom_call" | custom-call | flops 20000000000 | tf_op jit(solution)/shard_map/pallas_call | solution.py:377
  91.0 2.9 %collective-permute-start.13 = (bf16[8,64,1024]{2,1,0:T(8,128)(2,1)}, bf16[8,64,1024]{2,1,0:T(8,128)(2,1)S(1)}, u32[]{:S(2)}, u32[]{:S(2)}) collective-permute-start(bf16[8,64,1024]{2,1,0:T(8,128)(2,1)} %get-tuple-element.61), channel_id=1, source_target_pairs={{0,4},{4,0},{8,12},{12,8},{16,20},{20,16},{24,28},{28,24},{32,36},... | collective-permute-start | bytes 3145736 | tf_op jit(solution)/shard_map/ppermute | solution.py:391
  93.9 0.0 collective-permute-done.9.top
  93.9 0.0 collective-permute-done.10.bottom
  93.9 0.9 shard_map.107
  94.8 0.0 collective-permute-start.11
  94.8 2.7 %collective-permute-start.12 = (bf16[256,1024]{1,0:T(8,128)(2,1)S(1)}, bf16[256,1024]{1,0:T(8,128)(2,1)}, u32[]{:S(2)}, u32[]{:S(2)}) collective-permute-start(bf16[256,1024]{1,0:T(8,128)(2,1)S(1)} %get-tuple-element.46), channel_id=1, source_target_pairs={{0,192},{64,0},{128,64},{192,128},{1,193},{65,1},{129,65},{193,129... | collective-permute-start | bytes 1572872 | tf_op jit(solution)/shard_map/ppermute | solution.py:335
  97.4 0.0 collective-permute-done.13.other_ref
  97.5 1.6 shard_map.113
  99.0 0.0 reduce-scatter.2.cloned.1.call-update
  99.0 10.8 %collective-permute-done.11.g1 = bf16[256,1024]{1,0:T(8,128)(2,1)} collective-permute-done((bf16[256,1024]{1,0:T(8,128)(2,1)}, bf16[256,1024]{1,0:T(8,128)(2,1)}, u32[]{:S(2)}, u32[]{:S(2)}) %collective-permute-start.11) | collective-permute-done | bytes 524320 | tf_op jit(solution)/shard_map/ppermute | solution.py:335
  109.8 0.0 collective-permute-done.12.g2
  109.8 2.1 %shard_map.108 = (bf16[256,1024]{1,0:T(8,128)(2,1)S(1)}, bf16[128,1024]{1,0:T(8,128)(2,1)S(1)}) custom-call(bf16[256,1024]{1,0:T(8,128)(2,1)S(1)} %copy-done.12, bf16[256,1024]{1,0:T(8,128)(2,1)} %collective-permute-done.11.g1, bf16[256,1024]{1,0:T(8,128)(2,1)} %collective-permute-done.12.g2, bf16[256,128]{1,0:T(8,128)(2,1)S(1)} %bitcast.31, ...), custom_call_target="tpu_custom_call" | custom-call | flops 49999998976 | tf_op jit(solution)/shard_map/pallas_call | solution.py:395
  112.0 21.5 %all_to_all.44 = bf16[16,8,1024]{2,1,0:T(8,128)(2,1)S(1)} all-to-all(bf16[16,8,1024]{2,1,0:T(8,128)(2,1)S(1)} %bitcast.33), channel_id=1, replica_groups=mesh['dp'=4,'ctx'=16,'tp'=4] {'ctx'}, dimensions={0} | all-to-all | bytes 524288 | tf_op jit(solution)/shard_map/all_to_all | solution.py:403
  133.5 0.8 shard_map.109
  134.3 3.4 %all-to-all-start.3 = ((bf16[16,8,1024]{2,1,0:T(8,128)(2,1)}), bf16[16,8,1024]{2,1,0:T(8,128)(2,1)S(1)}, u32[]{:S(2)}, u32[]{:S(2)}) async-start(bf16[16,8,1024]{2,1,0:T(8,128)(2,1)} %bitcast.11), calls=%async_computation.3 | async-start | bytes 524288 | tf_op jit(solution)/shard_map/all_to_all | solution.py:405
  137.7 2.7 %shard_map.110 = (f32[256,1024]{1,0:T(8,128)S(1)}, f32[256,128]{1,0:T(8,128)S(1)}, bf16[256,128]{1,0:T(8,128)(2,1)}) custom-call(bf16[256,1024]{1,0:T(8,128)(2,1)S(1)} %bitcast.19, bf16[256,128]{1,0:T(8,128)(2,1)S(1)} %bitcast.26, bf16[256,128]{1,0:T(8,128)(2,1)S(1)} %bitcast.32, bf16[256,1024]{1,0:T(8,128)(2,1)S(1)} %get-tuple-element.49.g_ref, ...), custom_call_target="tpu_custom_call" | custom-call | tf_op jit(solution)/shard_map/pallas_call | solution.py:406
  140.4 9.0 %all-to-all-done.3 = bf16[16,8,1024]{2,1,0:T(8,128)(2,1)S(1)} async-done(((bf16[16,8,1024]{2,1,0:T(8,128)(2,1)}), bf16[16,8,1024]{2,1,0:T(8,128)(2,1)S(1)}, u32[]{:S(2)}, u32[]{:S(2)}) %all-to-all-start.3) | async-done | bytes 262176 | tf_op jit(solution)/shard_map/all_to_all | solution.py:405
  149.3 1.5 shard_map.111
  (21 shorter events, 0.1 us)
Async XLA Ops:
  7.2 49.6 %copy-start.5 = (bf16[1,256,128]{2,1,0:T(8,128)(2,1)S(1)}, bf16[1,256,128]{2,1,0:T(8,128)(2,1)}, u32[]{:S(2)}) copy-start(bf16[1,256,128]{2,1,0:T(8,128)(2,1)} %param.8) | copy-start | bytes 196612
  7.2 49.6 %copy-start.7 = (bf16[1,256,128]{2,1,0:T(8,128)(2,1)S(1)}, bf16[1,256,128]{2,1,0:T(8,128)(2,1)}, u32[]{:S(2)}) copy-start(bf16[1,256,128]{2,1,0:T(8,128)(2,1)} %param.9) | copy-start | bytes 196612
  7.2 51.5 %all-gather.2.cloned.1.call-start = ((), (), s32[]{:S(2)}) async-start(), calls=%async_computation.5 | async-start | bytes 2228224 | tf_op jit(solution)/shard_map/all_gather | solution.py:340
  7.2 0.9 copy-start.8
  8.1 0.7 copy-start.10
  9.5 1.0 copy-start
  10.6 0.8 copy-start.4
  11.4 0.7 copy-start.9
  12.1 44.7 %copy-start.1 = (bf16[1,256,1024]{2,1,0:T(8,128)(2,1)S(1)}, bf16[1,256,1024]{2,1,0:T(8,128)(2,1)}, u32[]{:S(2)}) copy-start(bf16[1,256,1024]{2,1,0:T(8,128)(2,1)} %param.7) | copy-start | bytes 1572868
  14.2 25.3 %all-to-all-start = ((bf16[16,8,1152]{2,1,0:T(8,128)(2,1)}), bf16[16,8,1152]{2,1,0:T(8,128)(2,1)S(1)}, u32[]{:S(2)}, u32[]{:S(2)}) async-start(bf16[16,8,1152]{2,1,0:T(8,128)(2,1)} %bitcast.5), calls=%async_computation | async-start | bytes 589824 | tf_op jit(solution)/shard_map/all_to_all | solution.py:347
  24.1 19.9 %collective-permute-start = (bf16[256,1024]{1,0:T(8,128)(2,1)}, bf16[256,1024]{1,0:T(8,128)(2,1)S(1)}, u32[]{:S(2)}, u32[]{:S(2)}) collective-permute-start(bf16[256,1024]{1,0:T(8,128)(2,1)} %bitcast.35), channel_id=1, source_target_pairs={{0,0},{1,64},{2,128},{3,192},{64,1},{65,65},{66,129},{67,193},{128... | collective-permute-start | bytes 1572872 | tf_op jit(solution)/shard_map/ppermute | solution.py:329
  40.5 16.3 %all-to-all-start.1 = ((bf16[16,8,1024]{2,1,0:T(8,128)(2,1)}), bf16[16,8,1024]{2,1,0:T(8,128)(2,1)S(1)}, u32[]{:S(2)}, u32[]{:S(2)}) async-start(bf16[16,8,1024]{2,1,0:T(8,128)(2,1)} %bitcast.7), calls=%async_computation.1 | async-start | bytes 524288 | tf_op jit(solution)/shard_map/all_to_all | solution.py:351
  44.0 106.9 %reduce-scatter.2.cloned.1.call-start = ((), (), s32[]{:S(2)}) async-start(), calls=%async_computation.6 | async-start | bytes 2359296 | tf_op jit(solution)/shard_map/reduce_scatter | solution.py:394
  44.0 24.2 %collective-permute-start.1 = (bf16[256,1024]{1,0:T(8,128)(2,1)S(1)}, bf16[256,1024]{1,0:T(8,128)(2,1)S(1)}, u32[]{:S(2)}, u32[]{:S(2)}) collective-permute-start(bf16[256,1024]{1,0:T(8,128)(2,1)S(1)} %collective-permute-done.c0), channel_id=1, source_target_pairs={{0,1},{1,2},{2,3},{3,0},{4,5},{5,6},{6,7},{7,4},{8,9},{9,10},{10,1... | collective-permute-start | bytes 1572872 | tf_op jit(solution)/shard_map/ppermute | solution.py:332
  50.6 17.7 %collective-permute-start.2 = (bf16[256,1024]{1,0:T(8,128)(2,1)S(1)}, bf16[256,1024]{1,0:T(8,128)(2,1)S(1)}, u32[]{:S(2)}, u32[]{:S(2)}) collective-permute-start(bf16[256,1024]{1,0:T(8,128)(2,1)S(1)} %collective-permute-done.c0), channel_id=1, source_target_pairs={{0,3},{1,0},{2,1},{3,2},{4,7},{5,4},{6,5},{7,6},{8,11},{9,8},{10,9... | collective-permute-start | bytes 1572872 | tf_op jit(solution)/shard_map/ppermute | solution.py:332
  58.7 13.8 %collective-permute-start.5 = (bf16[256,1024]{1,0:T(8,128)(2,1)S(1)}, bf16[256,1024]{1,0:T(8,128)(2,1)S(1)}, u32[]{:S(2)}, u32[]{:S(2)}) collective-permute-start(bf16[256,1024]{1,0:T(8,128)(2,1)S(1)} %shard_map.104.m0), channel_id=1, source_target_pairs={{0,64},{64,128},{128,192},{192,0},{1,65},{65,129},{129,193},{193,1... | collective-permute-start | bytes 1572872 | tf_op jit(solution)/shard_map/ppermute | solution.py:335
  60.0 13.4 %collective-permute-start.6 = (bf16[256,1024]{1,0:T(8,128)(2,1)S(1)}, bf16[256,1024]{1,0:T(8,128)(2,1)S(1)}, u32[]{:S(2)}, u32[]{:S(2)}) collective-permute-start(bf16[256,1024]{1,0:T(8,128)(2,1)S(1)} %shard_map.104.m0), channel_id=1, source_target_pairs={{0,192},{64,0},{128,64},{192,128},{1,193},{65,1},{129,65},{193,129... | collective-permute-start | bytes 1572872 | tf_op jit(solution)/shard_map/ppermute | solution.py:335
  68.2 7.6 %collective-permute-start.3 = (bf16[128,1024]{1,0:T(8,128)(2,1)S(1)}, bf16[128,1024]{1,0:T(8,128)(2,1)S(1)}, u32[]{:S(2)}, u32[]{:S(2)}) collective-permute-start(bf16[128,1024]{1,0:T(8,128)(2,1)S(1)} %slice.16), channel_id=1, source_target_pairs={{0,1},{1,2},{2,3},{3,0},{4,5},{5,6},{6,7},{7,4},{8,9},{9,10},{10,1... | collective-permute-start | bytes 786440 | tf_op jit(solution)/shard_map/ppermute | solution.py:332
  68.3 7.5 %copy-start.2 = (bf16[256,1024]{1,0:T(8,128)(2,1)}, bf16[256,1024]{1,0:T(8,128)(2,1)S(1)}, u32[]{:S(2)}) copy-start(bf16[256,1024]{1,0:T(8,128)(2,1)S(1)} %collective-permute-done.2.c2) | copy-start | bytes 1572868
  68.4 7.5 %collective-permute-start.4 = (bf16[128,1024]{1,0:T(8,128)(2,1)S(1)}, bf16[128,1024]{1,0:T(8,128)(2,1)S(1)}, u32[]{:S(2)}, u32[]{:S(2)}) collective-permute-start(bf16[128,1024]{1,0:T(8,128)(2,1)S(1)} %slice.17), channel_id=1, source_target_pairs={{0,3},{1,0},{2,1},{3,2},{4,7},{5,4},{6,5},{7,6},{8,11},{9,8},{10,9... | collective-permute-start | bytes 786440 | tf_op jit(solution)/shard_map/ppermute | solution.py:332
  72.5 11.9 %collective-permute-start.7 = (bf16[128,1024]{1,0:T(8,128)(2,1)S(1)}, bf16[128,1024]{1,0:T(8,128)(2,1)S(1)}, u32[]{:S(2)}, u32[]{:S(2)}) collective-permute-start(bf16[128,1024]{1,0:T(8,128)(2,1)S(1)} %slice.18), channel_id=1, source_target_pairs={{0,64},{64,128},{128,192},{192,0},{1,65},{65,129},{129,193},{193,1... | collective-permute-start | bytes 786440 | tf_op jit(solution)/shard_map/ppermute | solution.py:335
  73.4 7.6 %copy-start.13 = (bf16[256,1024]{1,0:T(8,128)(2,1)}, bf16[256,1024]{1,0:T(8,128)(2,1)S(1)}, u32[]{:S(2)}) copy-start(bf16[256,1024]{1,0:T(8,128)(2,1)S(1)} %collective-permute-done.6.m2) | copy-start | bytes 1572868
  73.4 11.0 %collective-permute-start.8 = (bf16[128,1024]{1,0:T(8,128)(2,1)S(1)}, bf16[128,1024]{1,0:T(8,128)(2,1)S(1)}, u32[]{:S(2)}, u32[]{:S(2)}) collective-permute-start(bf16[128,1024]{1,0:T(8,128)(2,1)S(1)} %slice.19), channel_id=1, source_target_pairs={{0,192},{64,0},{128,64},{192,128},{1,193},{65,1},{129,65},{193,129... | collective-permute-start | bytes 786440 | tf_op jit(solution)/shard_map/ppermute | solution.py:335
  81.0 0.8 copy-start.11
  81.8 12.1 %collective-permute-start.9 = (bf16[128,1024]{1,0:T(8,128)(2,1)S(1)}, bf16[128,1024]{1,0:T(8,128)(2,1)S(1)}, u32[]{:S(2)}, u32[]{:S(2)}) collective-permute-start(bf16[128,1024]{1,0:T(8,128)(2,1)S(1)} %get-tuple-element.41), channel_id=1, source_target_pairs={{0,64},{64,128},{128,192},{192,0},{1,65},{65,129},{129,193},{193,1... | collective-permute-start | bytes 786440 | tf_op jit(solution)/shard_map/ppermute | solution.py:335
  81.8 12.1 %collective-permute-start.10 = (bf16[128,1024]{1,0:T(8,128)(2,1)S(1)}, bf16[128,1024]{1,0:T(8,128)(2,1)S(1)}, u32[]{:S(2)}, u32[]{:S(2)}) collective-permute-start(bf16[128,1024]{1,0:T(8,128)(2,1)S(1)} %get-tuple-element.42), channel_id=1, source_target_pairs={{0,192},{64,0},{128,64},{192,128},{1,193},{65,1},{129,65},{193,129... | collective-permute-start | bytes 786440 | tf_op jit(solution)/shard_map/ppermute | solution.py:335
  84.4 1.0 copy-start.3
  91.0 6.5 %copy-start.6 = (bf16[8,64,1024]{2,1,0:T(8,128)(2,1)S(1)}, bf16[8,64,1024]{2,1,0:T(8,128)(2,1)}, u32[]{:S(2)}) copy-start(bf16[8,64,1024]{2,1,0:T(8,128)(2,1)} %get-tuple-element.60.mine_ref) | copy-start | bytes 3145732
  91.0 6.5 %collective-permute-start.13 = (bf16[8,64,1024]{2,1,0:T(8,128)(2,1)}, bf16[8,64,1024]{2,1,0:T(8,128)(2,1)S(1)}, u32[]{:S(2)}, u32[]{:S(2)}) collective-permute-start(bf16[8,64,1024]{2,1,0:T(8,128)(2,1)} %get-tuple-element.61), channel_id=1, source_target_pairs={{0,4},{4,0},{8,12},{12,8},{16,20},{20,16},{24,28},{28,24},{32,36},... | collective-permute-start | bytes 3145736 | tf_op jit(solution)/shard_map/ppermute | solution.py:391
  94.8 15.1 %collective-permute-start.11 = (bf16[256,1024]{1,0:T(8,128)(2,1)}, bf16[256,1024]{1,0:T(8,128)(2,1)}, u32[]{:S(2)}, u32[]{:S(2)}) collective-permute-start(bf16[256,1024]{1,0:T(8,128)(2,1)} %get-tuple-element.45), channel_id=1, source_target_pairs={{0,64},{64,128},{128,192},{192,0},{1,65},{65,129},{129,193},{193,1... | collective-permute-start | bytes 1572872 | tf_op jit(solution)/shard_map/ppermute | solution.py:335
  94.8 15.1 %collective-permute-start.12 = (bf16[256,1024]{1,0:T(8,128)(2,1)S(1)}, bf16[256,1024]{1,0:T(8,128)(2,1)}, u32[]{:S(2)}, u32[]{:S(2)}) collective-permute-start(bf16[256,1024]{1,0:T(8,128)(2,1)S(1)} %get-tuple-element.46), channel_id=1, source_target_pairs={{0,192},{64,0},{128,64},{192,128},{1,193},{65,1},{129,65},{193,129... | collective-permute-start | bytes 1572872 | tf_op jit(solution)/shard_map/ppermute | solution.py:335
  99.0 10.8 %copy-start.12 = (bf16[256,1024]{1,0:T(8,128)(2,1)S(1)}, bf16[256,1024]{1,0:T(8,128)(2,1)}, u32[]{:S(2)}) copy-start(bf16[256,1024]{1,0:T(8,128)(2,1)} %copy-done.11) | copy-start | bytes 1572868
  134.3 15.0 %all-to-all-start.3 = ((bf16[16,8,1024]{2,1,0:T(8,128)(2,1)}), bf16[16,8,1024]{2,1,0:T(8,128)(2,1)S(1)}, u32[]{:S(2)}, u32[]{:S(2)}) async-start(bf16[16,8,1024]{2,1,0:T(8,128)(2,1)} %bitcast.11), calls=%async_computation.3 | async-start | bytes 524288 | tf_op jit(solution)/shard_map/all_to_all | solution.py:405
Sparse Core Ops, SparseCore 0:
  9.8 48.7 all-gather.1
  99.2 41.1 reduce-scatter.1

commit v5 on v4

--- a/solution.py
+++ b/solution.py
@@ -20,7 +20,7 @@
 HIGHEST = lax.Precision.HIGHEST
 
 
-def call(kernel, out_shape, n_in, flops=0, bytes_accessed=0, scratch=(), in_specs=None):
+def call(kernel, out_shape, n_in, flops=0, bytes_accessed=0, scratch=(), in_specs=None, vmem=VMEM_LIMIT):
     out_specs = jax.tree.map(lambda _: pl.BlockSpec(memory_space=pltpu.VMEM), out_shape)
     return pl.pallas_call(
         kernel,
@@ -28,24 +28,37 @@
         in_specs=in_specs or [pl.BlockSpec(memory_space=pltpu.VMEM)] * n_in,
         out_specs=out_specs,
         scratch_shapes=list(scratch),
-        compiler_params=pltpu.CompilerParams(vmem_limit_bytes=VMEM_LIMIT),
+        compiler_params=pltpu.CompilerParams(vmem_limit_bytes=vmem),
         cost_estimate=pl.CostEstimate(
             flops=flops, bytes_accessed=bytes_accessed, transcendentals=0
         ),
     )
 
 
-def staged(kernel, out_shape, *args):
-    def whole(value):
-        return pl.BlockSpec(value.shape, lambda i: (0,) * len(value.shape))
-
-    return pl.pallas_call(
-        kernel,
-        grid=(1,),
-        out_shape=out_shape,
-        in_specs=[whole(value) for value in args],
-        out_specs=jax.tree.map(whole, out_shape),
-        compiler_params=pltpu.CompilerParams(vmem_limit_bytes=VMEM_LIMIT),
+def fetched(kernel, out_shape, *args):
+    count = len(args)
+
+    def body(*refs):
+        sources, results = refs[:count], refs[count : -count - 1]
+        held, sems = refs[-count - 1 : -1], refs[-1]
+        copies = [
+            pltpu.make_async_copy(source, place, sems.at[k])
+            for k, (source, place) in enumerate(zip(sources, held))
+        ]
+        for copy in copies:
+            copy.start()
+        for copy in copies:
+            copy.wait()
+        kernel(*held, *results)
+
+    return call(
+        body,
+        out_shape,
+        count,
+        scratch=[pltpu.VMEM(value.shape, value.dtype) for value in args]
+        + [pltpu.SemaphoreType.DMA((count,))],
+        in_specs=[pl.BlockSpec(memory_space=pl.ANY)] * count,
+        vmem=60 * 1024 * 1024,
     )(*args)
 
 
@@ -336,10 +349,10 @@
 
     turned = transposed(cotangent[0])
     cots = ring_gather(turned, along_tp)
-    dequant = staged(dequant_kernel, shape(out_weight.shape), out_weight, scale_exponent)
+    dequant = fetched(dequant_kernel, shape(out_weight.shape), out_weight, scale_exponent)
     weight = lax.all_gather(dequant, "ctx", axis=0, tiled=True)
 
-    packed, cum_rows, cum_columns = staged(
+    packed, cum_rows, cum_columns = fetched(
         state_kernel,
         [shape((STATE, columns + LANES)), shape((heads, length), f32), shape((length, LANES), f32)],
         x, w, log_decay[0],

time: 159 us -> 157 us (0.987)
  waiting for transfers between devices: 42.5 us -> 39.4 us
  local copies, waits for them, and re-layouts: 6.13 us -> 3.58 us
  starting transfers between devices: 48.1 us -> 50.4 us
  Pallas kernels: 25.2 us -> 27.3 us
    unnamed x28 -> x26, local copies, waits for them, and re-layouts: 6.06 us -> 3.5 us
    pallas_call x2, Pallas kernels: 2.69 us -> 4.75 us  [fetched(): call(body, out_shape, count, scratch=[pltpu.VMEM(value.shape, value.dtype...]
    ppermute x4, waiting for transfers between devices: 7.19 us -> 5.2 us  [along_tp(): return lax.ppermute(value, 'tp', [(i, (i + n) % tp) for i in range(tp)])]
  transfers between devices with their start and end apart: 19 -> 19, of which waited for: 7 -> 5; matrix products, arithmetic and copies ran while one was open for 0% -> 0% of each run, Pallas kernels for 16% -> 16%
where the time goes in v5:
time: 157 us
  starting transfers between devices  50.4 us (32%)
  waiting for transfers between devices  39.4 us (25%)
  Pallas kernels  27.3 us (17%)
  blocking collectives  21.6 us (14%)
  between operations  14.3 us (9%)
  local copies, waits for them, and re-layouts  3.58 us (2%)
    all_to_all x1, blocking collectives, per_device(): summary = lax.all_to_all(summary, 'ctx', 0, 0, tiled=True)  21.6 us
    ppermute x4, starting transfers between devices, along_tp(): return lax.ppermute(value, 'tp', [(i, (i + n) % tp) for i in range(tp)])  17.1 us
    ppermute x8, waiting for transfers between devices, along_dp(): return lax.ppermute(value, 'dp', [(i, (i + n) % dp) for i in range(dp)])  13.4 us
    all_to_all x1, waiting for transfers between devices, per_device(): packed = lax.all_to_all(packed, 'ctx', 0, 0, tiled=True)  12.1 us
    ppermute x8, starting transfers between devices, along_dp(): return lax.ppermute(value, 'dp', [(i, (i + n) % dp) for i in range(dp)])  11.3 us
    all_to_all x1, starting transfers between devices, per_device(): packed = lax.all_to_all(packed, 'ctx', 0, 0, tiled=True)  9.99 us
    all_to_all x1, waiting for transfers between devices, per_device(): leaving = lax.all_to_all(leaving, 'ctx', 0, 0, tiled=True)  8.56 us
    pallas_call x1, Pallas kernels, per_device(): call(weight_kernel, [shape((ctx // 2, rows, columns))] * 2, 8, flops=2000...  5.46 us
  transfers between devices with their start and end apart: 19, of which 5 were waited for; matrix products, arithmetic and copies ran while one was open for 0% of the time, Pallas kernels for 16%

profile of v5, /device:TPU:1, one launch (start us, length us, event | category | flops | bytes accessed | tf_op | source)
XLA Modules:
  0.0 156.6 jit_solution(174858830984737394)
XLA Ops:
  7.2 0.0 copy-start
  7.2 0.0 copy-start.5
  7.2 0.0 copy-start.7
  7.2 0.0 all-gather.2.cloned.1.call-start
  7.2 1.7 %shard_map.105 = bf16[64,1024]{1,0:T(8,128)(2,1)} custom-call(bf16[64,1024]{1,0:T(8,128)(2,1)} %refs_0_.1, s32[2,1024]{1,0:T(2,128)} %refs_1_.1), custom_call_target="tpu_custom_call" | custom-call | tf_op jit(solution)/shard_map/pallas_call | solution.py:54
  8.9 0.0 all-gather.2.cloned.1.call-update
  8.9 3.1 %shard_map.102 = (bf16[128,1152]{1,0:T(8,128)(2,1)}, f32[16,256]{1,0:T(8,128)}, f32[256,128]{1,0:T(8,128)}) custom-call(bf16[256,1024]{1,0:T(8,128)(2,1)} %bitcast.17, bf16[256,128]{1,0:T(8,128)(2,1)} %bitcast.24, f32[16,256]{1,0:T(8,128)} %bitcast.35), custom_call_target="tpu_custom_call" | custom-call | tf_op jit(solution)/shard_map/pallas_call | solution.py:54
  12.0 10.0 %all-to-all-start = ((bf16[16,8,1152]{2,1,0:T(8,128)(2,1)}), bf16[16,8,1152]{2,1,0:T(8,128)(2,1)S(1)}, u32[]{:S(2)}, u32[]{:S(2)}) async-start(bf16[16,8,1152]{2,1,0:T(8,128)(2,1)} %bitcast.34), calls=%async_computation | async-start | bytes 589824 | tf_op jit(solution)/shard_map/all_to_all | solution.py:360
  22.0 1.7 %collective-permute-start = (bf16[256,1024]{1,0:T(8,128)(2,1)}, bf16[256,1024]{1,0:T(8,128)(2,1)S(1)}, u32[]{:S(2)}, u32[]{:S(2)}) collective-permute-start(bf16[256,1024]{1,0:T(8,128)(2,1)} %bitcast.36), channel_id=1, source_target_pairs={{0,0},{1,64},{2,128},{3,192},{64,1},{65,65},{66,129},{67,193},{128... | collective-permute-start | bytes 1572872 | tf_op jit(solution)/shard_map/ppermute | solution.py:342
  23.7 12.1 %all-to-all-done = bf16[16,8,1152]{2,1,0:T(8,128)(2,1)S(1)} async-done(((bf16[16,8,1152]{2,1,0:T(8,128)(2,1)}), bf16[16,8,1152]{2,1,0:T(8,128)(2,1)S(1)}, u32[]{:S(2)}, u32[]{:S(2)}) %all-to-all-start) | async-done | bytes 294944 | tf_op jit(solution)/shard_map/all_to_all | solution.py:360
  35.9 1.0 shard_map.103
  36.9 3.4 %all-to-all-start.1 = ((bf16[16,8,1024]{2,1,0:T(8,128)(2,1)}), bf16[16,8,1024]{2,1,0:T(8,128)(2,1)S(1)}, u32[]{:S(2)}, u32[]{:S(2)}) async-start(bf16[16,8,1024]{2,1,0:T(8,128)(2,1)} %bitcast.7), calls=%async_computation.1 | async-start | bytes 524288 | tf_op jit(solution)/shard_map/all_to_all | solution.py:364
  40.3 0.0 reduce-scatter.2.cloned.1.call-start
  40.4 0.0 collective-permute-done.c0
  40.4 8.1 %collective-permute-start.1 = (bf16[256,1024]{1,0:T(8,128)(2,1)S(1)}, bf16[256,1024]{1,0:T(8,128)(2,1)S(1)}, u32[]{:S(2)}, u32[]{:S(2)}) collective-permute-start(bf16[256,1024]{1,0:T(8,128)(2,1)S(1)} %collective-permute-done.c0), channel_id=1, source_target_pairs={{0,1},{1,2},{2,3},{3,0},{4,5},{5,6},{6,7},{7,4},{8,9},{9,10},{10,1... | collective-permute-start | bytes 1572872 | tf_op jit(solution)/shard_map/ppermute | solution.py:345
  48.5 6.1 %collective-permute-start.2 = (bf16[256,1024]{1,0:T(8,128)(2,1)S(1)}, bf16[256,1024]{1,0:T(8,128)(2,1)S(1)}, u32[]{:S(2)}, u32[]{:S(2)}) collective-permute-start(bf16[256,1024]{1,0:T(8,128)(2,1)S(1)} %collective-permute-done.c0), channel_id=1, source_target_pairs={{0,3},{1,0},{2,1},{3,2},{4,7},{5,4},{6,5},{7,6},{8,11},{9,8},{10,9... | collective-permute-start | bytes 1572872 | tf_op jit(solution)/shard_map/ppermute | solution.py:345
  54.7 0.0 all-to-all-done.1
  54.7 0.0 copy-done
  54.7 0.9 copy-done.1
  55.6 0.7 copy-done.8
  56.3 1.4 shard_map.104.m0
  57.8 0.0 all-gather.2.cloned.1.call-done.weight_ref
  57.8 1.3 collective-permute-start.5
  59.0 1.8 %collective-permute-start.6 = (bf16[256,1024]{1,0:T(8,128)(2,1)S(1)}, bf16[256,1024]{1,0:T(8,128)(2,1)S(1)}, u32[]{:S(2)}, u32[]{:S(2)}) collective-permute-start(bf16[256,1024]{1,0:T(8,128)(2,1)S(1)} %shard_map.104.m0), channel_id=1, source_target_pairs={{0,192},{64,0},{128,64},{192,128},{1,193},{65,1},{129,65},{193,129... | collective-permute-start | bytes 1572872 | tf_op jit(solution)/shard_map/ppermute | solution.py:348
  60.9 5.2 %collective-permute-done.1.c1 = bf16[256,1024]{1,0:T(8,128)(2,1)S(1)} collective-permute-done((bf16[256,1024]{1,0:T(8,128)(2,1)S(1)}, bf16[256,1024]{1,0:T(8,128)(2,1)S(1)}, u32[]{:S(2)}, u32[]{:S(2)}) %collective-permute-start.1) | collective-permute-done | bytes 524320 | tf_op jit(solution)/shard_map/ppermute | solution.py:345
  66.1 0.1 collective-permute-start.3
  66.2 0.0 collective-permute-done.2.c2
  66.2 0.0 copy-start.3
  66.2 2.7 %collective-permute-start.4 = (bf16[128,1024]{1,0:T(8,128)(2,1)S(1)}, bf16[128,1024]{1,0:T(8,128)(2,1)S(1)}, u32[]{:S(2)}, u32[]{:S(2)}) collective-permute-start(bf16[128,1024]{1,0:T(8,128)(2,1)S(1)} %slice.17), channel_id=1, source_target_pairs={{0,3},{1,0},{2,1},{3,2},{4,7},{5,4},{6,5},{7,6},{8,11},{9,8},{10,9... | collective-permute-start | bytes 786440 | tf_op jit(solution)/shard_map/ppermute | solution.py:345
  69.0 2.6 %collective-permute-done.5.m1 = bf16[256,1024]{1,0:T(8,128)(2,1)S(1)} collective-permute-done((bf16[256,1024]{1,0:T(8,128)(2,1)S(1)}, bf16[256,1024]{1,0:T(8,128)(2,1)S(1)}, u32[]{:S(2)}, u32[]{:S(2)}) %collective-permute-start.5) | collective-permute-done | bytes 524320 | tf_op jit(solution)/shard_map/ppermute | solution.py:348
  71.6 0.8 collective-permute-start.7
  72.4 0.0 collective-permute-done.6.m2
  72.4 2.0 %collective-permute-start.8 = (bf16[128,1024]{1,0:T(8,128)(2,1)S(1)}, bf16[128,1024]{1,0:T(8,128)(2,1)S(1)}, u32[]{:S(2)}, u32[]{:S(2)}) collective-permute-start(bf16[128,1024]{1,0:T(8,128)(2,1)S(1)} %slice.19), channel_id=1, source_target_pairs={{0,192},{64,0},{128,64},{192,128},{1,193},{65,1},{129,65},{193,129... | collective-permute-start | bytes 786440 | tf_op jit(solution)/shard_map/ppermute | solution.py:348
  74.5 0.0 collective-permute-done.3.c3
  74.5 0.0 collective-permute-done.4.c4
  74.5 5.1 %shard_map.106 = (bf16[256,1024]{1,0:T(8,128)(2,1)S(1)}, bf16[256,1024]{1,0:T(8,128)(2,1)S(1)}, bf16[256,1024]{1,0:T(8,128)(2,1)S(1)}, bf16[128,1024]{1,0:T(8,128)(2,1)S(1)}, bf16[128,1024]{1,0:T(8,128)(2,1)S(1)}) custom-call(bf16[256,1024]{1,0:T(8,128)(2,1)S(1)} %collective-permute-done.c0, bf16[256,1024]{1,0:T(8,128)(2,1)S(1)} %collective-permute-done.1.c1, ...), custom_call_target="tpu_custom_call" | custom-call | tf_op jit(solution)/shard_map/pallas_call | solution.py:375
  79.6 0.0 copy-done.12
  79.6 0.0 copy-start.10
  79.6 0.8 copy-done.10
  80.4 0.0 collective-permute-start.9
  80.4 2.7 %collective-permute-start.10 = (bf16[128,1024]{1,0:T(8,128)(2,1)S(1)}, bf16[128,1024]{1,0:T(8,128)(2,1)S(1)}, u32[]{:S(2)}, u32[]{:S(2)}) collective-permute-start(bf16[128,1024]{1,0:T(8,128)(2,1)S(1)} %get-tuple-element.42), channel_id=1, source_target_pairs={{0,192},{64,0},{128,64},{192,128},{1,193},{65,1},{129,65},{193,129... | collective-permute-start | bytes 786440 | tf_op jit(solution)/shard_map/ppermute | solution.py:348
  83.1 0.0 collective-permute-done.7.m3
  83.1 0.0 collective-permute-done.8.m4
  83.1 1.0 copy-done.4
  84.1 5.5 %shard_map.112 = (bf16[8,64,1024]{2,1,0:T(8,128)(2,1)}, bf16[8,64,1024]{2,1,0:T(8,128)(2,1)}) custom-call(bf16[256,1024]{1,0:T(8,128)(2,1)S(1)} %collective-permute-done.c0, bf16[256,1024]{1,0:T(8,128)(2,1)S(1)} %collective-permute-done.1.c1, bf16[256,1024]{1,0:T(8,128)(2,1)S(1)} %copy-done.4, bf16[128,1024]{1,0:T(8,128)(2,1)S(1)} %collective-permute-done.3.c3, ...), custom_call_target="tpu_custom_call" | custom-call | flops 20000000000 | tf_op jit(solution)/shard_map/pallas_call | solution.py:390
  89.6 3.2 %collective-permute-start.13 = (bf16[8,64,1024]{2,1,0:T(8,128)(2,1)}, bf16[8,64,1024]{2,1,0:T(8,128)(2,1)S(1)}, u32[]{:S(2)}, u32[]{:S(2)}) collective-permute-start(bf16[8,64,1024]{2,1,0:T(8,128)(2,1)} %get-tuple-element.61), channel_id=1, source_target_pairs={{0,4},{4,0},{8,12},{12,8},{16,20},{20,16},{24,28},{28,24},{32,36},... | collective-permute-start | bytes 3145736 | tf_op jit(solution)/shard_map/ppermute | solution.py:404
  92.8 0.0 collective-permute-done.9.top
  92.8 0.0 collective-permute-done.10.bottom
  92.8 0.9 shard_map.107
  93.7 0.0 collective-permute-start.11
  93.7 2.7 %collective-permute-start.12 = (bf16[256,1024]{1,0:T(8,128)(2,1)S(1)}, bf16[256,1024]{1,0:T(8,128)(2,1)}, u32[]{:S(2)}, u32[]{:S(2)}) collective-permute-start(bf16[256,1024]{1,0:T(8,128)(2,1)S(1)} %get-tuple-element.46), channel_id=1, source_target_pairs={{0,192},{64,0},{128,64},{192,128},{1,193},{65,1},{129,65},{193,129... | collective-permute-start | bytes 1572872 | tf_op jit(solution)/shard_map/ppermute | solution.py:348
  96.4 0.0 collective-permute-done.13.other_ref
  96.4 1.6 shard_map.113
  97.9 0.0 reduce-scatter.2.cloned.1.call-update
  98.0 0.0 copy-start.9
  98.0 10.8 %collective-permute-done.11.g1 = bf16[256,1024]{1,0:T(8,128)(2,1)} collective-permute-done((bf16[256,1024]{1,0:T(8,128)(2,1)}, bf16[256,1024]{1,0:T(8,128)(2,1)}, u32[]{:S(2)}, u32[]{:S(2)}) %collective-permute-start.11) | collective-permute-done | bytes 524320 | tf_op jit(solution)/shard_map/ppermute | solution.py:348
  108.7 0.0 collective-permute-done.12.g2
  108.7 2.1 %shard_map.108 = (bf16[256,1024]{1,0:T(8,128)(2,1)S(1)}, bf16[128,1024]{1,0:T(8,128)(2,1)S(1)}) custom-call(bf16[256,1024]{1,0:T(8,128)(2,1)S(1)} %copy-done.11, bf16[256,1024]{1,0:T(8,128)(2,1)} %collective-permute-done.11.g1, bf16[256,1024]{1,0:T(8,128)(2,1)} %collective-permute-done.12.g2, bf16[256,128]{1,0:T(8,128)(2,1)S(1)} %bitcast.31, ...), custom_call_target="tpu_custom_call" | custom-call | flops 49999998976 | tf_op jit(solution)/shard_map/pallas_call | solution.py:408
  110.9 21.6 %all_to_all.44 = bf16[16,8,1024]{2,1,0:T(8,128)(2,1)S(1)} all-to-all(bf16[16,8,1024]{2,1,0:T(8,128)(2,1)S(1)} %bitcast.33), channel_id=1, replica_groups=mesh['dp'=4,'ctx'=16,'tp'=4] {'ctx'}, dimensions={0} | all-to-all | bytes 524288 | tf_op jit(solution)/shard_map/all_to_all | solution.py:416
  132.5 0.8 shard_map.109
  133.3 3.7 %all-to-all-start.3 = ((bf16[16,8,1024]{2,1,0:T(8,128)(2,1)}), bf16[16,8,1024]{2,1,0:T(8,128)(2,1)S(1)}, u32[]{:S(2)}, u32[]{:S(2)}) async-start(bf16[16,8,1024]{2,1,0:T(8,128)(2,1)} %bitcast.11), calls=%async_computation.3 | async-start | bytes 524288 | tf_op jit(solution)/shard_map/all_to_all | solution.py:418
  137.0 2.7 %shard_map.110 = (f32[256,1024]{1,0:T(8,128)S(1)}, f32[256,128]{1,0:T(8,128)S(1)}, bf16[256,128]{1,0:T(8,128)(2,1)}) custom-call(bf16[256,1024]{1,0:T(8,128)(2,1)S(1)} %bitcast.19, bf16[256,128]{1,0:T(8,128)(2,1)S(1)} %bitcast.26, bf16[256,128]{1,0:T(8,128)(2,1)S(1)} %bitcast.32, bf16[256,1024]{1,0:T(8,128)(2,1)S(1)} %get-tuple-element.49.g_ref, ...), custom_call_target="tpu_custom_call" | custom-call | tf_op jit(solution)/shard_map/pallas_call | solution.py:419
  139.6 8.6 %all-to-all-done.3 = bf16[16,8,1024]{2,1,0:T(8,128)(2,1)S(1)} async-done(((bf16[16,8,1024]{2,1,0:T(8,128)(2,1)}), bf16[16,8,1024]{2,1,0:T(8,128)(2,1)S(1)}, u32[]{:S(2)}, u32[]{:S(2)}) %all-to-all-start.3) | async-done | bytes 262176 | tf_op jit(solution)/shard_map/all_to_all | solution.py:418
  148.2 1.5 shard_map.111
  (19 shorter events, 0.1 us)
Async XLA Ops:
  7.2 47.5 %copy-start = (bf16[1,256,1024]{2,1,0:T(8,128)(2,1)S(1)}, bf16[1,256,1024]{2,1,0:T(8,128)(2,1)}, u32[]{:S(2)}) copy-start(bf16[1,256,1024]{2,1,0:T(8,128)(2,1)} %param.7) | copy-start | bytes 1572868
  7.2 47.5 %copy-start.5 = (bf16[1,256,128]{2,1,0:T(8,128)(2,1)S(1)}, bf16[1,256,128]{2,1,0:T(8,128)(2,1)}, u32[]{:S(2)}) copy-start(bf16[1,256,128]{2,1,0:T(8,128)(2,1)} %param.8) | copy-start | bytes 196612
  7.2 47.5 %copy-start.7 = (bf16[1,256,128]{2,1,0:T(8,128)(2,1)S(1)}, bf16[1,256,128]{2,1,0:T(8,128)(2,1)}, u32[]{:S(2)}) copy-start(bf16[1,256,128]{2,1,0:T(8,128)(2,1)} %param.9) | copy-start | bytes 196612
  7.2 50.6 %all-gather.2.cloned.1.call-start = ((), (), s32[]{:S(2)}) async-start(), calls=%async_computation.5 | async-start | bytes 2228224 | tf_op jit(solution)/shard_map/all_gather | solution.py:353
  12.0 23.8 %all-to-all-start = ((bf16[16,8,1152]{2,1,0:T(8,128)(2,1)}), bf16[16,8,1152]{2,1,0:T(8,128)(2,1)S(1)}, u32[]{:S(2)}, u32[]{:S(2)}) async-start(bf16[16,8,1152]{2,1,0:T(8,128)(2,1)} %bitcast.34), calls=%async_computation | async-start | bytes 589824 | tf_op jit(solution)/shard_map/all_to_all | solution.py:360
  22.0 18.4 %collective-permute-start = (bf16[256,1024]{1,0:T(8,128)(2,1)}, bf16[256,1024]{1,0:T(8,128)(2,1)S(1)}, u32[]{:S(2)}, u32[]{:S(2)}) collective-permute-start(bf16[256,1024]{1,0:T(8,128)(2,1)} %bitcast.36), channel_id=1, source_target_pairs={{0,0},{1,64},{2,128},{3,192},{64,1},{65,65},{66,129},{67,193},{128... | collective-permute-start | bytes 1572872 | tf_op jit(solution)/shard_map/ppermute | solution.py:342
  36.9 17.8 %all-to-all-start.1 = ((bf16[16,8,1024]{2,1,0:T(8,128)(2,1)}), bf16[16,8,1024]{2,1,0:T(8,128)(2,1)S(1)}, u32[]{:S(2)}, u32[]{:S(2)}) async-start(bf16[16,8,1024]{2,1,0:T(8,128)(2,1)} %bitcast.7), calls=%async_computation.1 | async-start | bytes 524288 | tf_op jit(solution)/shard_map/all_to_all | solution.py:364
  40.3 109.4 %reduce-scatter.2.cloned.1.call-start = ((), (), s32[]{:S(2)}) async-start(), calls=%async_computation.6 | async-start | bytes 2359296 | tf_op jit(solution)/shard_map/reduce_scatter | solution.py:407
  40.4 25.7 %collective-permute-start.1 = (bf16[256,1024]{1,0:T(8,128)(2,1)S(1)}, bf16[256,1024]{1,0:T(8,128)(2,1)S(1)}, u32[]{:S(2)}, u32[]{:S(2)}) collective-permute-start(bf16[256,1024]{1,0:T(8,128)(2,1)S(1)} %collective-permute-done.c0), channel_id=1, source_target_pairs={{0,1},{1,2},{2,3},{3,0},{4,5},{5,6},{6,7},{7,4},{8,9},{9,10},{10,1... | collective-permute-start | bytes 1572872 | tf_op jit(solution)/shard_map/ppermute | solution.py:345
  48.5 17.7 %collective-permute-start.2 = (bf16[256,1024]{1,0:T(8,128)(2,1)S(1)}, bf16[256,1024]{1,0:T(8,128)(2,1)S(1)}, u32[]{:S(2)}, u32[]{:S(2)}) collective-permute-start(bf16[256,1024]{1,0:T(8,128)(2,1)S(1)} %collective-permute-done.c0), channel_id=1, source_target_pairs={{0,3},{1,0},{2,1},{3,2},{4,7},{5,4},{6,5},{7,6},{8,11},{9,8},{10,9... | collective-permute-start | bytes 1572872 | tf_op jit(solution)/shard_map/ppermute | solution.py:345
  54.7 0.9 copy-start.1
  55.6 0.7 copy-start.8
  57.8 13.8 %collective-permute-start.5 = (bf16[256,1024]{1,0:T(8,128)(2,1)S(1)}, bf16[256,1024]{1,0:T(8,128)(2,1)S(1)}, u32[]{:S(2)}, u32[]{:S(2)}) collective-permute-start(bf16[256,1024]{1,0:T(8,128)(2,1)S(1)} %shard_map.104.m0), channel_id=1, source_target_pairs={{0,64},{64,128},{128,192},{192,0},{1,65},{65,129},{129,193},{193,1... | collective-permute-start | bytes 1572872 | tf_op jit(solution)/shard_map/ppermute | solution.py:348
  59.0 13.4 %collective-permute-start.6 = (bf16[256,1024]{1,0:T(8,128)(2,1)S(1)}, bf16[256,1024]{1,0:T(8,128)(2,1)S(1)}, u32[]{:S(2)}, u32[]{:S(2)}) collective-permute-start(bf16[256,1024]{1,0:T(8,128)(2,1)S(1)} %shard_map.104.m0), channel_id=1, source_target_pairs={{0,192},{64,0},{128,64},{192,128},{1,193},{65,1},{129,65},{193,129... | collective-permute-start | bytes 1572872 | tf_op jit(solution)/shard_map/ppermute | solution.py:348
  66.1 8.4 %collective-permute-start.3 = (bf16[128,1024]{1,0:T(8,128)(2,1)S(1)}, bf16[128,1024]{1,0:T(8,128)(2,1)S(1)}, u32[]{:S(2)}, u32[]{:S(2)}) collective-permute-start(bf16[128,1024]{1,0:T(8,128)(2,1)S(1)} %slice.16), channel_id=1, source_target_pairs={{0,1},{1,2},{2,3},{3,0},{4,5},{5,6},{6,7},{7,4},{8,9},{9,10},{10,1... | collective-permute-start | bytes 786440 | tf_op jit(solution)/shard_map/ppermute | solution.py:345
  66.2 8.3 %copy-start.3 = (bf16[256,1024]{1,0:T(8,128)(2,1)}, bf16[256,1024]{1,0:T(8,128)(2,1)S(1)}, u32[]{:S(2)}) copy-start(bf16[256,1024]{1,0:T(8,128)(2,1)S(1)} %collective-permute-done.2.c2) | copy-start | bytes 1572868
  66.2 8.3 %collective-permute-start.4 = (bf16[128,1024]{1,0:T(8,128)(2,1)S(1)}, bf16[128,1024]{1,0:T(8,128)(2,1)S(1)}, u32[]{:S(2)}, u32[]{:S(2)}) collective-permute-start(bf16[128,1024]{1,0:T(8,128)(2,1)S(1)} %slice.17), channel_id=1, source_target_pairs={{0,3},{1,0},{2,1},{3,2},{4,7},{5,4},{6,5},{7,6},{8,11},{9,8},{10,9... | collective-permute-start | bytes 786440 | tf_op jit(solution)/shard_map/ppermute | solution.py:345
  71.6 11.5 %collective-permute-start.7 = (bf16[128,1024]{1,0:T(8,128)(2,1)S(1)}, bf16[128,1024]{1,0:T(8,128)(2,1)S(1)}, u32[]{:S(2)}, u32[]{:S(2)}) collective-permute-start(bf16[128,1024]{1,0:T(8,128)(2,1)S(1)} %slice.18), channel_id=1, source_target_pairs={{0,64},{64,128},{128,192},{192,0},{1,65},{65,129},{129,193},{193,1... | collective-permute-start | bytes 786440 | tf_op jit(solution)/shard_map/ppermute | solution.py:348
  72.4 7.2 %copy-start.12 = (bf16[256,1024]{1,0:T(8,128)(2,1)}, bf16[256,1024]{1,0:T(8,128)(2,1)S(1)}, u32[]{:S(2)}) copy-start(bf16[256,1024]{1,0:T(8,128)(2,1)S(1)} %collective-permute-done.6.m2) | copy-start | bytes 1572868
  72.4 10.7 %collective-permute-start.8 = (bf16[128,1024]{1,0:T(8,128)(2,1)S(1)}, bf16[128,1024]{1,0:T(8,128)(2,1)S(1)}, u32[]{:S(2)}, u32[]{:S(2)}) collective-permute-start(bf16[128,1024]{1,0:T(8,128)(2,1)S(1)} %slice.19), channel_id=1, source_target_pairs={{0,192},{64,0},{128,64},{192,128},{1,193},{65,1},{129,65},{193,129... | collective-permute-start | bytes 786440 | tf_op jit(solution)/shard_map/ppermute | solution.py:348
  79.6 0.8 copy-start.10
  80.4 12.4 %collective-permute-start.9 = (bf16[128,1024]{1,0:T(8,128)(2,1)S(1)}, bf16[128,1024]{1,0:T(8,128)(2,1)S(1)}, u32[]{:S(2)}, u32[]{:S(2)}) collective-permute-start(bf16[128,1024]{1,0:T(8,128)(2,1)S(1)} %get-tuple-element.41), channel_id=1, source_target_pairs={{0,64},{64,128},{128,192},{192,0},{1,65},{65,129},{129,193},{193,1... | collective-permute-start | bytes 786440 | tf_op jit(solution)/shard_map/ppermute | solution.py:348
  80.4 12.4 %collective-permute-start.10 = (bf16[128,1024]{1,0:T(8,128)(2,1)S(1)}, bf16[128,1024]{1,0:T(8,128)(2,1)S(1)}, u32[]{:S(2)}, u32[]{:S(2)}) collective-permute-start(bf16[128,1024]{1,0:T(8,128)(2,1)S(1)} %get-tuple-element.42), channel_id=1, source_target_pairs={{0,192},{64,0},{128,64},{192,128},{1,193},{65,1},{129,65},{193,129... | collective-permute-start | bytes 786440 | tf_op jit(solution)/shard_map/ppermute | solution.py:348
  83.1 1.0 copy-start.4
  89.6 6.7 %copy-start.6 = (bf16[8,64,1024]{2,1,0:T(8,128)(2,1)S(1)}, bf16[8,64,1024]{2,1,0:T(8,128)(2,1)}, u32[]{:S(2)}) copy-start(bf16[8,64,1024]{2,1,0:T(8,128)(2,1)} %get-tuple-element.60.mine_ref) | copy-start | bytes 3145732
  89.6 6.7 %collective-permute-start.13 = (bf16[8,64,1024]{2,1,0:T(8,128)(2,1)}, bf16[8,64,1024]{2,1,0:T(8,128)(2,1)S(1)}, u32[]{:S(2)}, u32[]{:S(2)}) collective-permute-start(bf16[8,64,1024]{2,1,0:T(8,128)(2,1)} %get-tuple-element.61), channel_id=1, source_target_pairs={{0,4},{4,0},{8,12},{12,8},{16,20},{20,16},{24,28},{28,24},{32,36},... | collective-permute-start | bytes 3145736 | tf_op jit(solution)/shard_map/ppermute | solution.py:404
  93.7 15.1 %collective-permute-start.11 = (bf16[256,1024]{1,0:T(8,128)(2,1)}, bf16[256,1024]{1,0:T(8,128)(2,1)}, u32[]{:S(2)}, u32[]{:S(2)}) collective-permute-start(bf16[256,1024]{1,0:T(8,128)(2,1)} %get-tuple-element.45), channel_id=1, source_target_pairs={{0,64},{64,128},{128,192},{192,0},{1,65},{65,129},{129,193},{193,1... | collective-permute-start | bytes 1572872 | tf_op jit(solution)/shard_map/ppermute | solution.py:348
  93.7 15.1 %collective-permute-start.12 = (bf16[256,1024]{1,0:T(8,128)(2,1)S(1)}, bf16[256,1024]{1,0:T(8,128)(2,1)}, u32[]{:S(2)}, u32[]{:S(2)}) collective-permute-start(bf16[256,1024]{1,0:T(8,128)(2,1)S(1)} %get-tuple-element.46), channel_id=1, source_target_pairs={{0,192},{64,0},{128,64},{192,128},{1,193},{65,1},{129,65},{193,129... | collective-permute-start | bytes 1572872 | tf_op jit(solution)/shard_map/ppermute | solution.py:348
  97.9 10.8 %copy-start.2 = (f32[256,128]{1,0:T(8,128)S(1)}, f32[256,128]{1,0:T(8,128)}, u32[]{:S(2)}) copy-start(f32[256,128]{1,0:T(8,128)} %get-tuple-element.33.columns_ref) | copy-start | bytes 393220
  97.9 10.8 %copy-start.11 = (bf16[256,1024]{1,0:T(8,128)(2,1)S(1)}, bf16[256,1024]{1,0:T(8,128)(2,1)}, u32[]{:S(2)}) copy-start(bf16[256,1024]{1,0:T(8,128)(2,1)} %copy-done.10) | copy-start | bytes 1572868
  98.0 39.0 %copy-start.9 = (f32[16,256]{1,0:T(8,128)S(1)}, f32[16,256]{1,0:T(8,128)}, u32[]{:S(2)}) copy-start(f32[16,256]{1,0:T(8,128)} %get-tuple-element.34.rows_ref) | copy-start | bytes 49156
  133.3 14.9 %all-to-all-start.3 = ((bf16[16,8,1024]{2,1,0:T(8,128)(2,1)}), bf16[16,8,1024]{2,1,0:T(8,128)(2,1)S(1)}, u32[]{:S(2)}, u32[]{:S(2)}) async-start(bf16[16,8,1024]{2,1,0:T(8,128)(2,1)} %bitcast.11), calls=%async_computation.3 | async-start | bytes 524288 | tf_op jit(solution)/shard_map/all_to_all | solution.py:418
Sparse Core Ops, SparseCore 0:
  9.9 47.8 all-gather.1
  98.1 39.6 reduce-scatter.1

commit v6 on v5

--- a/solution.py
+++ b/solution.py
@@ -359,7 +359,10 @@
     )
     packed = lax.all_to_all(packed, "ctx", 0, 0, tiled=True)
     entering, decays = call(
-        forward_scan_kernel, [shape((STATE, columns)), shape((ctx, columns), f32)], 1
+        forward_scan_kernel,
+        [shape((STATE, columns)), shape((ctx, columns), f32)],
+        1,
+        flops=5_000_000_000,
     )(packed)
     entering = lax.all_to_all(entering, "ctx", 0, 0, tiled=True)
 

time: 157 us -> 156 us (level)
  waiting for transfers between devices: 39.4 us -> 42.5 us
  starting transfers between devices: 50.4 us -> 48.7 us
  local copies, waits for them, and re-layouts: 3.58 us -> 1.95 us
    unnamed x26 -> x22, local copies, waits for them, and re-layouts: 3.5 us -> 1.87 us
  transfers between devices with their start and end apart: 19 -> 19, of which waited for: 5 -> 6; matrix products, arithmetic and copies ran while one was open for 0% -> 0% of each run, Pallas kernels for 16% -> 17%
where the time goes in v6:
time: 156 us; the launch traced here: 155 us
  starting transfers between devices  48.7 us (31%)
  waiting for transfers between devices  42.5 us (27%)
  Pallas kernels  27.3 us (18%)
  blocking collectives  20.8 us (13%)
  between operations  14.3 us (9%)
  local copies, waits for them, and re-layouts  1.95 us (1%)
    all_to_all x1, blocking collectives, per_device(): summary = lax.all_to_all(summary, 'ctx', 0, 0, tiled=True)  20.8 us
    ppermute x4, starting transfers between devices, along_tp(): return lax.ppermute(value, 'tp', [(i, (i + n) % tp) for i in range(tp)])  17.1 us
    ppermute x8, waiting for transfers between devices, along_dp(): return lax.ppermute(value, 'dp', [(i, (i + n) % dp) for i in range(dp)])  14.3 us
    all_to_all x1, waiting for transfers between devices, per_device(): packed = lax.all_to_all(packed, 'ctx', 0, 0, tiled=True)  12.1 us
    ppermute x8, starting transfers between devices, along_dp(): return lax.ppermute(value, 'dp', [(i, (i + n) % dp) for i in range(dp)])  11 us
    all_to_all x1, starting transfers between devices, per_device(): packed = lax.all_to_all(packed, 'ctx', 0, 0, tiled=True)  9.99 us
    all_to_all x1, waiting for transfers between devices, per_device(): leaving = lax.all_to_all(leaving, 'ctx', 0, 0, tiled=True)  8.92 us
    ppermute x4, waiting for transfers between devices, along_tp(): return lax.ppermute(value, 'tp', [(i, (i + n) % tp) for i in range(tp)])  5.54 us
  transfers between devices with their start and end apart: 19, of which 6 were waited for; matrix products, arithmetic and copies ran while one was open for 0% of the time, Pallas kernels for 17%

profile of v6, /device:TPU:1, one launch (start us, length us, event | category | flops | bytes accessed | tf_op | source)
XLA Modules:
  0.0 155.5 jit_solution(9734883320155447357)
XLA Ops:
  7.2 0.0 all-gather.2.cloned.1.call-start
  7.2 1.6 %shard_map.105 = bf16[64,1024]{1,0:T(8,128)(2,1)} custom-call(bf16[64,1024]{1,0:T(8,128)(2,1)} %refs_0_.1, s32[2,1024]{1,0:T(2,128)} %refs_1_.1), custom_call_target="tpu_custom_call" | custom-call | tf_op jit(solution)/shard_map/pallas_call | solution.py:54
  8.8 0.0 all-gather.2.cloned.1.call-update
  8.8 3.1 %shard_map.102 = (bf16[128,1152]{1,0:T(8,128)(2,1)}, f32[16,256]{1,0:T(8,128)}, f32[256,128]{1,0:T(8,128)}) custom-call(bf16[256,1024]{1,0:T(8,128)(2,1)} %bitcast.17, bf16[256,128]{1,0:T(8,128)(2,1)} %bitcast.23, f32[16,256]{1,0:T(8,128)} %bitcast.35), custom_call_target="tpu_custom_call" | custom-call | tf_op jit(solution)/shard_map/pallas_call | solution.py:54
  12.0 10.0 %all-to-all-start = ((bf16[16,8,1152]{2,1,0:T(8,128)(2,1)}), bf16[16,8,1152]{2,1,0:T(8,128)(2,1)S(1)}, u32[]{:S(2)}, u32[]{:S(2)}) async-start(bf16[16,8,1152]{2,1,0:T(8,128)(2,1)} %bitcast.34), calls=%async_computation | async-start | bytes 589824 | tf_op jit(solution)/shard_map/all_to_all | solution.py:360
  21.9 1.7 %collective-permute-start = (bf16[256,1024]{1,0:T(8,128)(2,1)}, bf16[256,1024]{1,0:T(8,128)(2,1)S(1)}, u32[]{:S(2)}, u32[]{:S(2)}) collective-permute-start(bf16[256,1024]{1,0:T(8,128)(2,1)} %bitcast.36), channel_id=1, source_target_pairs={{0,0},{1,64},{2,128},{3,192},{64,1},{65,65},{66,129},{67,193},{128... | collective-permute-start | bytes 1572872 | tf_op jit(solution)/shard_map/ppermute | solution.py:342
  23.6 12.1 %all-to-all-done = bf16[16,8,1152]{2,1,0:T(8,128)(2,1)S(1)} async-done(((bf16[16,8,1152]{2,1,0:T(8,128)(2,1)}), bf16[16,8,1152]{2,1,0:T(8,128)(2,1)S(1)}, u32[]{:S(2)}, u32[]{:S(2)}) %all-to-all-start) | async-done | bytes 294944 | tf_op jit(solution)/shard_map/all_to_all | solution.py:360
  35.8 0.0 copy-start.7
  35.8 1.0 shard_map.103
  36.8 3.5 %all-to-all-start.1 = ((bf16[16,8,1024]{2,1,0:T(8,128)(2,1)}), bf16[16,8,1024]{2,1,0:T(8,128)(2,1)S(1)}, u32[]{:S(2)}, u32[]{:S(2)}) async-start(bf16[16,8,1024]{2,1,0:T(8,128)(2,1)} %bitcast.7), calls=%async_computation.1 | async-start | bytes 524288 | tf_op jit(solution)/shard_map/all_to_all | solution.py:367
  40.3 0.0 reduce-scatter.2.cloned.1.call-start
  40.3 0.0 collective-permute-done.c0
  40.3 8.1 %collective-permute-start.1 = (bf16[256,1024]{1,0:T(8,128)(2,1)S(1)}, bf16[256,1024]{1,0:T(8,128)(2,1)S(1)}, u32[]{:S(2)}, u32[]{:S(2)}) collective-permute-start(bf16[256,1024]{1,0:T(8,128)(2,1)S(1)} %collective-permute-done.c0), channel_id=1, source_target_pairs={{0,1},{1,2},{2,3},{3,0},{4,5},{5,6},{6,7},{7,4},{8,9},{9,10},{10,1... | collective-permute-start | bytes 1572872 | tf_op jit(solution)/shard_map/ppermute | solution.py:345
  48.4 6.1 %collective-permute-start.2 = (bf16[256,1024]{1,0:T(8,128)(2,1)S(1)}, bf16[256,1024]{1,0:T(8,128)(2,1)S(1)}, u32[]{:S(2)}, u32[]{:S(2)}) collective-permute-start(bf16[256,1024]{1,0:T(8,128)(2,1)S(1)} %collective-permute-done.c0), channel_id=1, source_target_pairs={{0,3},{1,0},{2,1},{3,2},{4,7},{5,4},{6,5},{7,6},{8,11},{9,8},{10,9... | collective-permute-start | bytes 1572872 | tf_op jit(solution)/shard_map/ppermute | solution.py:345
  54.6 0.0 all-to-all-done.1
  54.6 0.0 copy-done
  54.6 0.0 copy-done.1
  54.6 0.0 copy-done.4
  54.6 0.0 copy-done.6
  54.6 0.0 copy-done.7
  54.6 1.4 shard_map.104.m0
  56.1 1.6 %all-gather.2.cloned.1.call-done.weight_ref = bf16[1024,1024]{1,0:T(8,128)(2,1)} async-done(((bf16[64,1024]{1,0:T(8,128)(2,1)}), bf16[1024,1024]{1,0:T(8,128)(2,1)}) %all-gather.2.cloned.1.call-update) | async-done | bytes 2097168 | tf_op jit(solution)/shard_map/all_gather | solution.py:353
  57.6 1.3 collective-permute-start.5
  59.0 1.5 collective-permute-start.6
  60.5 5.5 %collective-permute-done.1.c1 = bf16[256,1024]{1,0:T(8,128)(2,1)S(1)} collective-permute-done((bf16[256,1024]{1,0:T(8,128)(2,1)S(1)}, bf16[256,1024]{1,0:T(8,128)(2,1)S(1)}, u32[]{:S(2)}, u32[]{:S(2)}) %collective-permute-start.1) | collective-permute-done | bytes 524320 | tf_op jit(solution)/shard_map/ppermute | solution.py:345
  66.0 0.1 collective-permute-start.3
  66.1 0.0 collective-permute-done.2.c2
  66.1 0.0 copy-start.2
  66.2 2.7 %collective-permute-start.4 = (bf16[128,1024]{1,0:T(8,128)(2,1)S(1)}, bf16[128,1024]{1,0:T(8,128)(2,1)S(1)}, u32[]{:S(2)}, u32[]{:S(2)}) collective-permute-start(bf16[128,1024]{1,0:T(8,128)(2,1)S(1)} %slice.17), channel_id=1, source_target_pairs={{0,3},{1,0},{2,1},{3,2},{4,7},{5,4},{6,5},{7,6},{8,11},{9,8},{10,9... | collective-permute-start | bytes 786440 | tf_op jit(solution)/shard_map/ppermute | solution.py:345
  68.9 3.6 %collective-permute-done.5.m1 = bf16[256,1024]{1,0:T(8,128)(2,1)S(1)} collective-permute-done((bf16[256,1024]{1,0:T(8,128)(2,1)S(1)}, bf16[256,1024]{1,0:T(8,128)(2,1)S(1)}, u32[]{:S(2)}, u32[]{:S(2)}) %collective-permute-start.5) | collective-permute-done | bytes 524320 | tf_op jit(solution)/shard_map/ppermute | solution.py:348
  72.5 0.1 collective-permute-start.7
  72.5 0.0 collective-permute-done.6.m2
  72.6 0.0 copy-start.10
  72.6 2.7 %collective-permute-start.8 = (bf16[128,1024]{1,0:T(8,128)(2,1)S(1)}, bf16[128,1024]{1,0:T(8,128)(2,1)S(1)}, u32[]{:S(2)}, u32[]{:S(2)}) collective-permute-start(bf16[128,1024]{1,0:T(8,128)(2,1)S(1)} %slice.19), channel_id=1, source_target_pairs={{0,192},{64,0},{128,64},{192,128},{1,193},{65,1},{129,65},{193,129... | collective-permute-start | bytes 786440 | tf_op jit(solution)/shard_map/ppermute | solution.py:348
  75.3 0.0 collective-permute-done.3.c3
  75.3 0.0 collective-permute-done.4.c4
  75.3 0.0 copy-done.2
  75.3 5.1 %shard_map.106 = (bf16[256,1024]{1,0:T(8,128)(2,1)S(1)}, bf16[256,1024]{1,0:T(8,128)(2,1)S(1)}, bf16[256,1024]{1,0:T(8,128)(2,1)S(1)}, bf16[128,1024]{1,0:T(8,128)(2,1)S(1)}, bf16[128,1024]{1,0:T(8,128)(2,1)S(1)}) custom-call(bf16[256,1024]{1,0:T(8,128)(2,1)S(1)} %collective-permute-done.c0, bf16[256,1024]{1,0:T(8,128)(2,1)S(1)} %collective-permute-done.1.c1, ...), custom_call_target="tpu_custom_call" | custom-call | tf_op jit(solution)/shard_map/pallas_call | solution.py:378
  80.4 0.0 copy-done.10
  80.4 0.8 copy-done.8
  81.2 0.0 collective-permute-start.9
  81.2 2.7 %collective-permute-start.10 = (bf16[128,1024]{1,0:T(8,128)(2,1)S(1)}, bf16[128,1024]{1,0:T(8,128)(2,1)S(1)}, u32[]{:S(2)}, u32[]{:S(2)}) collective-permute-start(bf16[128,1024]{1,0:T(8,128)(2,1)S(1)} %get-tuple-element.42), channel_id=1, source_target_pairs={{0,192},{64,0},{128,64},{192,128},{1,193},{65,1},{129,65},{193,129... | collective-permute-start | bytes 786440 | tf_op jit(solution)/shard_map/ppermute | solution.py:348
  83.9 0.0 collective-permute-done.7.m3
  83.9 0.0 collective-permute-done.8.m4
  83.9 1.0 copy-done.3
  85.0 5.5 %shard_map.112 = (bf16[8,64,1024]{2,1,0:T(8,128)(2,1)}, bf16[8,64,1024]{2,1,0:T(8,128)(2,1)}) custom-call(bf16[256,1024]{1,0:T(8,128)(2,1)S(1)} %collective-permute-done.c0, bf16[256,1024]{1,0:T(8,128)(2,1)S(1)} %collective-permute-done.1.c1, bf16[256,1024]{1,0:T(8,128)(2,1)S(1)} %copy-done.3, bf16[128,1024]{1,0:T(8,128)(2,1)S(1)} %collective-permute-done.3.c3, ...), custom_call_target="tpu_custom_call" | custom-call | flops 20000000000 | tf_op jit(solution)/shard_map/pallas_call | solution.py:393
  90.4 2.0 %collective-permute-start.13 = (bf16[8,64,1024]{2,1,0:T(8,128)(2,1)}, bf16[8,64,1024]{2,1,0:T(8,128)(2,1)S(1)}, u32[]{:S(2)}, u32[]{:S(2)}) collective-permute-start(bf16[8,64,1024]{2,1,0:T(8,128)(2,1)} %get-tuple-element.61), channel_id=1, source_target_pairs={{0,4},{4,0},{8,12},{12,8},{16,20},{20,16},{24,28},{28,24},{32,36},... | collective-permute-start | bytes 3145736 | tf_op jit(solution)/shard_map/ppermute | solution.py:407
  92.5 0.0 collective-permute-done.9.top
  92.5 0.0 collective-permute-done.10.bottom
  92.5 0.9 shard_map.107
  93.3 0.0 collective-permute-start.11
  93.3 2.7 %collective-permute-start.12 = (bf16[256,1024]{1,0:T(8,128)(2,1)S(1)}, bf16[256,1024]{1,0:T(8,128)(2,1)}, u32[]{:S(2)}, u32[]{:S(2)}) collective-permute-start(bf16[256,1024]{1,0:T(8,128)(2,1)S(1)} %get-tuple-element.46), channel_id=1, source_target_pairs={{0,192},{64,0},{128,64},{192,128},{1,193},{65,1},{129,65},{193,129... | collective-permute-start | bytes 1572872 | tf_op jit(solution)/shard_map/ppermute | solution.py:348
  96.0 0.0 collective-permute-done.13.other_ref
  96.0 1.6 %shard_map.113 = f32[8,64,1024]{2,1,0:T(8,128)} custom-call(bf16[8,64,1024]{2,1,0:T(8,128)(2,1)S(1)} %copy-done.5, bf16[8,64,1024]{2,1,0:T(8,128)(2,1)S(1)} %collective-permute-done.13.other_ref), custom_call_target="tpu_custom_call" | custom-call | tf_op jit(solution)/shard_map/pallas_call | solution.py:408
  97.6 0.0 reduce-scatter.2.cloned.1.call-update
  97.6 10.8 %collective-permute-done.11.g1 = bf16[256,1024]{1,0:T(8,128)(2,1)} collective-permute-done((bf16[256,1024]{1,0:T(8,128)(2,1)}, bf16[256,1024]{1,0:T(8,128)(2,1)}, u32[]{:S(2)}, u32[]{:S(2)}) %collective-permute-start.11) | collective-permute-done | bytes 524320 | tf_op jit(solution)/shard_map/ppermute | solution.py:348
  108.4 0.0 collective-permute-done.12.g2
  108.4 2.1 %shard_map.108 = (bf16[256,1024]{1,0:T(8,128)(2,1)S(1)}, bf16[128,1024]{1,0:T(8,128)(2,1)S(1)}) custom-call(bf16[256,1024]{1,0:T(8,128)(2,1)S(1)} %copy-done.9, bf16[256,1024]{1,0:T(8,128)(2,1)} %collective-permute-done.11.g1, bf16[256,1024]{1,0:T(8,128)(2,1)} %collective-permute-done.12.g2, bf16[256,128]{1,0:T(8,128)(2,1)S(1)} %bitcast.31, ...), custom_call_target="tpu_custom_call" | custom-call | flops 49999998976 | tf_op jit(solution)/shard_map/pallas_call | solution.py:411
  110.5 20.8 %all_to_all.44 = bf16[16,8,1024]{2,1,0:T(8,128)(2,1)S(1)} all-to-all(bf16[16,8,1024]{2,1,0:T(8,128)(2,1)S(1)} %bitcast.33), channel_id=1, replica_groups=mesh['dp'=4,'ctx'=16,'tp'=4] {'ctx'}, dimensions={0} | all-to-all | bytes 524288 | tf_op jit(solution)/shard_map/all_to_all | solution.py:419
  131.3 0.8 shard_map.109
  132.1 3.4 %all-to-all-start.3 = ((bf16[16,8,1024]{2,1,0:T(8,128)(2,1)}), bf16[16,8,1024]{2,1,0:T(8,128)(2,1)S(1)}, u32[]{:S(2)}, u32[]{:S(2)}) async-start(bf16[16,8,1024]{2,1,0:T(8,128)(2,1)} %bitcast.11), calls=%async_computation.3 | async-start | bytes 524288 | tf_op jit(solution)/shard_map/all_to_all | solution.py:421
  135.5 2.7 %shard_map.110 = (f32[256,1024]{1,0:T(8,128)S(1)}, f32[256,128]{1,0:T(8,128)S(1)}, bf16[256,128]{1,0:T(8,128)(2,1)}) custom-call(bf16[256,1024]{1,0:T(8,128)(2,1)S(1)} %bitcast.19, bf16[256,128]{1,0:T(8,128)(2,1)S(1)} %bitcast.25, bf16[256,128]{1,0:T(8,128)(2,1)S(1)} %bitcast.32, bf16[256,1024]{1,0:T(8,128)(2,1)S(1)} %get-tuple-element.49.g_ref, ...), custom_call_target="tpu_custom_call" | custom-call | tf_op jit(solution)/shard_map/pallas_call | solution.py:422
  138.2 8.9 %all-to-all-done.3 = bf16[16,8,1024]{2,1,0:T(8,128)(2,1)S(1)} async-done(((bf16[16,8,1024]{2,1,0:T(8,128)(2,1)}), bf16[16,8,1024]{2,1,0:T(8,128)(2,1)S(1)}, u32[]{:S(2)}, u32[]{:S(2)}) %all-to-all-start.3) | async-done | bytes 262176 | tf_op jit(solution)/shard_map/all_to_all | solution.py:421
  147.1 1.5 shard_map.111
  (15 shorter events, 0.1 us)
Async XLA Ops:
  7.2 50.5 %all-gather.2.cloned.1.call-start = ((), (), s32[]{:S(2)}) async-start(), calls=%async_computation.5 | async-start | bytes 2228224 | tf_op jit(solution)/shard_map/all_gather | solution.py:353
  12.0 23.8 %all-to-all-start = ((bf16[16,8,1152]{2,1,0:T(8,128)(2,1)}), bf16[16,8,1152]{2,1,0:T(8,128)(2,1)S(1)}, u32[]{:S(2)}, u32[]{:S(2)}) async-start(bf16[16,8,1152]{2,1,0:T(8,128)(2,1)} %bitcast.34), calls=%async_computation | async-start | bytes 589824 | tf_op jit(solution)/shard_map/all_to_all | solution.py:360
  21.9 18.4 %collective-permute-start = (bf16[256,1024]{1,0:T(8,128)(2,1)}, bf16[256,1024]{1,0:T(8,128)(2,1)S(1)}, u32[]{:S(2)}, u32[]{:S(2)}) collective-permute-start(bf16[256,1024]{1,0:T(8,128)(2,1)} %bitcast.36), channel_id=1, source_target_pairs={{0,0},{1,64},{2,128},{3,192},{64,1},{65,65},{66,129},{67,193},{128... | collective-permute-start | bytes 1572872 | tf_op jit(solution)/shard_map/ppermute | solution.py:342
  35.7 18.8 %copy-start = (bf16[1,256,1024]{2,1,0:T(8,128)(2,1)S(1)}, bf16[1,256,1024]{2,1,0:T(8,128)(2,1)}, u32[]{:S(2)}) copy-start(bf16[1,256,1024]{2,1,0:T(8,128)(2,1)} %param.7) | copy-start | bytes 1572868
  35.7 18.8 %copy-start.1 = (f32[256,128]{1,0:T(8,128)S(1)}, f32[256,128]{1,0:T(8,128)}, u32[]{:S(2)}) copy-start(f32[256,128]{1,0:T(8,128)} %get-tuple-element.33.columns_ref) | copy-start | bytes 393220
  35.8 18.8 %copy-start.4 = (bf16[1,256,128]{2,1,0:T(8,128)(2,1)S(1)}, bf16[1,256,128]{2,1,0:T(8,128)(2,1)}, u32[]{:S(2)}) copy-start(bf16[1,256,128]{2,1,0:T(8,128)(2,1)} %param.8) | copy-start | bytes 196612
  35.8 18.8 %copy-start.6 = (bf16[1,256,128]{2,1,0:T(8,128)(2,1)S(1)}, bf16[1,256,128]{2,1,0:T(8,128)(2,1)}, u32[]{:S(2)}) copy-start(bf16[1,256,128]{2,1,0:T(8,128)(2,1)} %param.9) | copy-start | bytes 196612
  35.8 18.9 %copy-start.7 = (f32[16,256]{1,0:T(8,128)S(1)}, f32[16,256]{1,0:T(8,128)}, u32[]{:S(2)}) copy-start(f32[16,256]{1,0:T(8,128)} %get-tuple-element.34.rows_ref) | copy-start | bytes 49156
  36.8 17.8 %all-to-all-start.1 = ((bf16[16,8,1024]{2,1,0:T(8,128)(2,1)}), bf16[16,8,1024]{2,1,0:T(8,128)(2,1)S(1)}, u32[]{:S(2)}, u32[]{:S(2)}) async-start(bf16[16,8,1024]{2,1,0:T(8,128)(2,1)} %bitcast.7), calls=%async_computation.1 | async-start | bytes 524288 | tf_op jit(solution)/shard_map/all_to_all | solution.py:367
  40.3 108.4 %reduce-scatter.2.cloned.1.call-start = ((), (), s32[]{:S(2)}) async-start(), calls=%async_computation.6 | async-start | bytes 2359296 | tf_op jit(solution)/shard_map/reduce_scatter | solution.py:410
  40.3 25.7 %collective-permute-start.1 = (bf16[256,1024]{1,0:T(8,128)(2,1)S(1)}, bf16[256,1024]{1,0:T(8,128)(2,1)S(1)}, u32[]{:S(2)}, u32[]{:S(2)}) collective-permute-start(bf16[256,1024]{1,0:T(8,128)(2,1)S(1)} %collective-permute-done.c0), channel_id=1, source_target_pairs={{0,1},{1,2},{2,3},{3,0},{4,5},{5,6},{6,7},{7,4},{8,9},{9,10},{10,1... | collective-permute-start | bytes 1572872 | tf_op jit(solution)/shard_map/ppermute | solution.py:345
  48.4 17.7 %collective-permute-start.2 = (bf16[256,1024]{1,0:T(8,128)(2,1)S(1)}, bf16[256,1024]{1,0:T(8,128)(2,1)S(1)}, u32[]{:S(2)}, u32[]{:S(2)}) collective-permute-start(bf16[256,1024]{1,0:T(8,128)(2,1)S(1)} %collective-permute-done.c0), channel_id=1, source_target_pairs={{0,3},{1,0},{2,1},{3,2},{4,7},{5,4},{6,5},{7,6},{8,11},{9,8},{10,9... | collective-permute-start | bytes 1572872 | tf_op jit(solution)/shard_map/ppermute | solution.py:345
  57.6 14.8 %collective-permute-start.5 = (bf16[256,1024]{1,0:T(8,128)(2,1)S(1)}, bf16[256,1024]{1,0:T(8,128)(2,1)S(1)}, u32[]{:S(2)}, u32[]{:S(2)}) collective-permute-start(bf16[256,1024]{1,0:T(8,128)(2,1)S(1)} %shard_map.104.m0), channel_id=1, source_target_pairs={{0,64},{64,128},{128,192},{192,0},{1,65},{65,129},{129,193},{193,1... | collective-permute-start | bytes 1572872 | tf_op jit(solution)/shard_map/ppermute | solution.py:348
  59.0 13.6 %collective-permute-start.6 = (bf16[256,1024]{1,0:T(8,128)(2,1)S(1)}, bf16[256,1024]{1,0:T(8,128)(2,1)S(1)}, u32[]{:S(2)}, u32[]{:S(2)}) collective-permute-start(bf16[256,1024]{1,0:T(8,128)(2,1)S(1)} %shard_map.104.m0), channel_id=1, source_target_pairs={{0,192},{64,0},{128,64},{192,128},{1,193},{65,1},{129,65},{193,129... | collective-permute-start | bytes 1572872 | tf_op jit(solution)/shard_map/ppermute | solution.py:348
  66.0 9.3 %collective-permute-start.3 = (bf16[128,1024]{1,0:T(8,128)(2,1)S(1)}, bf16[128,1024]{1,0:T(8,128)(2,1)S(1)}, u32[]{:S(2)}, u32[]{:S(2)}) collective-permute-start(bf16[128,1024]{1,0:T(8,128)(2,1)S(1)} %slice.16), channel_id=1, source_target_pairs={{0,1},{1,2},{2,3},{3,0},{4,5},{5,6},{6,7},{7,4},{8,9},{9,10},{10,1... | collective-permute-start | bytes 786440 | tf_op jit(solution)/shard_map/ppermute | solution.py:345
  66.1 9.2 %copy-start.2 = (bf16[256,1024]{1,0:T(8,128)(2,1)}, bf16[256,1024]{1,0:T(8,128)(2,1)S(1)}, u32[]{:S(2)}) copy-start(bf16[256,1024]{1,0:T(8,128)(2,1)S(1)} %collective-permute-done.2.c2) | copy-start | bytes 1572868
  66.2 9.2 %collective-permute-start.4 = (bf16[128,1024]{1,0:T(8,128)(2,1)S(1)}, bf16[128,1024]{1,0:T(8,128)(2,1)S(1)}, u32[]{:S(2)}, u32[]{:S(2)}) collective-permute-start(bf16[128,1024]{1,0:T(8,128)(2,1)S(1)} %slice.17), channel_id=1, source_target_pairs={{0,3},{1,0},{2,1},{3,2},{4,7},{5,4},{6,5},{7,6},{8,11},{9,8},{10,9... | collective-permute-start | bytes 786440 | tf_op jit(solution)/shard_map/ppermute | solution.py:345
  72.5 11.5 %collective-permute-start.7 = (bf16[128,1024]{1,0:T(8,128)(2,1)S(1)}, bf16[128,1024]{1,0:T(8,128)(2,1)S(1)}, u32[]{:S(2)}, u32[]{:S(2)}) collective-permute-start(bf16[128,1024]{1,0:T(8,128)(2,1)S(1)} %slice.18), channel_id=1, source_target_pairs={{0,64},{64,128},{128,192},{192,0},{1,65},{65,129},{129,193},{193,1... | collective-permute-start | bytes 786440 | tf_op jit(solution)/shard_map/ppermute | solution.py:348
  72.6 7.9 %copy-start.10 = (bf16[256,1024]{1,0:T(8,128)(2,1)}, bf16[256,1024]{1,0:T(8,128)(2,1)S(1)}, u32[]{:S(2)}) copy-start(bf16[256,1024]{1,0:T(8,128)(2,1)S(1)} %collective-permute-done.6.m2) | copy-start | bytes 1572868
  72.6 11.3 %collective-permute-start.8 = (bf16[128,1024]{1,0:T(8,128)(2,1)S(1)}, bf16[128,1024]{1,0:T(8,128)(2,1)S(1)}, u32[]{:S(2)}, u32[]{:S(2)}) collective-permute-start(bf16[128,1024]{1,0:T(8,128)(2,1)S(1)} %slice.19), channel_id=1, source_target_pairs={{0,192},{64,0},{128,64},{192,128},{1,193},{65,1},{129,65},{193,129... | collective-permute-start | bytes 786440 | tf_op jit(solution)/shard_map/ppermute | solution.py:348
  80.4 0.8 copy-start.8
  81.2 11.2 %collective-permute-start.9 = (bf16[128,1024]{1,0:T(8,128)(2,1)S(1)}, bf16[128,1024]{1,0:T(8,128)(2,1)S(1)}, u32[]{:S(2)}, u32[]{:S(2)}) collective-permute-start(bf16[128,1024]{1,0:T(8,128)(2,1)S(1)} %get-tuple-element.41), channel_id=1, source_target_pairs={{0,64},{64,128},{128,192},{192,0},{1,65},{65,129},{129,193},{193,1... | collective-permute-start | bytes 786440 | tf_op jit(solution)/shard_map/ppermute | solution.py:348
  81.2 11.2 %collective-permute-start.10 = (bf16[128,1024]{1,0:T(8,128)(2,1)S(1)}, bf16[128,1024]{1,0:T(8,128)(2,1)S(1)}, u32[]{:S(2)}, u32[]{:S(2)}) collective-permute-start(bf16[128,1024]{1,0:T(8,128)(2,1)S(1)} %get-tuple-element.42), channel_id=1, source_target_pairs={{0,192},{64,0},{128,64},{192,128},{1,193},{65,1},{129,65},{193,129... | collective-permute-start | bytes 786440 | tf_op jit(solution)/shard_map/ppermute | solution.py:348
  83.9 1.0 copy-start.3
  90.4 5.6 %copy-start.5 = (bf16[8,64,1024]{2,1,0:T(8,128)(2,1)S(1)}, bf16[8,64,1024]{2,1,0:T(8,128)(2,1)}, u32[]{:S(2)}) copy-start(bf16[8,64,1024]{2,1,0:T(8,128)(2,1)} %get-tuple-element.60.mine_ref) | copy-start | bytes 3145732
  90.4 5.6 %collective-permute-start.13 = (bf16[8,64,1024]{2,1,0:T(8,128)(2,1)}, bf16[8,64,1024]{2,1,0:T(8,128)(2,1)S(1)}, u32[]{:S(2)}, u32[]{:S(2)}) collective-permute-start(bf16[8,64,1024]{2,1,0:T(8,128)(2,1)} %get-tuple-element.61), channel_id=1, source_target_pairs={{0,4},{4,0},{8,12},{12,8},{16,20},{20,16},{24,28},{28,24},{32,36},... | collective-permute-start | bytes 3145736 | tf_op jit(solution)/shard_map/ppermute | solution.py:407
  93.3 15.1 %collective-permute-start.11 = (bf16[256,1024]{1,0:T(8,128)(2,1)}, bf16[256,1024]{1,0:T(8,128)(2,1)}, u32[]{:S(2)}, u32[]{:S(2)}) collective-permute-start(bf16[256,1024]{1,0:T(8,128)(2,1)} %get-tuple-element.45), channel_id=1, source_target_pairs={{0,64},{64,128},{128,192},{192,0},{1,65},{65,129},{129,193},{193,1... | collective-permute-start | bytes 1572872 | tf_op jit(solution)/shard_map/ppermute | solution.py:348
  93.3 15.1 %collective-permute-start.12 = (bf16[256,1024]{1,0:T(8,128)(2,1)S(1)}, bf16[256,1024]{1,0:T(8,128)(2,1)}, u32[]{:S(2)}, u32[]{:S(2)}) collective-permute-start(bf16[256,1024]{1,0:T(8,128)(2,1)S(1)} %get-tuple-element.46), channel_id=1, source_target_pairs={{0,192},{64,0},{128,64},{192,128},{1,193},{65,1},{129,65},{193,129... | collective-permute-start | bytes 1572872 | tf_op jit(solution)/shard_map/ppermute | solution.py:348
  97.6 10.8 %copy-start.9 = (bf16[256,1024]{1,0:T(8,128)(2,1)S(1)}, bf16[256,1024]{1,0:T(8,128)(2,1)}, u32[]{:S(2)}) copy-start(bf16[256,1024]{1,0:T(8,128)(2,1)} %copy-done.8) | copy-start | bytes 1572868
  132.1 15.0 %all-to-all-start.3 = ((bf16[16,8,1024]{2,1,0:T(8,128)(2,1)}), bf16[16,8,1024]{2,1,0:T(8,128)(2,1)S(1)}, u32[]{:S(2)}, u32[]{:S(2)}) async-start(bf16[16,8,1024]{2,1,0:T(8,128)(2,1)} %bitcast.11), calls=%async_computation.3 | async-start | bytes 524288 | tf_op jit(solution)/shard_map/all_to_all | solution.py:421
Sparse Core Ops, SparseCore 0:
  9.8 47.7 all-gather.1
  97.7 40.6 reduce-scatter.1
